TPU v7x, 32 devices: a whole 2x2x4 slice. The times are simulated.
32 devices in a mesh: groups: 2 (over y), dp: 4 (over x, core), tensor: 4 (over z).
Axes of the slice: x: 2, y: 2, z: 4, core: 2. Of those that a mesh axis runs over, the one named last changes fastest.
Arguments:
- tokens: bfloat16 [64, 8192], P(('groups', 'tensor'), 'dp'), parts along dimension 0, may hold values from -6 to 6
- basis: bfloat16 [8192, 1024], P('dp'), may hold values from -0.0625 to 0.0625
- gate_weight: bfloat16 [8192, 16384], P('dp', 'tensor'), may hold values from -0.0625 to 0.0625
- up_weight: bfloat16 [8192, 16384], P('dp', 'tensor'), may hold values from -0.0625 to 0.0625
- down_weight: bfloat16 [16384, 8192], P('tensor', 'dp'), may hold values from -0.046875 to 0.046875
Outputs:
- mixed: bfloat16 [64, 8192], P(('groups', 'tensor'), 'dp'), parts along dimension 0
There are 2 independent parts, one for each index of `groups`. A program takes and returns all parts, laid end to end along the dimension named above; an argument that names none is the same for every part. Nothing has to cross between parts.
All inputs are finite; a program needn't handle non-finite values.
Results may differ from a plain program's by a relative error of at most 0.0095.
Values may be sent and summed in bfloat16 or wider, within the bound.
No kernel may reach another device: no remote copies, remote signals or barrier semaphores. Data moves between devices by JAX's collectives and lax.ppermute only.
A program may use at most 128 MiB of HBM per device.

v0:
```python
import jax
import jax.numpy as jnp
from jax import lax
from jax.sharding import PartitionSpec as P

D = 8192
R = 1024


def shards(tokens, basis, gate_weight, up_weight, down_weight):
    factor = (D / R) ** 0.5
    contract = (((1,), (1,)), ((), ()))
    partial_value = jnp.dot(tokens, basis, preferred_element_type=jnp.float32)
    code_rows = lax.psum(partial_value, "dp").astype(jnp.bfloat16)
    product = lax.dot_general(
        lax.all_gather(code_rows, "tensor", axis=0, tiled=True),
        basis,
        contract,
        preferred_element_type=jnp.float32,
    )
    restored = (factor * product).astype(jnp.bfloat16)
    gate_part = jnp.dot(restored, gate_weight, preferred_element_type=jnp.float32)
    up_part = jnp.dot(restored, up_weight, preferred_element_type=jnp.float32)
    gate_sum, up_sum = lax.psum((gate_part, up_part), "dp")
    hidden = (jax.nn.silu(gate_sum) * up_sum).astype(jnp.bfloat16)
    basis_float = basis.astype(jnp.float32)
    summed = lax.psum_scatter(
        jnp.dot(hidden, down_weight, preferred_element_type=jnp.float32),
        "tensor",
        scatter_dimension=0,
        tiled=True,
    )
    code_part = jnp.dot(summed, basis_float, precision=lax.Precision.HIGHEST)
    out_codes = lax.psum(code_part, "dp").astype(jnp.bfloat16)
    decoded = lax.dot_general(out_codes, basis, contract, preferred_element_type=jnp.float32)
    return (factor * decoded).astype(jnp.bfloat16)


def solution(mesh):
    placed = (
        P(("groups", "tensor"), "dp"),
        P("dp", None),
        P("dp", "tensor"),
        P("dp", "tensor"),
        P("tensor", "dp"),
    )
    return jax.shard_map(
        shards, mesh=mesh, in_specs=placed, out_specs=P(("groups", "tensor"), "dp"), check_vma=False
    )
```

profile of v0, /device:TPU:0, one launch (start us, length us, event | category | flops | bytes accessed | tf_op | source)
XLA Modules:
  0.0 146.0 jit_solution(12155345290253646266)
XLA Ops:
  6.5 0.0 copy-start
  6.5 0.0 all-reduce.3.cloned.1.call-start
  6.5 0.8 copy-done
  7.3 2.8 %fusion.6 = f32[8,1024]{1,0:T(8,128)S(1)} fusion(bf16[8,2048]{1,0:T(8,128)(2,1)S(1)} %copy-done, bf16[2048,1024]{1,0:T(8,128)(2,1)} %param.6), kind=kOutput, calls=%fused_computation.9 | convolution fusion | flops 33554432 | bytes 4259840 | tf_op jit(solution)/shard_map/dot_general | solution.py:13
  10.1 12.9 %psum.28 = bf16[8,1024]{1,0:T(8,128)(2,1)S(1)} all-reduce(f32[8,1024]{1,0:T(8,128)S(1)} %fusion.6), channel_id=1, replica_groups=mesh['groups'=2,'dp'=4,'tensor'=4] {'dp'}, use_global_device_ids=true, to_apply=%region_0.0 | all-reduce | flops 8192 | bytes 49152 | tf_op jit(solution)/shard_map/psum | solution.py:14
  23.0 13.4 %all_gather.3 = bf16[32,1024]{1,0:T(8,128)(2,1)S(1)} all-gather(bf16[8,1024]{1,0:T(8,128)(2,1)S(1)} %psum.28), channel_id=1, replica_groups=mesh['groups'=2,'dp'=4,'tensor'=4] {'tensor'}, dimensions={0}, use_global_device_ids=true | all-gather | bytes 81920 | tf_op jit(solution)/shard_map/all_gather | solution.py:16
  36.4 3.5 %fusion = bf16[32,2048]{1,0:T(8,128)(2,1)S(1)} fusion(bf16[32,1024]{1,0:T(8,128)(2,1)S(1)} %all_gather.3, bf16[2048,1024]{1,0:T(8,128)(2,1)} %param.6), kind=kOutput, calls=%fused_computation.1 | convolution fusion | flops 134348800 | bytes 4390912 | tf_op jit(solution)/shard_map/dot_general | solution.py:15
  39.9 0.0 copy-start.1
  40.0 9.7 %fusion.8 = f32[32,4096]{1,0:T(8,128)} fusion(bf16[32,2048]{1,0:T(8,128)(2,1)S(1)} %fusion, bf16[2048,4096]{1,0:T(8,128)(2,1)} %param.8), kind=kOutput, calls=%fused_computation.11 | convolution fusion | flops 536870912 | bytes 17432576 | tf_op jit(solution)/shard_map/dot_general | solution.py:23
  49.7 1.0 copy-done.1
  50.7 3.8 %fusion.7 = f32[32,4096]{1,0:T(8,128)} fusion(bf16[32,2048]{1,0:T(8,128)(2,1)S(1)} %fusion, bf16[2048,4096]{1,0:T(8,128)(2,1)S(1)} %copy-done.1), kind=kOutput, calls=%fused_computation.10 | convolution fusion | flops 536870912 | bytes 17432576 | tf_op jit(solution)/shard_map/dot_general | solution.py:22
  54.5 0.0 all-reduce.3.cloned.1.call-update
  54.5 0.0 reduce-scatter.2.cloned.1.call-start
  54.6 36.3 %all-reduce.3.cloned.1.call-done = (f32[32,4096]{1,0:T(8,128)}, f32[32,4096]{1,0:T(8,128)}) async-done(((f32[32,4096]{1,0:T(8,128)}, f32[32,4096]{1,0:T(8,128)}), (f32[32,4096]{1,0:T(8,128)}, f32[32,4096]{1,0:T(8,128)})) %all-reduce.3.cloned.1.call-update) | async-done | bytes 1048592 | tf_op jit(solution)/shard_map/psum | solution.py:24
  90.8 9.8 %fusion.2 = f32[32,2048]{1,0:T(8,128)} fusion(bf16[4096,2048]{1,0:T(8,128)(2,1)} %param.9, f32[32,4096]{1,0:T(8,128)} %get-tuple-element.5, f32[32,4096]{1,0:T(8,128)} %get-tuple-element.6), kind=kOutput, calls=%fused_computation.5 | convolution fusion | flops 537657344 | bytes 18087936 | tf_op jit(solution)/shard_map/dot_general | solution.py:28
  100.7 0.0 reduce-scatter.2.cloned.1.call-update
  100.7 20.2 %reduce-scatter.2.cloned.1.call-done = f32[8,2048]{1,0:T(8,128)} async-done(((f32[32,2048]{1,0:T(8,128)}), f32[8,2048]{1,0:T(8,128)}) %reduce-scatter.2.cloned.1.call-update) | async-done | bytes 65552 | tf_op jit(solution)/shard_map/reduce_scatter | solution.py:27
  120.9 4.0 %fusion.9 = f32[8,1024]{1,0:T(8,128)S(1)} fusion(f32[8,2048]{1,0:T(8,128)} %reduce-scatter.2.cloned.1.call-done, bf16[2048,1024]{1,0:T(8,128)(2,1)} %param.6), kind=kOutput, calls=%fused_computation.12 | convolution fusion | flops 201326592 | bytes 4292608 | tf_op jit(solution)/shard_map/dot_general | solution.py:33
  124.8 10.3 %psum.31 = bf16[8,1024]{1,0:T(8,128)(2,1)S(1)} all-reduce(f32[8,1024]{1,0:T(8,128)S(1)} %fusion.9), channel_id=1, replica_groups=mesh['groups'=2,'dp'=4,'tensor'=4] {'dp'}, use_global_device_ids=true, to_apply=%region_4.5 | all-reduce | flops 8192 | bytes 49152 | tf_op jit(solution)/shard_map/psum | solution.py:34
  135.1 4.0 %fusion.1 = bf16[8,2048]{1,0:T(8,128)(2,1)} fusion(bf16[2048,1024]{1,0:T(8,128)(2,1)} %param.6, bf16[8,1024]{1,0:T(8,128)(2,1)S(1)} %psum.31), kind=kOutput, calls=%fused_computation.3 | convolution fusion | flops 33587200 | bytes 4243456 | tf_op jit(solution)/shard_map/dot_general | solution.py:35
Async XLA Ops:
  6.5 0.8 copy-start
  6.5 84.3 %all-reduce.3.cloned.1.call-start = ((), (), s32[]{:S(2)}) async-start(), calls=%async_computation.2 | async-start | bytes 2097152 | tf_op jit(solution)/shard_map/psum | solution.py:24
  39.9 10.7 %copy-start.1 = (bf16[2048,4096]{1,0:T(8,128)(2,1)S(1)}, bf16[2048,4096]{1,0:T(8,128)(2,1)}, u32[]{:S(2)}) copy-start(bf16[2048,4096]{1,0:T(8,128)(2,1)} %param.7) | copy-start | bytes 50331652
  54.5 66.4 %reduce-scatter.2.cloned.1.call-start = ((), (), s32[]{:S(2)}) async-start(), calls=%async_computation.1 | async-start | bytes 327680 | tf_op jit(solution)/shard_map/reduce_scatter | solution.py:27
Sparse Core Ops, SparseCore 0:
  54.6 36.1 all-reduce.2
  100.8 20.0 reduce-scatter.1
where the time goes:
time: 146 us
  waiting for transfers between devices  56.5 us (39%)
  matrix products  37.6 us (26%)
  blocking collectives  36.6 us (25%)
  between operations  13.4 us (9%)
  local copies, waits for them, and re-layouts  1.77 us (1%)
    psum x1, waiting for transfers between devices, shards(): gate_sum, up_sum = lax.psum((gate_part, up_part), 'dp')  36.3 us
    reduce_scatter x1, waiting for transfers between devices, shards(): lax.psum_scatter(jnp.dot(hidden, down_weight, preferred_element_type=jnp....  20.2 us
    all_gather x1, blocking collectives, shards(): lax.all_gather(code_rows, 'tensor', axis=0, tiled=True)  13.4 us
    psum x1, blocking collectives, shards(): code_rows = lax.psum(partial_value, 'dp').astype(jnp.bfloat16)  12.9 us
    psum x1, blocking collectives, shards(): out_codes = lax.psum(code_part, 'dp').astype(jnp.bfloat16)  10.3 us
    dot_general x1, matrix products, shards(): jnp.dot(hidden, down_weight, preferred_element_type=jnp.float32)  9.81 us
    dot_general x1, matrix products, shards(): up_part = jnp.dot(restored, up_weight, preferred_element_type=jnp.float32)  9.73 us
    dot_general x1, matrix products, shards(): lax.dot_general(out_codes, basis, contract, preferred_element_type=jnp.fl...  4 us
  transfers between devices with their start and end apart: 2, of which 2 were waited for; matrix products, arithmetic and copies ran while one was open for 0% of the time, Pallas kernels for 0%

commit v1 on v0

v1 whole, which is shorter than its diff:
```python
import functools

import jax
import jax.numpy as jnp
from jax import lax
from jax.experimental import pallas as pl
from jax.experimental.pallas import tpu as pltpu
from jax.sharding import PartitionSpec as P

D = 8192
R = 1024
F32 = jnp.float32
BF16 = jnp.bfloat16
LIMIT = 6 * 1024 * 1024
VMEM = pl.BlockSpec(memory_space=pltpu.VMEM)
SMEM = pl.BlockSpec(memory_space=pltpu.SMEM)


def call(body, out, microseconds, scalars, *arrays, scratch=(), hold=0):
    inputs = len(scalars) + len(arrays)
    kept = arrays[len(arrays) - hold :] if hold else ()

    def run(*refs):
        body(*refs[: inputs + 1], *refs[inputs + 1 + hold :])

    got = pl.pallas_call(
        run,
        out_shape=[out] + [jax.ShapeDtypeStruct(a.shape, a.dtype) for a in kept],
        in_specs=[SMEM] * len(scalars) + [VMEM] * len(arrays),
        out_specs=[VMEM] * (1 + hold),
        scratch_shapes=list(scratch),
        input_output_aliases={inputs - hold + i: 1 + i for i in range(hold)},
        cost_estimate=pl.CostEstimate(flops=0, bytes_accessed=int(microseconds * 3.69e6), transcendentals=0),
        compiler_params=pltpu.CompilerParams(vmem_limit_bytes=LIMIT),
    )(*scalars, *[pin(a) if a.size > 2**20 else a for a in arrays])
    return got if hold else got[0]


def pin(array):
    return pltpu.with_memory_space_constraint(array, pltpu.VMEM)


def swap(value, axis, mask, size):
    return lax.ppermute(value, axis, [(i, i ^ mask) for i in range(size)])


def tile_of(extent, most):
    tile = most
    while extent % tile:
        tile //= 2
    return tile


def dot(a, b):
    return jnp.dot(a, b, preferred_element_type=F32)


def dot_t(a, b):
    return lax.dot_general(a, b, (((1,), (1,)), ((), ())), preferred_element_type=F32)


def add_body(a_ref, b_ref, out_ref):
    out_ref[...] = (a_ref[...].astype(F32) + b_ref[...].astype(F32)).astype(BF16)


def join_body(a_ref, b_ref, out_ref):
    rows = a_ref.shape[0]
    out_ref[:rows] = a_ref[...]
    out_ref[rows:] = b_ref[...]


def code_body(x_ref, basis_ref, out_ref):
    tile = tile_of(R, 512)
    for t in range(0, R, tile):
        out_ref[:, t : t + tile] = dot(x_ref[...], basis_ref[:, t : t + tile]).astype(BF16)


def decode_body(codes_ref, basis_ref, out_ref, *, factor):
    width = basis_ref.shape[0]
    tile = tile_of(width, 512)
    for t in range(0, width, tile):
        out_ref[:, t : t + tile] = (factor * dot_t(codes_ref[...], basis_ref[t : t + tile, :])).astype(BF16)


def wide_body(x_ref, weight_ref, out_ref):
    tile = tile_of(out_ref.shape[1], 512)
    for t in range(0, out_ref.shape[1], tile):
        out_ref[:, t : t + tile] = dot(x_ref[...], weight_ref[:, t : t + tile]).astype(BF16)


def down_first_body(start_ref, h_ref, down_ref, out_ref):
    depth, width = h_ref.shape[1], out_ref.shape[1]
    tile = tile_of(width, 512)
    at = pl.ds(pl.multiple_of(start_ref[0], 128), depth)
    for t in range(0, width, tile):
        out_ref[:, t : t + tile] = dot(h_ref[...], down_ref[at, t : t + tile])


def down_last_body(start_ref, h_ref, down_ref, acc_ref, basis_ref, out_ref, rows_ref):
    depth, width = h_ref.shape[1], acc_ref.shape[1]
    tile = tile_of(width, 512)
    at = pl.ds(pl.multiple_of(start_ref[0], 128), depth)
    for t in range(0, width, tile):
        rows_ref[:, t : t + tile] = (
            acc_ref[:, t : t + tile] + dot(h_ref[...], down_ref[at, t : t + tile])
        ).astype(BF16)
    tile = tile_of(R, 512)
    for t in range(0, R, tile):
        out_ref[:, t : t + tile] = dot(rows_ref[...], basis_ref[:, t : t + tile]).astype(BF16)


def shards(tokens, basis, gate_weight, up_weight, down_weight, *, dp, tensor):
    factor = (D / R) ** 0.5
    local = tokens.shape[0]
    rows = local * tensor
    width = tokens.shape[1]
    ff = gate_weight.shape[1]
    core = lax.axis_index("dp") % 2
    sds = jax.ShapeDtypeStruct

    codes = call(code_body, sds((local, R), BF16), 1, (), tokens, basis)
    mask = 1
    while mask < dp:
        other = swap(codes, "dp", mask, dp)
        codes = call(add_body, sds(codes.shape, BF16), 1.3 if mask == 1 else 3.8, (), codes, other)
        mask *= 2
    mask = 1
    while mask < tensor:
        other = swap(codes, "tensor", mask, tensor)
        codes = call(join_body, sds((2 * codes.shape[0], R), BF16), 4.5, (), codes, other)
        mask *= 2
    restored = call(functools.partial(decode_body, factor=factor), sds((rows, width), BF16), 1, (), codes, basis)

    half = ff // 2
    mine = (core * half).astype(jnp.int32)
    theirs = ((1 - core) * half).astype(jnp.int32)
    sums = []
    for weight in (gate_weight, up_weight):
        part = call(wide_body, sds((rows, ff), BF16), 4, (), restored, weight)
        kept = lax.dynamic_slice_in_dim(part, mine, half, 1)
        got = swap(lax.dynamic_slice_in_dim(part, theirs, half, 1), "dp", 1, dp)
        sums.append((kept.astype(F32) + got.astype(F32)).astype(BF16))
    mask = 2
    while mask < dp:
        sums = [(s.astype(F32) + swap(s, "dp", mask, dp).astype(F32)).astype(F32 if 2 * mask == dp else BF16) for s in sums]
        mask *= 2
    gate, up = sums
    own = (gate.astype(F32) / (1 + jnp.exp(-gate.astype(F32))) * up.astype(F32)).astype(BF16)
    away = swap(own, "dp", 1, dp)
    acc = call(down_first_body, sds((rows, width), F32), 2, (mine.reshape(1),), own, down_weight)
    codes = call(
        down_last_body,
        sds((rows, R), BF16),
        3,
        (theirs.reshape(1),),
        away,
        down_weight,
        acc,
        basis,
        scratch=[pltpu.VMEM((rows, width), BF16)],
    )
    mask = tensor // 2
    while mask:
        top = codes.shape[0] // 2
        other = swap(codes[top:], "tensor", mask, tensor)
        codes = (codes[:top].astype(F32) + other.astype(F32)).astype(BF16)
        mask //= 2
    mask = dp // 2
    while mask:
        other = swap(codes, "dp", mask, dp)
        codes = (codes.astype(F32) + other.astype(F32)).astype(BF16)
        mask //= 2
    return call(
        functools.partial(decode_body, factor=factor), sds((local, width), BF16), 1, (), codes, basis
    )


def solution(mesh):
    placed = (
        P(("groups", "tensor"), "dp"),
        P("dp", None),
        P("dp", "tensor"),
        P("dp", "tensor"),
        P("tensor", "dp"),
    )
    return jax.shard_map(
        functools.partial(shards, dp=mesh.shape["dp"], tensor=mesh.shape["tensor"]),
        mesh=mesh,
        in_specs=placed,
        out_specs=P(("groups", "tensor"), "dp"),
        check_vma=False,
    )
```

time: 146 us -> 68.7 us (0.47)
  matrix products: 37.6 us -> 0 us
  waiting for transfers between devices: 56.5 us -> 19 us
  blocking collectives: 36.6 us -> 0 us
  starting transfers between devices: 0.04 us -> 18.4 us
  local copies, waits for them, and re-layouts: 1.77 us -> 16.9 us
  Pallas kernels: 0 us -> 13.7 us
  between operations: 13.4 us -> 0.18 us
    dot_general x7 -> x0, matrix products: 37.6 us -> none  [the longest x1 9.81 us: shards(): jnp.dot(hidden, down_weight, preferred_element_type=jnp.float32)]
    psum x1 -> x0, waiting for transfers between devices: 36.3 us -> none  [shards(): gate_sum, up_sum = lax.psum((gate_part, up_part), 'dp')]
    psum x2 -> x0, blocking collectives: 23.1 us -> none  [the longest x1 12.9 us: shards(): code_rows = lax.psum(partial_value, 'dp').astype(jnp.bfloat16)]
    reduce_scatter x1 -> x0, waiting for transfers between devices: 20.2 us -> none  [shards(): lax.psum_scatter(jnp.dot(hidden, down_weight, preferred_element_type=jnp....]
    ppermute x0 -> x13, waiting for transfers between devices: none -> 19 us  [swap(): return lax.ppermute(value, axis, [(i, i ^ mask) for i in range(size)])]
    ppermute x0 -> x13, starting transfers between devices: none -> 18.4 us  [swap(): return lax.ppermute(value, axis, [(i, i ^ mask) for i in range(size)])]
    unnamed x4 -> x20, local copies, waits for them, and re-layouts: 1.77 us -> 16.9 us
    pallas_call x0 -> x11, Pallas kernels: none -> 13.7 us  [call(): pl.pallas_call(run, out_shape=[out] + [jax.ShapeDtypeStruct(a.shape, a.dt...]
  transfers between devices with their start and end apart: 2 -> 13, of which waited for: 2 -> 10; matrix products, arithmetic and copies ran while one was open for 0% -> 0% of each run, Pallas kernels for 0% -> 7%
where the time goes in v1:
time: 68.7 us; the launch traced here: 68.4 us
  waiting for transfers between devices  19 us (28%)
  starting transfers between devices  18.4 us (27%)
  local copies, waits for them, and re-layouts  16.9 us (25%)
  Pallas kernels  13.7 us (20%)
    ppermute x13, waiting for transfers between devices, swap(): return lax.ppermute(value, axis, [(i, i ^ mask) for i in range(size)])  19 us
    ppermute x13, starting transfers between devices, swap(): return lax.ppermute(value, axis, [(i, i ^ mask) for i in range(size)])  18.4 us
    unnamed x20, local copies, waits for them, and re-layouts  16.9 us
    pallas_call x11, Pallas kernels, call(): pl.pallas_call(run, out_shape=[out] + [jax.ShapeDtypeStruct(a.shape, a.dt...  13.7 us
  transfers between devices with their start and end apart: 13, of which 10 were waited for; matrix products, arithmetic and copies ran while one was open for 0% of the time, Pallas kernels for 7%

profile of v1, /device:TPU:0, one launch (start us, length us, event | category | flops | bytes accessed | tf_op | source)
XLA Modules:
  0.0 68.4 jit_solution(2586468243277792698)
XLA Ops:
  0.0 2.2 %copy-done = bf16[2048,1024]{1,0:T(8,128)(2,1)S(1)} copy-done((bf16[2048,1024]{1,0:T(8,128)(2,1)S(1)}, bf16[2048,1024]{1,0:T(8,128)(2,1)}, u32[]{:S(2)}) %copy-start) | copy-done | bytes 4194328
  2.2 0.8 %copy-done.5 = bf16[8,2048]{1,0:T(8,128)(2,1)S(1)} copy-done((bf16[8,2048]{1,0:T(8,128)(2,1)S(1)}, bf16[8,2048]{1,0:T(8,128)(2,1)}, u32[]{:S(2)}) %copy-start.5) | copy-done | bytes 32792
  2.9 0.6 shard_map.55.refs_0_
  3.6 0.5 collective-permute-start
  4.1 0.8 %collective-permute-done.refs_1_ = bf16[8,1024]{1,0:T(8,128)(2,1)S(1)} collective-permute-done((bf16[8,1024]{1,0:T(8,128)(2,1)S(1)}, bf16[8,1024]{1,0:T(8,128)(2,1)S(1)}, u32[]{:S(2)}, u32[]{:S(2)}) %collective-permute-start) | collective-permute-done | bytes 16416 | tf_op jit(solution)/shard_map/ppermute | solution.py:44
  4.9 2.8 %collective-permute-start.1 = (bf16[8,1024]{1,0:T(8,128)(2,1)S(1)}, bf16[8,1024]{1,0:T(8,128)(2,1)S(1)}, u32[]{:S(2)}, u32[]{:S(2)}) collective-permute-start(bf16[8,1024]{1,0:T(8,128)(2,1)S(1)} %shard_map.56.refs_0_), channel_id=1, source_target_pairs={{0,8},{4,12},{8,0},{12,4},{1,9},{5,13},{9,1},{13,5},{2,10},{6,14},... | collective-permute-start | bytes 49160 | tf_op jit(solution)/shard_map/ppermute | solution.py:44
  7.7 1.7 %collective-permute-done.1.refs_1_ = bf16[8,1024]{1,0:T(8,128)(2,1)S(1)} collective-permute-done((bf16[8,1024]{1,0:T(8,128)(2,1)S(1)}, bf16[8,1024]{1,0:T(8,128)(2,1)S(1)}, u32[]{:S(2)}, u32[]{:S(2)}) %collective-permute-start.1) | collective-permute-done | bytes 16416 | tf_op jit(solution)/shard_map/ppermute | solution.py:44
  9.5 2.1 %collective-permute-start.2 = (bf16[8,1024]{1,0:T(8,128)(2,1)S(1)}, bf16[8,1024]{1,0:T(8,128)(2,1)S(1)}, u32[]{:S(2)}, u32[]{:S(2)}) collective-permute-start(bf16[8,1024]{1,0:T(8,128)(2,1)S(1)} %shard_map.57.refs_0_), channel_id=1, source_target_pairs={{0,1},{1,0},{2,3},{3,2},{4,5},{5,4},{6,7},{7,6},{8,9},{9,8},{10,11... | collective-permute-start | bytes 49160 | tf_op jit(solution)/shard_map/ppermute | solution.py:44
  11.6 1.7 %collective-permute-done.2.refs_1_ = bf16[8,1024]{1,0:T(8,128)(2,1)S(1)} collective-permute-done((bf16[8,1024]{1,0:T(8,128)(2,1)S(1)}, bf16[8,1024]{1,0:T(8,128)(2,1)S(1)}, u32[]{:S(2)}, u32[]{:S(2)}) %collective-permute-start.2) | collective-permute-done | bytes 16416 | tf_op jit(solution)/shard_map/ppermute | solution.py:44
  13.3 3.0 %collective-permute-start.3 = (bf16[16,1024]{1,0:T(8,128)(2,1)S(1)}, bf16[16,1024]{1,0:T(8,128)(2,1)S(1)}, u32[]{:S(2)}, u32[]{:S(2)}) collective-permute-start(bf16[16,1024]{1,0:T(8,128)(2,1)S(1)} %shard_map.58.refs_0_), channel_id=1, source_target_pairs={{0,2},{1,3},{2,0},{3,1},{4,6},{5,7},{6,4},{7,5},{8,10},{9,11},{10,... | collective-permute-start | bytes 98312 | tf_op jit(solution)/shard_map/ppermute | solution.py:44
  16.3 1.9 %collective-permute-done.3.refs_1_ = bf16[16,1024]{1,0:T(8,128)(2,1)S(1)} collective-permute-done((bf16[16,1024]{1,0:T(8,128)(2,1)S(1)}, bf16[16,1024]{1,0:T(8,128)(2,1)S(1)}, u32[]{:S(2)}, u32[]{:S(2)}) %collective-permute-start.3) | collective-permute-done | bytes 32800 | tf_op jit(solution)/shard_map/ppermute | solution.py:44
  18.2 2.2 %copy-done.1 = bf16[2048,1024]{1,0:T(8,128)(2,1)S(1)} copy-done((bf16[2048,1024]{1,0:T(8,128)(2,1)S(1)}, bf16[2048,1024]{1,0:T(8,128)(2,1)}, u32[]{:S(2)}) %copy-start.1) | copy-done | bytes 4194328
  20.4 1.3 %shard_map.60.refs_0_ = bf16[32,2048]{1,0:T(8,128)(2,1)S(1)} custom-call(bf16[32,1024]{1,0:T(8,128)(2,1)S(1)} %shard_map.59.refs_0_, bf16[2048,1024]{1,0:T(8,128)(2,1)S(1)} %copy-done.1), custom_call_target="tpu_custom_call" | custom-call | bytes 3690000 | tf_op jit(solution)/shard_map/pallas_call | solution.py:26
  21.7 0.0 copy-start.3
  21.8 5.8 %copy-done.3 = bf16[2048,4096]{1,0:T(8,128)(2,1)S(1)} copy-done((bf16[2048,4096]{1,0:T(8,128)(2,1)S(1)}, bf16[2048,4096]{1,0:T(8,128)(2,1)}, u32[]{:S(2)}) %copy-start.3) | copy-done | bytes 16777240
  27.5 3.0 %shard_map.61 = bf16[32,4096]{1,0:T(8,128)(2,1)S(1)} custom-call(bf16[32,2048]{1,0:T(8,128)(2,1)S(1)} %shard_map.60.refs_0_, bf16[2048,4096]{1,0:T(8,128)(2,1)S(1)} %copy-done.3), custom_call_target="tpu_custom_call" | custom-call | bytes 14760000 | tf_op jit(solution)/shard_map/pallas_call | solution.py:26
  30.6 0.0 slice-start.2
  30.6 0.0 slice-start.3
  30.6 0.0 copy-start.2
  30.6 0.1 collective-permute-start.4
  30.7 0.0 copy-start.4
  30.7 5.9 %copy-done.4 = bf16[2048,4096]{1,0:T(8,128)(2,1)S(1)} copy-done((bf16[2048,4096]{1,0:T(8,128)(2,1)S(1)}, bf16[2048,4096]{1,0:T(8,128)(2,1)}, u32[]{:S(2)}) %copy-start.4) | copy-done | bytes 16777240
  36.6 3.0 %shard_map.62 = bf16[32,4096]{1,0:T(8,128)(2,1)S(1)} custom-call(bf16[32,2048]{1,0:T(8,128)(2,1)S(1)} %shard_map.60.refs_0_, bf16[2048,4096]{1,0:T(8,128)(2,1)S(1)} %copy-done.4), custom_call_target="tpu_custom_call" | custom-call | bytes 14760000 | tf_op jit(solution)/shard_map/pallas_call | solution.py:26
  39.6 0.4 collective-permute-start.6
  40.1 0.0 collective-permute-done.4
  40.1 1.9 %collective-permute-start.5 = (bf16[32,2048]{1,0:T(8,128)(2,1)S(1)}, bf16[32,2048]{1,0:T(8,128)(2,1)S(1)}, u32[]{:S(2)}, u32[]{:S(2)}) collective-permute-start(bf16[32,2048]{1,0:T(8,128)(2,1)S(1)} %add_convert_fusion.1), channel_id=1, source_target_pairs={{0,8},{4,12},{8,0},{12,4},{1,9},{5,13},{9,1},{13,5},{2,10},{6,14},... | collective-permute-start | bytes 393224 | tf_op jit(solution)/shard_map/ppermute | solution.py:44
  42.0 0.0 collective-permute-done.6
  42.0 1.0 %collective-permute-start.7 = (bf16[32,2048]{1,0:T(8,128)(2,1)S(1)}, bf16[32,2048]{1,0:T(8,128)(2,1)S(1)}, u32[]{:S(2)}, u32[]{:S(2)}) collective-permute-start(bf16[32,2048]{1,0:T(8,128)(2,1)S(1)} %add_convert_fusion), channel_id=1, source_target_pairs={{0,8},{4,12},{8,0},{12,4},{1,9},{5,13},{9,1},{13,5},{2,10},{6,14},... | collective-permute-start | bytes 393224 | tf_op jit(solution)/shard_map/ppermute | solution.py:44
  43.0 3.5 %collective-permute-done.5 = bf16[32,2048]{1,0:T(8,128)(2,1)S(1)} collective-permute-done((bf16[32,2048]{1,0:T(8,128)(2,1)S(1)}, bf16[32,2048]{1,0:T(8,128)(2,1)S(1)}, u32[]{:S(2)}, u32[]{:S(2)}) %collective-permute-start.5) | collective-permute-done | bytes 131104 | tf_op jit(solution)/shard_map/ppermute | solution.py:44
  46.5 2.1 %collective-permute-done.7 = bf16[32,2048]{1,0:T(8,128)(2,1)S(1)} collective-permute-done((bf16[32,2048]{1,0:T(8,128)(2,1)S(1)}, bf16[32,2048]{1,0:T(8,128)(2,1)S(1)}, u32[]{:S(2)}, u32[]{:S(2)}) %collective-permute-start.7) | collective-permute-done | bytes 131104 | tf_op jit(solution)/shard_map/ppermute | solution.py:44
  48.6 0.1 multiply_convert_fusion.refs_1_
  48.7 0.1 collective-permute-start.8
  48.8 0.0 slice-done
  48.8 0.0 slice-done.1
  48.8 0.0 slice-done.2
  48.9 1.6 %shard_map.63.refs_3_ = f32[32,2048]{1,0:T(8,128)S(1)} custom-call(s32[1]{0:T(128)} %bitcast.1.refs_0_, bf16[32,2048]{1,0:T(8,128)(2,1)S(1)} %multiply_convert_fusion.refs_1_, bf16[4096,2048]{1,0:T(8,128)(2,1)S(1)} %bitcast.3), custom_call_target="tpu_custom_call" | custom-call | bytes 7380000 | tf_op jit(solution)/shard_map/pallas_call | solution.py:26
  50.4 0.0 collective-permute-done.8.refs_1_
  50.4 0.0 copy-done.2
  50.5 2.3 %shard_map.64 = bf16[32,1024]{1,0:T(8,128)(2,1)S(1)} custom-call(s32[1]{0:T(128)} %bitcast.refs_0_, bf16[32,2048]{1,0:T(8,128)(2,1)S(1)} %collective-permute-done.8.refs_1_, bf16[4096,2048]{1,0:T(8,128)(2,1)S(1)} %bitcast.3, f32[32,2048]{1,0:T(8,128)S(1)} %shard_map.63.refs_3_, bf16[2048,1024]{1,0:T(8,128)(2,1)S(1)} %copy-done.2), custom_call_target="tpu_custom_call" | custom-call | bytes 11070000 | tf_op jit(solution)/shard_map/pallas_call | solution.py:26
  52.8 2.9 %collective-permute-start.9 = (bf16[16,1024]{1,0:T(8,128)(2,1)S(1)}, bf16[16,1024]{1,0:T(8,128)(2,1)S(1)}, u32[]{:S(2)}, u32[]{:S(2)}) collective-permute-start(bf16[16,1024]{1,0:T(8,128)(2,1)S(1)} %slice.17), channel_id=1, source_target_pairs={{0,2},{1,3},{2,0},{3,1},{4,6},{5,7},{6,4},{7,5},{8,10},{9,11},{10,... | collective-permute-start | bytes 98312 | tf_op jit(solution)/shard_map/ppermute | solution.py:44
  55.7 2.0 %collective-permute-done.9 = bf16[16,1024]{1,0:T(8,128)(2,1)S(1)} collective-permute-done((bf16[16,1024]{1,0:T(8,128)(2,1)S(1)}, bf16[16,1024]{1,0:T(8,128)(2,1)S(1)}, u32[]{:S(2)}, u32[]{:S(2)}) %collective-permute-start.9) | collective-permute-done | bytes 32800 | tf_op jit(solution)/shard_map/ppermute | solution.py:44
  57.7 1.9 %collective-permute-start.10 = (bf16[8,1024]{1,0:T(8,128)(2,1)S(1)}, bf16[8,1024]{1,0:T(8,128)(2,1)S(1)}, u32[]{:S(2)}, u32[]{:S(2)}) collective-permute-start(bf16[8,1024]{1,0:T(8,128)(2,1)S(1)} %slice.19), channel_id=1, source_target_pairs={{0,1},{1,0},{2,3},{3,2},{4,5},{5,4},{6,7},{7,6},{8,9},{9,8},{10,11... | collective-permute-start | bytes 49160 | tf_op jit(solution)/shard_map/ppermute | solution.py:44
  59.6 1.9 %collective-permute-done.10 = bf16[8,1024]{1,0:T(8,128)(2,1)S(1)} collective-permute-done((bf16[8,1024]{1,0:T(8,128)(2,1)S(1)}, bf16[8,1024]{1,0:T(8,128)(2,1)S(1)}, u32[]{:S(2)}, u32[]{:S(2)}) %collective-permute-start.10) | collective-permute-done | bytes 16416 | tf_op jit(solution)/shard_map/ppermute | solution.py:44
  61.5 1.7 %collective-permute-start.11 = (bf16[8,1024]{1,0:T(8,128)(2,1)S(1)}, bf16[8,1024]{1,0:T(8,128)(2,1)S(1)}, u32[]{:S(2)}, u32[]{:S(2)}) collective-permute-start(bf16[8,1024]{1,0:T(8,128)(2,1)S(1)} %add_convert_fusion.5), channel_id=1, source_target_pairs={{0,8},{4,12},{8,0},{12,4},{1,9},{5,13},{9,1},{13,5},{2,10},{6,14},... | collective-permute-start | bytes 49160 | tf_op jit(solution)/shard_map/ppermute | solution.py:44
  63.3 2.1 %collective-permute-done.11 = bf16[8,1024]{1,0:T(8,128)(2,1)S(1)} collective-permute-done((bf16[8,1024]{1,0:T(8,128)(2,1)S(1)}, bf16[8,1024]{1,0:T(8,128)(2,1)S(1)}, u32[]{:S(2)}, u32[]{:S(2)}) %collective-permute-start.11) | collective-permute-done | bytes 16416 | tf_op jit(solution)/shard_map/ppermute | solution.py:44
  65.3 0.1 collective-permute-start.12
  65.4 1.2 %collective-permute-done.12 = bf16[8,1024]{1,0:T(8,128)(2,1)S(1)} collective-permute-done((bf16[8,1024]{1,0:T(8,128)(2,1)S(1)}, bf16[8,1024]{1,0:T(8,128)(2,1)S(1)}, u32[]{:S(2)}, u32[]{:S(2)}) %collective-permute-start.12) | collective-permute-done | bytes 16416 | tf_op jit(solution)/shard_map/ppermute | solution.py:44
  66.6 1.8 %shard_map.65 = bf16[8,2048]{1,0:T(8,128)(2,1)} custom-call(bf16[8,1024]{1,0:T(8,128)(2,1)S(1)} %add_convert_fusion.3.refs_0_, bf16[2048,1024]{1,0:T(8,128)(2,1)S(1)} %copy-done.2), custom_call_target="tpu_custom_call" | custom-call | bytes 3690000 | tf_op jit(solution)/shard_map/pallas_call | solution.py:26
  (21 shorter events, 0.2 us)
Async XLA Ops:
  0.0 2.2 %copy-start = (bf16[2048,1024]{1,0:T(8,128)(2,1)S(1)}, bf16[2048,1024]{1,0:T(8,128)(2,1)}, u32[]{:S(2)}) copy-start(bf16[2048,1024]{1,0:T(8,128)(2,1)} %refs_1_.9) | copy-start | bytes 12582916
  2.2 0.8 %copy-start.5 = (bf16[8,2048]{1,0:T(8,128)(2,1)S(1)}, bf16[8,2048]{1,0:T(8,128)(2,1)}, u32[]{:S(2)}) copy-start(bf16[8,2048]{1,0:T(8,128)(2,1)} %refs_0_.1) | copy-start | bytes 98308
  3.6 1.3 %collective-permute-start = (bf16[8,1024]{1,0:T(8,128)(2,1)S(1)}, bf16[8,1024]{1,0:T(8,128)(2,1)S(1)}, u32[]{:S(2)}, u32[]{:S(2)}) collective-permute-start(bf16[8,1024]{1,0:T(8,128)(2,1)S(1)} %shard_map.55.refs_0_), channel_id=1, source_target_pairs={{0,4},{4,0},{8,12},{12,8},{1,5},{5,1},{9,13},{13,9},{2,6},{6,2},{1... | collective-permute-start | bytes 49160 | tf_op jit(solution)/shard_map/ppermute | solution.py:44
  4.9 4.5 %collective-permute-start.1 = (bf16[8,1024]{1,0:T(8,128)(2,1)S(1)}, bf16[8,1024]{1,0:T(8,128)(2,1)S(1)}, u32[]{:S(2)}, u32[]{:S(2)}) collective-permute-start(bf16[8,1024]{1,0:T(8,128)(2,1)S(1)} %shard_map.56.refs_0_), channel_id=1, source_target_pairs={{0,8},{4,12},{8,0},{12,4},{1,9},{5,13},{9,1},{13,5},{2,10},{6,14},... | collective-permute-start | bytes 49160 | tf_op jit(solution)/shard_map/ppermute | solution.py:44
  9.5 3.8 %collective-permute-start.2 = (bf16[8,1024]{1,0:T(8,128)(2,1)S(1)}, bf16[8,1024]{1,0:T(8,128)(2,1)S(1)}, u32[]{:S(2)}, u32[]{:S(2)}) collective-permute-start(bf16[8,1024]{1,0:T(8,128)(2,1)S(1)} %shard_map.57.refs_0_), channel_id=1, source_target_pairs={{0,1},{1,0},{2,3},{3,2},{4,5},{5,4},{6,7},{7,6},{8,9},{9,8},{10,11... | collective-permute-start | bytes 49160 | tf_op jit(solution)/shard_map/ppermute | solution.py:44
  13.3 4.9 %collective-permute-start.3 = (bf16[16,1024]{1,0:T(8,128)(2,1)S(1)}, bf16[16,1024]{1,0:T(8,128)(2,1)S(1)}, u32[]{:S(2)}, u32[]{:S(2)}) collective-permute-start(bf16[16,1024]{1,0:T(8,128)(2,1)S(1)} %shard_map.58.refs_0_), channel_id=1, source_target_pairs={{0,2},{1,3},{2,0},{3,1},{4,6},{5,7},{6,4},{7,5},{8,10},{9,11},{10,... | collective-permute-start | bytes 98312 | tf_op jit(solution)/shard_map/ppermute | solution.py:44
  18.2 2.2 %copy-start.1 = (bf16[2048,1024]{1,0:T(8,128)(2,1)S(1)}, bf16[2048,1024]{1,0:T(8,128)(2,1)}, u32[]{:S(2)}) copy-start(bf16[2048,1024]{1,0:T(8,128)(2,1)} %refs_1_.9) | copy-start | bytes 12582916
  21.7 5.8 %copy-start.3 = (bf16[2048,4096]{1,0:T(8,128)(2,1)S(1)}, bf16[2048,4096]{1,0:T(8,128)(2,1)}, u32[]{:S(2)}) copy-start(bf16[2048,4096]{1,0:T(8,128)(2,1)} %refs_1_.7) | copy-start | bytes 50331652
  27.5 21.3 %slice-start = ((s8[16777216]{0:T(1024)(128)(4,1)}), s8[4194304]{0:T(1024)(128)(4,1)S(1)}, s32[]{:S(2)}) async-start(s8[16777216]{0:T(1024)(128)(4,1)} %bitcast.2), calls=%async_computation | async-start | bytes 8388608
  27.5 21.3 %slice-start.1 = ((s8[16777216]{0:T(1024)(128)(4,1)}), s8[4194304]{0:T(1024)(128)(4,1)S(1)}, s32[]{:S(2)}) async-start(s8[16777216]{0:T(1024)(128)(4,1)} %bitcast.2), calls=%async_computation.1 | async-start | bytes 8388608
  30.6 18.3 %slice-start.2 = ((s8[16777216]{0:T(1024)(128)(4,1)}), s8[4194304]{0:T(1024)(128)(4,1)S(1)}, s32[]{:S(2)}) async-start(s8[16777216]{0:T(1024)(128)(4,1)} %bitcast.2), calls=%async_computation.2 | async-start | bytes 8388608
  30.6 18.3 %slice-start.3 = ((s8[16777216]{0:T(1024)(128)(4,1)}), s8[4194304]{0:T(1024)(128)(4,1)S(1)}, s32[]{:S(2)}) async-start(s8[16777216]{0:T(1024)(128)(4,1)} %bitcast.2), calls=%async_computation.3 | async-start | bytes 8388608
  30.6 19.8 %copy-start.2 = (bf16[2048,1024]{1,0:T(8,128)(2,1)S(1)}, bf16[2048,1024]{1,0:T(8,128)(2,1)}, u32[]{:S(2)}) copy-start(bf16[2048,1024]{1,0:T(8,128)(2,1)} %refs_1_.9) | copy-start | bytes 12582916
  30.6 9.4 %collective-permute-start.4 = (bf16[32,2048]{1,0:T(8,128)(2,1)S(1)}, bf16[32,2048]{1,0:T(8,128)(2,1)S(1)}, u32[]{:S(2)}, u32[]{:S(2)}) collective-permute-start(bf16[32,2048]{1,0:T(8,128)(2,1)S(1)} %constant_dynamic-slice_fusion.1), channel_id=1, source_target_pairs={{0,4},{4,0},{8,12},{12,8},{1,5},{5,1},{9,13},{13,9},{2,6},{6,2},{1... | collective-permute-start | bytes 393224 | tf_op jit(solution)/shard_map/ppermute | solution.py:44
  30.7 5.9 %copy-start.4 = (bf16[2048,4096]{1,0:T(8,128)(2,1)S(1)}, bf16[2048,4096]{1,0:T(8,128)(2,1)}, u32[]{:S(2)}) copy-start(bf16[2048,4096]{1,0:T(8,128)(2,1)} %refs_1_.8) | copy-start | bytes 50331652
  39.6 2.3 %collective-permute-start.6 = (bf16[32,2048]{1,0:T(8,128)(2,1)S(1)}, bf16[32,2048]{1,0:T(8,128)(2,1)S(1)}, u32[]{:S(2)}, u32[]{:S(2)}) collective-permute-start(bf16[32,2048]{1,0:T(8,128)(2,1)S(1)} %constant_dynamic-slice_fusion), channel_id=1, source_target_pairs={{0,4},{4,0},{8,12},{12,8},{1,5},{5,1},{9,13},{13,9},{2,6},{6,2},{1... | collective-permute-start | bytes 393224 | tf_op jit(solution)/shard_map/ppermute | solution.py:44
  40.1 6.4 %collective-permute-start.5 = (bf16[32,2048]{1,0:T(8,128)(2,1)S(1)}, bf16[32,2048]{1,0:T(8,128)(2,1)S(1)}, u32[]{:S(2)}, u32[]{:S(2)}) collective-permute-start(bf16[32,2048]{1,0:T(8,128)(2,1)S(1)} %add_convert_fusion.1), channel_id=1, source_target_pairs={{0,8},{4,12},{8,0},{12,4},{1,9},{5,13},{9,1},{13,5},{2,10},{6,14},... | collective-permute-start | bytes 393224 | tf_op jit(solution)/shard_map/ppermute | solution.py:44
  42.0 6.6 %collective-permute-start.7 = (bf16[32,2048]{1,0:T(8,128)(2,1)S(1)}, bf16[32,2048]{1,0:T(8,128)(2,1)S(1)}, u32[]{:S(2)}, u32[]{:S(2)}) collective-permute-start(bf16[32,2048]{1,0:T(8,128)(2,1)S(1)} %add_convert_fusion), channel_id=1, source_target_pairs={{0,8},{4,12},{8,0},{12,4},{1,9},{5,13},{9,1},{13,5},{2,10},{6,14},... | collective-permute-start | bytes 393224 | tf_op jit(solution)/shard_map/ppermute | solution.py:44
  48.7 1.7 %collective-permute-start.8 = (bf16[32,2048]{1,0:T(8,128)(2,1)S(1)}, bf16[32,2048]{1,0:T(8,128)(2,1)S(1)}, u32[]{:S(2)}, u32[]{:S(2)}) collective-permute-start(bf16[32,2048]{1,0:T(8,128)(2,1)S(1)} %multiply_convert_fusion.refs_1_), channel_id=1, source_target_pairs={{0,4},{4,0},{8,12},{12,8},{1,5},{5,1},{9,13},{13,9},{2,6},{6,2},{1... | collective-permute-start | bytes 393224 | tf_op jit(solution)/shard_map/ppermute | solution.py:44
  52.8 4.9 %collective-permute-start.9 = (bf16[16,1024]{1,0:T(8,128)(2,1)S(1)}, bf16[16,1024]{1,0:T(8,128)(2,1)S(1)}, u32[]{:S(2)}, u32[]{:S(2)}) collective-permute-start(bf16[16,1024]{1,0:T(8,128)(2,1)S(1)} %slice.17), channel_id=1, source_target_pairs={{0,2},{1,3},{2,0},{3,1},{4,6},{5,7},{6,4},{7,5},{8,10},{9,11},{10,... | collective-permute-start | bytes 98312 | tf_op jit(solution)/shard_map/ppermute | solution.py:44
  57.7 3.8 %collective-permute-start.10 = (bf16[8,1024]{1,0:T(8,128)(2,1)S(1)}, bf16[8,1024]{1,0:T(8,128)(2,1)S(1)}, u32[]{:S(2)}, u32[]{:S(2)}) collective-permute-start(bf16[8,1024]{1,0:T(8,128)(2,1)S(1)} %slice.19), channel_id=1, source_target_pairs={{0,1},{1,0},{2,3},{3,2},{4,5},{5,4},{6,7},{7,6},{8,9},{9,8},{10,11... | collective-permute-start | bytes 49160 | tf_op jit(solution)/shard_map/ppermute | solution.py:44
  61.5 3.8 %collective-permute-start.11 = (bf16[8,1024]{1,0:T(8,128)(2,1)S(1)}, bf16[8,1024]{1,0:T(8,128)(2,1)S(1)}, u32[]{:S(2)}, u32[]{:S(2)}) collective-permute-start(bf16[8,1024]{1,0:T(8,128)(2,1)S(1)} %add_convert_fusion.5), channel_id=1, source_target_pairs={{0,8},{4,12},{8,0},{12,4},{1,9},{5,13},{9,1},{13,5},{2,10},{6,14},... | collective-permute-start | bytes 49160 | tf_op jit(solution)/shard_map/ppermute | solution.py:44
  65.3 1.2 %collective-permute-start.12 = (bf16[8,1024]{1,0:T(8,128)(2,1)S(1)}, bf16[8,1024]{1,0:T(8,128)(2,1)S(1)}, u32[]{:S(2)}, u32[]{:S(2)}) collective-permute-start(bf16[8,1024]{1,0:T(8,128)(2,1)S(1)} %add_convert_fusion.4), channel_id=1, source_target_pairs={{0,4},{4,0},{8,12},{12,8},{1,5},{5,1},{9,13},{13,9},{2,6},{6,2},{1... | collective-permute-start | bytes 49160 | tf_op jit(solution)/shard_map/ppermute | solution.py:44

commit v2 on v0

v2 whole, which is shorter than its diff:
```python
import functools

import jax
import jax.numpy as jnp
from jax import lax
from jax.experimental import pallas as pl
from jax.experimental.pallas import tpu as pltpu
from jax.sharding import PartitionSpec as P

D = 8192
R = 1024
F32 = jnp.float32
BF16 = jnp.bfloat16
LIMIT = 2 * 1024 * 1024
PIECES = 4
WAIT = 30
SUM = 6
PAIR = 1
VMEM = pl.BlockSpec(memory_space=pltpu.VMEM)
HBM = pl.BlockSpec(memory_space=pltpu.HBM)
sds = jax.ShapeDtypeStruct


def call(body, out, microseconds, *arrays, scratch=(), fixed=()):
    many = isinstance(out, list)
    return pl.pallas_call(
        body,
        out_shape=out,
        in_specs=[HBM if i in fixed else VMEM for i in range(len(arrays))],
        out_specs=[VMEM] * len(out) if many else VMEM,
        scratch_shapes=list(scratch),
        cost_estimate=pl.CostEstimate(flops=int(microseconds * 1.15e9), bytes_accessed=2**16, transcendentals=0),
        compiler_params=pltpu.CompilerParams(vmem_limit_bytes=LIMIT),
    )(*[pltpu.with_memory_space_constraint(a, pltpu.HBM) if i in fixed else a for i, a in enumerate(arrays)])


def swap(value, axis, mask, size):
    return lax.ppermute(value, axis, [(i, i ^ mask) for i in range(size)])


def tile_of(extent, most):
    tile = most
    while extent % tile:
        tile //= 2
    return tile


def dot(a, b):
    return jnp.dot(a, b, preferred_element_type=F32)


def dot_t(a, b):
    return lax.dot_general(a, b, (((1,), (1,)), ((), ())), preferred_element_type=F32)


def core_index():
    return lax.rem(lax.axis_index("dp"), 2)


def code_body(x_ref, basis_ref, out_ref, held_ref, tokens_ref, sems):
    deep = basis_ref.shape[0] // PIECES
    first = pltpu.make_async_copy(x_ref, tokens_ref, sems.at[PIECES])
    first.start()
    copies = []
    for p in range(PIECES):
        at = pl.ds(p * deep, deep)
        copies.append(pltpu.make_async_copy(basis_ref.at[at], held_ref.at[at], sems.at[p]))
        copies[-1].start()
    first.wait()
    for p in range(PIECES):
        copies[p].wait()
        part = dot(tokens_ref[:, p * deep : (p + 1) * deep], held_ref[p * deep : (p + 1) * deep, :])
        out_ref[...] = part if p == 0 else out_ref[...] + part


def add_body(a_ref, b_ref, *out_refs):
    total = a_ref[...] + b_ref[...].astype(F32)
    for out_ref in out_refs:
        out_ref[...] = total.astype(out_ref.dtype)


def half_body(a_ref, b_ref, keep_ref, send_ref):
    top = keep_ref.shape[0]
    keep_ref[...] = a_ref[:top] + b_ref[:top].astype(F32)
    send_ref[...] = (a_ref[top:] + b_ref[top:].astype(F32)).astype(BF16)


def join_body(a_ref, b_ref, out_ref):
    rows = a_ref.shape[0]
    out_ref[:rows] = a_ref[...]
    out_ref[rows:] = b_ref[...]


def hidden_body(a_ref, b_ref, out_ref):
    half = out_ref.shape[1]
    gate = a_ref[:, :half] + b_ref[:, :half].astype(F32)
    up = a_ref[:, half:] + b_ref[:, half:].astype(F32)
    out_ref[...] = (gate / (1 + jnp.exp(-gate)) * up).astype(BF16)


def decode(codes, basis_ref, out_ref):
    factor = (D / R) ** 0.5
    width = basis_ref.shape[0]
    tile = tile_of(width, 512)
    for t in range(0, width, tile):
        out_ref[:, t : t + tile] = (factor * dot_t(codes, basis_ref[t : t + tile, :])).astype(BF16)


def restore_body(codes_ref, basis_ref, out_ref):
    decode(codes_ref[...], basis_ref, out_ref)


def final_body(a_ref, b_ref, basis_ref, out_ref):
    decode((a_ref[...] + b_ref[...]).astype(BF16), basis_ref, out_ref)


def pair_body(x_ref, gate_ref, up_ref, *refs, start):
    keep_ref, send_ref = refs[-2:]
    half = keep_ref.shape[1] // 2
    tile = tile_of(half, 512)
    core = core_index()
    for out_ref, which in ((send_ref, 1 - core), (keep_ref, core)):
        for t in range(0, half, tile):
            at = pl.ds(pl.multiple_of(start + t + which * half, 128), tile)
            out_ref[:, t : t + tile] = dot(x_ref[...], gate_ref[:, at]).astype(out_ref.dtype)
            out_ref[:, half + t : half + t + tile] = dot(x_ref[...], up_ref[:, at]).astype(out_ref.dtype)


def down_body(*refs, start, half, own, away, first):
    h_refs, (weight_ref, *acc, out_ref) = refs[: own + away], refs[own + away :]
    core = core_index()
    which = ([core] if own else []) + ([1 - core] if away else [])
    width = out_ref.shape[1]
    tile = tile_of(width, 512)
    for t in range(0, width, tile):
        total = None if first else acc[0][:, t : t + tile]
        for h_ref, w in zip(h_refs, which):
            at = pl.ds(pl.multiple_of(start + w * half, 16), half)
            part = dot(h_ref[...], weight_ref[at, t : t + tile])
            total = part if total is None else total + part
        out_ref[:, t : t + tile] = total.astype(out_ref.dtype)


def last_body(h_ref, weight_ref, acc_ref, basis_ref, keep_ref, send_ref, rows_ref, *, start, half):
    down_body(h_ref, weight_ref, acc_ref, rows_ref, start=start, half=half, own=0, away=1, first=False)
    top = keep_ref.shape[0]
    tile = tile_of(R, 512)
    for t in range(0, R, tile):
        part = dot(rows_ref[...], basis_ref[:, t : t + tile])
        keep_ref[:, t : t + tile] = part[:top]
        send_ref[:, t : t + tile] = part[top:].astype(BF16)


def both(shape):
    return [sds(shape, F32), sds(shape, BF16)]


def shards(tokens, basis, gate_weight, up_weight, down_weight, *, dp, tensor):
    local, width = tokens.shape
    rows = local * tensor
    ff = gate_weight.shape[1]

    codes, basis = call(
        code_body,
        [sds((local, R), F32), sds(basis.shape, BF16)],
        1,
        tokens,
        basis,
        scratch=[pltpu.VMEM(tokens.shape, BF16), pltpu.SemaphoreType.DMA((PIECES + 1,))],
        fixed=(0, 1),
    )
    codes, send = call(add_body, both(codes.shape), WAIT, codes, swap(codes, "dp", 1, dp))
    mask = 2
    while 2 * mask < dp:
        codes, send = call(add_body, both(codes.shape), 0.1, codes, swap(send, "dp", mask, dp))
        mask *= 2
    codes = call(add_body, sds(codes.shape, BF16), 0.1, codes, swap(send, "dp", mask, dp))
    mask = 1
    while mask < tensor:
        codes = call(
            join_body, sds((2 * codes.shape[0], R), BF16), 0.1, codes, swap(codes, "tensor", mask, tensor)
        )
        mask *= 2
    restored = call(restore_body, sds((rows, width), BF16), 0.5, codes, basis)

    shares = SHARES if ff % 1024 == 0 else (1, 1)
    spans, at = [], 0
    for share in shares:
        spans.append((at, ff * share // sum(shares)))
        at += spans[-1][1]
    sums = []
    after = []
    for q, (start, span) in enumerate(spans):
        keep, send = call(
            functools.partial(pair_body, start=start),
            both((rows, span)),
            PAIR * span / ff,
            restored,
            gate_weight,
            up_weight,
            *after,
        )
        sums.append((keep, swap(send, "dp", 1, dp)))
        after = [keep]
        if q > 0:
            sums[q - 1] = call(add_body, both((rows, spans[q - 1][1])), SUM, *sums[q - 1])
            after.append(sums[q - 1][1])
    sums[-1] = call(add_body, both((rows, spans[-1][1])), SUM, *sums[-1])
    acc = None
    for (start, span), (total, send) in zip(spans, sums):
        mask = 2
        while 2 * mask < dp:
            total, send = call(add_body, both(total.shape), 0.1, total, swap(send, "dp", mask, dp))
            mask *= 2
        half = span // 2
        own = call(hidden_body, sds((rows, half), BF16), 0.1, total, swap(send, "dp", mask, dp))
        away = swap(own, "dp", 1, dp)
        time = 3 * span / ff
        shape = sds((rows, width), F32)
        if start + span < ff:
            body = functools.partial(down_body, start=start, half=half, own=1, away=1, first=acc is None)
            acc = call(body, shape, time, own, away, down_weight, *([] if acc is None else [acc]))
        else:
            body = functools.partial(down_body, start=start, half=half, own=1, away=0, first=False)
            acc = call(body, shape, time / 2, own, down_weight, acc)
            codes, send = call(
                functools.partial(last_body, start=start, half=half),
                [sds((rows // 2, R), F32), sds((rows // 2, R), BF16)],
                1,
                away,
                down_weight,
                acc,
                basis,
                scratch=[pltpu.VMEM((rows, width), BF16)],
            )

    mask = tensor // 2
    while mask > 1:
        top = codes.shape[0] // 2
        codes, send = call(
            half_body, [sds((top, R), F32), sds((top, R), BF16)], 0.1, codes, swap(send, "tensor", mask, tensor)
        )
        mask //= 2
    codes, send = call(add_body, both(codes.shape), 0.1, codes, swap(send, "tensor", 1, tensor))
    mask = dp // 2
    while mask > 1:
        codes, send = call(add_body, both(codes.shape), 0.1, codes, swap(send, "dp", mask, dp))
        mask //= 2
    return call(final_body, sds((local, width), BF16), 1, codes, swap(codes, "dp", 1, dp), basis)


SHARES = (2, 1, 1)


def solution(mesh):
    placed = (
        P(("groups", "tensor"), "dp"),
        P("dp", None),
        P("dp", "tensor"),
        P("dp", "tensor"),
        P("tensor", "dp"),
    )
    return jax.shard_map(
        functools.partial(shards, dp=mesh.shape["dp"], tensor=mesh.shape["tensor"]),
        mesh=mesh,
        in_specs=placed,
        out_specs=P(("groups", "tensor"), "dp"),
        check_vma=False,
    )
```

time: 146 us -> 55.5 us (0.38)
  waiting for transfers between devices: 56.5 us -> 18.7 us
  matrix products: 37.6 us -> 0 us
  blocking collectives: 36.6 us -> 0 us
  starting transfers between devices: 0.04 us -> 19.5 us
  Pallas kernels: 0 us -> 16.7 us
  between operations: 13.4 us -> 0.26 us
  local copies, waits for them, and re-layouts: 1.77 us -> 0.07 us
    dot_general x7 -> x0, matrix products: 37.6 us -> none  [the longest x1 9.81 us: shards(): jnp.dot(hidden, down_weight, preferred_element_type=jnp.float32)]
    psum x1 -> x0, waiting for transfers between devices: 36.3 us -> none  [shards(): gate_sum, up_sum = lax.psum((gate_part, up_part), 'dp')]
    psum x2 -> x0, blocking collectives: 23.1 us -> none  [the longest x1 12.9 us: shards(): code_rows = lax.psum(partial_value, 'dp').astype(jnp.bfloat16)]
    reduce_scatter x1 -> x0, waiting for transfers between devices: 20.2 us -> none  [shards(): lax.psum_scatter(jnp.dot(hidden, down_weight, preferred_element_type=jnp....]
    ppermute x0 -> x17, starting transfers between devices: none -> 19.5 us  [swap(): return lax.ppermute(value, axis, [(i, i ^ mask) for i in range(size)])]
    ppermute x0 -> x17, waiting for transfers between devices: none -> 18.7 us  [swap(): return lax.ppermute(value, axis, [(i, i ^ mask) for i in range(size)])]
    pallas_call x0 -> x23, Pallas kernels: none -> 16.7 us  [call(): pl.pallas_call(body, out_shape=out, in_specs=[HBM if i in fixed else VMEM...]
    all_gather x1 -> x0, blocking collectives: 13.4 us -> none  [shards(): lax.all_gather(code_rows, 'tensor', axis=0, tiled=True)]
  transfers between devices with their start and end apart: 2 -> 17, of which waited for: 2 -> 10; matrix products, arithmetic and copies ran while one was open for 0% -> 0% of each run, Pallas kernels for 0% -> 11%
where the time goes in v2:
time: 55.5 us; the launch traced here: 55.3 us
  starting transfers between devices  19.5 us (35%)
  waiting for transfers between devices  18.7 us (34%)
  Pallas kernels  16.7 us (30%)
    ppermute x17, starting transfers between devices, swap(): return lax.ppermute(value, axis, [(i, i ^ mask) for i in range(size)])  19.5 us
    ppermute x17, waiting for transfers between devices, swap(): return lax.ppermute(value, axis, [(i, i ^ mask) for i in range(size)])  18.7 us
    pallas_call x23, Pallas kernels, call(): pl.pallas_call(body, out_shape=out, in_specs=[HBM if i in fixed else VMEM...  16.7 us
  transfers between devices with their start and end apart: 17, of which 10 were waited for; matrix products, arithmetic and copies ran while one was open for 0% of the time, Pallas kernels for 11%

profile of v2, /device:TPU:0, one launch (start us, length us, event | category | flops | bytes accessed | tf_op | source)
XLA Modules:
  0.0 55.3 jit_solution(5544344928442002185)
XLA Ops:
  0.0 2.5 %shard_map.55 = (f32[8,1024]{1,0:T(8,128)S(1)}, bf16[2048,1024]{1,0:T(8,128)(2,1)S(1)}) custom-call(bf16[8,2048]{1,0:T(8,128)(2,1)} %x_ref.1, bf16[2048,1024]{1,0:T(8,128)(2,1)} %basis_ref.1), custom_call_target="tpu_custom_call" | custom-call | flops 1150000000 | bytes 65536 | tf_op jit(solution)/shard_map/pallas_call | solution.py:26
  2.5 0.0 slice-start.4
  2.5 0.0 slice-start.8
  2.5 0.0 slice-start.5
  2.5 0.0 slice-start.6
  2.6 0.0 slice-start.9
  2.6 0.0 slice-start.10
  2.6 0.5 collective-permute-start
  3.1 0.9 %collective-permute-done.b_ref = f32[8,1024]{1,0:T(8,128)S(1)} collective-permute-done((f32[8,1024]{1,0:T(8,128)S(1)}, f32[8,1024]{1,0:T(8,128)S(1)}, u32[]{:S(2)}, u32[]{:S(2)}) %collective-permute-start) | collective-permute-done | bytes 32800 | tf_op jit(solution)/shard_map/ppermute | solution.py:38
  4.0 2.8 %collective-permute-start.1 = (bf16[8,1024]{1,0:T(8,128)(2,1)S(1)}, bf16[8,1024]{1,0:T(8,128)(2,1)S(1)}, u32[]{:S(2)}, u32[]{:S(2)}) collective-permute-start(bf16[8,1024]{1,0:T(8,128)(2,1)S(1)} %get-tuple-element.30), channel_id=1, source_target_pairs={{0,8},{4,12},{8,0},{12,4},{1,9},{5,13},{9,1},{13,5},{2,10},{6,14},... | collective-permute-start | bytes 49160 | tf_op jit(solution)/shard_map/ppermute | solution.py:38
  6.8 1.7 %collective-permute-done.1.b_ref = bf16[8,1024]{1,0:T(8,128)(2,1)S(1)} collective-permute-done((bf16[8,1024]{1,0:T(8,128)(2,1)S(1)}, bf16[8,1024]{1,0:T(8,128)(2,1)S(1)}, u32[]{:S(2)}, u32[]{:S(2)}) %collective-permute-start.1) | collective-permute-done | bytes 16416 | tf_op jit(solution)/shard_map/ppermute | solution.py:38
  8.5 2.1 %collective-permute-start.2 = (bf16[8,1024]{1,0:T(8,128)(2,1)S(1)}, bf16[8,1024]{1,0:T(8,128)(2,1)S(1)}, u32[]{:S(2)}, u32[]{:S(2)}) collective-permute-start(bf16[8,1024]{1,0:T(8,128)(2,1)S(1)} %shard_map.57.a_ref), channel_id=1, source_target_pairs={{0,1},{1,0},{2,3},{3,2},{4,5},{5,4},{6,7},{7,6},{8,9},{9,8},{10,11... | collective-permute-start | bytes 49160 | tf_op jit(solution)/shard_map/ppermute | solution.py:38
  10.6 1.7 %collective-permute-done.2.b_ref = bf16[8,1024]{1,0:T(8,128)(2,1)S(1)} collective-permute-done((bf16[8,1024]{1,0:T(8,128)(2,1)S(1)}, bf16[8,1024]{1,0:T(8,128)(2,1)S(1)}, u32[]{:S(2)}, u32[]{:S(2)}) %collective-permute-start.2) | collective-permute-done | bytes 16416 | tf_op jit(solution)/shard_map/ppermute | solution.py:38
  12.4 3.0 %collective-permute-start.3 = (bf16[16,1024]{1,0:T(8,128)(2,1)S(1)}, bf16[16,1024]{1,0:T(8,128)(2,1)S(1)}, u32[]{:S(2)}, u32[]{:S(2)}) collective-permute-start(bf16[16,1024]{1,0:T(8,128)(2,1)S(1)} %shard_map.58.a_ref), channel_id=1, source_target_pairs={{0,2},{1,3},{2,0},{3,1},{4,6},{5,7},{6,4},{7,5},{8,10},{9,11},{10,... | collective-permute-start | bytes 98312 | tf_op jit(solution)/shard_map/ppermute | solution.py:38
  15.4 1.9 %collective-permute-done.3.b_ref = bf16[16,1024]{1,0:T(8,128)(2,1)S(1)} collective-permute-done((bf16[16,1024]{1,0:T(8,128)(2,1)S(1)}, bf16[16,1024]{1,0:T(8,128)(2,1)S(1)}, u32[]{:S(2)}, u32[]{:S(2)}) %collective-permute-start.3) | collective-permute-done | bytes 32800 | tf_op jit(solution)/shard_map/ppermute | solution.py:38
  17.3 1.3 %shard_map.60.x_ref = bf16[32,2048]{1,0:T(8,128)(2,1)S(1)} custom-call(bf16[32,1024]{1,0:T(8,128)(2,1)S(1)} %shard_map.59.codes_ref, bf16[2048,1024]{1,0:T(8,128)(2,1)S(1)} %get-tuple-element.31.basis_ref), custom_call_target="tpu_custom_call" | custom-call | flops 575000000 | bytes 65536 | tf_op jit(solution)/shard_map/pallas_call | solution.py:26
  18.6 0.0 slice-done.4
  18.7 3.0 %shard_map.61 = (f32[32,2048]{1,0:T(8,128)S(1)}, bf16[32,2048]{1,0:T(8,128)(2,1)S(1)}) custom-call(bf16[32,2048]{1,0:T(8,128)(2,1)S(1)} %shard_map.60.x_ref, bf16[2048,4096]{1,0:T(8,128)(2,1)S(1)} %bitcast.3, bf16[2048,4096]{1,0:T(8,128)(2,1)S(1)} %bitcast.5), custom_call_target="tpu_custom_call" | custom-call | flops 575000000 | bytes 65536 | tf_op jit(solution)/shard_map/pallas_call | solution.py:26
  21.7 0.0 collective-permute-start.4
  21.7 1.6 %shard_map.62 = (f32[32,1024]{1,0:T(8,128)S(1)}, bf16[32,1024]{1,0:T(8,128)(2,1)S(1)}) custom-call(bf16[32,2048]{1,0:T(8,128)(2,1)S(1)} %shard_map.60.x_ref, bf16[2048,4096]{1,0:T(8,128)(2,1)S(1)} %bitcast.3, bf16[2048,4096]{1,0:T(8,128)(2,1)S(1)} %bitcast.5, f32[32,2048]{1,0:T(8,128)S(1)} %get-tuple-element.32.refs_0_.a_ref), custom_call_target="tpu_custom_call" | custom-call | flops 287500000 | bytes 65536 | tf_op jit(solution)/shard_map/pallas_call | solution.py:26
  23.3 0.5 collective-permute-start.8
  23.8 0.0 collective-permute-done.4.b_ref
  23.9 1.6 %shard_map.64 = (f32[32,1024]{1,0:T(8,128)S(1)}, bf16[32,1024]{1,0:T(8,128)(2,1)S(1)}) custom-call(bf16[32,2048]{1,0:T(8,128)(2,1)S(1)} %shard_map.60.x_ref, bf16[2048,4096]{1,0:T(8,128)(2,1)S(1)} %bitcast.3, bf16[2048,4096]{1,0:T(8,128)(2,1)S(1)} %bitcast.5, f32[32,1024]{1,0:T(8,128)S(1)} %get-tuple-element.33.refs_0_.a_ref, ...), custom_call_target="tpu_custom_call" | custom-call | flops 287500000 | bytes 65536 | tf_op jit(solution)/shard_map/pallas_call | solution.py:26
  25.5 0.0 collective-permute-start.5
  25.5 0.0 slice-start.1
  25.5 1.9 %collective-permute-start.9 = (bf16[32,1024]{1,0:T(8,128)(2,1)S(1)}, bf16[32,1024]{1,0:T(8,128)(2,1)S(1)}, u32[]{:S(2)}, u32[]{:S(2)}) collective-permute-start(bf16[32,1024]{1,0:T(8,128)(2,1)S(1)} %get-tuple-element.42), channel_id=1, source_target_pairs={{0,8},{4,12},{8,0},{12,4},{1,9},{5,13},{9,1},{13,5},{2,10},{6,14},... | collective-permute-start | bytes 196616 | tf_op jit(solution)/shard_map/ppermute | solution.py:38
  27.4 0.2 collective-permute-start.11
  27.7 1.9 %collective-permute-start.6 = (bf16[32,1024]{1,0:T(8,128)(2,1)S(1)}, bf16[32,1024]{1,0:T(8,128)(2,1)S(1)}, u32[]{:S(2)}, u32[]{:S(2)}) collective-permute-start(bf16[32,1024]{1,0:T(8,128)(2,1)S(1)} %get-tuple-element.39), channel_id=1, source_target_pairs={{0,8},{4,12},{8,0},{12,4},{1,9},{5,13},{9,1},{13,5},{2,10},{6,14},... | collective-permute-start | bytes 196616 | tf_op jit(solution)/shard_map/ppermute | solution.py:38
  29.6 4.2 %collective-permute-done.11.b_ref = bf16[32,2048]{1,0:T(8,128)(2,1)S(1)} collective-permute-done((bf16[32,2048]{1,0:T(8,128)(2,1)S(1)}, bf16[32,2048]{1,0:T(8,128)(2,1)S(1)}, u32[]{:S(2)}, u32[]{:S(2)}) %collective-permute-start.11) | collective-permute-done | bytes 131104 | tf_op jit(solution)/shard_map/ppermute | solution.py:38
  33.7 0.1 shard_map.69.refs_0_
  33.8 0.1 collective-permute-start.12
  33.9 0.5 collective-permute-start.10
  34.5 0.1 collective-permute-start.7
  34.6 0.5 collective-permute-done.12.refs_1_
  35.1 1.6 %shard_map.70.refs_3_ = f32[32,2048]{1,0:T(8,128)S(1)} custom-call(bf16[32,1024]{1,0:T(8,128)(2,1)S(1)} %shard_map.69.refs_0_, bf16[32,1024]{1,0:T(8,128)(2,1)S(1)} %collective-permute-done.12.refs_1_, bf16[4096,2048]{1,0:T(8,128)(2,1)S(1)} %bitcast.1), custom_call_target="tpu_custom_call" | custom-call | flops 1724999936 | bytes 65536 | tf_op jit(solution)/shard_map/pallas_call | solution.py:26
  36.7 0.8 %shard_map.71.refs_2_ = f32[32,2048]{1,0:T(8,128)S(1)} custom-call(bf16[32,512]{1,0:T(8,128)(2,1)S(1)} %shard_map.68.refs_0_, bf16[32,512]{1,0:T(8,128)(2,1)S(1)} %collective-permute-done.10.refs_1_, bf16[4096,2048]{1,0:T(8,128)(2,1)S(1)} %bitcast.1, f32[32,2048]{1,0:T(8,128)S(1)} %shard_map.70.refs_3_), custom_call_target="tpu_custom_call" | custom-call | flops 862499968 | bytes 65536 | tf_op jit(solution)/shard_map/pallas_call | solution.py:26
  37.6 0.5 shard_map.72.acc_ref
  38.0 0.0 collective-permute-done.7.h_ref
  38.0 1.2 %shard_map.73 = (f32[16,1024]{1,0:T(8,128)S(1)}, bf16[16,1024]{1,0:T(8,128)(2,1)S(1)}) custom-call(bf16[32,512]{1,0:T(8,128)(2,1)S(1)} %collective-permute-done.7.h_ref, bf16[4096,2048]{1,0:T(8,128)(2,1)S(1)} %bitcast.1, f32[32,2048]{1,0:T(8,128)S(1)} %shard_map.72.acc_ref, bf16[2048,1024]{1,0:T(8,128)(2,1)S(1)} %get-tuple-element.31.basis_ref), custom_call_target="tpu_custom_call" | custom-call | flops 1150000000 | bytes 65536 | tf_op jit(solution)/shard_map/pallas_call | solution.py:26
  39.3 2.6 %collective-permute-start.13 = (bf16[16,1024]{1,0:T(8,128)(2,1)S(1)}, bf16[16,1024]{1,0:T(8,128)(2,1)S(1)}, u32[]{:S(2)}, u32[]{:S(2)}) collective-permute-start(bf16[16,1024]{1,0:T(8,128)(2,1)S(1)} %get-tuple-element.45), channel_id=1, source_target_pairs={{0,2},{1,3},{2,0},{3,1},{4,6},{5,7},{6,4},{7,5},{8,10},{9,11},{10,... | collective-permute-start | bytes 98312 | tf_op jit(solution)/shard_map/ppermute | solution.py:38
  41.9 2.2 %collective-permute-done.13.b_ref = bf16[16,1024]{1,0:T(8,128)(2,1)S(1)} collective-permute-done((bf16[16,1024]{1,0:T(8,128)(2,1)S(1)}, bf16[16,1024]{1,0:T(8,128)(2,1)S(1)}, u32[]{:S(2)}, u32[]{:S(2)}) %collective-permute-start.13) | collective-permute-done | bytes 32800 | tf_op jit(solution)/shard_map/ppermute | solution.py:38
  44.1 1.7 %collective-permute-start.14 = (bf16[8,1024]{1,0:T(8,128)(2,1)S(1)}, bf16[8,1024]{1,0:T(8,128)(2,1)S(1)}, u32[]{:S(2)}, u32[]{:S(2)}) collective-permute-start(bf16[8,1024]{1,0:T(8,128)(2,1)S(1)} %get-tuple-element.47), channel_id=1, source_target_pairs={{0,1},{1,0},{2,3},{3,2},{4,5},{5,4},{6,7},{7,6},{8,9},{9,8},{10,11... | collective-permute-start | bytes 49160 | tf_op jit(solution)/shard_map/ppermute | solution.py:38
  45.8 2.1 %collective-permute-done.14.b_ref = bf16[8,1024]{1,0:T(8,128)(2,1)S(1)} collective-permute-done((bf16[8,1024]{1,0:T(8,128)(2,1)S(1)}, bf16[8,1024]{1,0:T(8,128)(2,1)S(1)}, u32[]{:S(2)}, u32[]{:S(2)}) %collective-permute-start.14) | collective-permute-done | bytes 16416 | tf_op jit(solution)/shard_map/ppermute | solution.py:38
  47.9 1.5 %collective-permute-start.15 = (bf16[8,1024]{1,0:T(8,128)(2,1)S(1)}, bf16[8,1024]{1,0:T(8,128)(2,1)S(1)}, u32[]{:S(2)}, u32[]{:S(2)}) collective-permute-start(bf16[8,1024]{1,0:T(8,128)(2,1)S(1)} %get-tuple-element.49), channel_id=1, source_target_pairs={{0,8},{4,12},{8,0},{12,4},{1,9},{5,13},{9,1},{13,5},{2,10},{6,14},... | collective-permute-start | bytes 49160 | tf_op jit(solution)/shard_map/ppermute | solution.py:38
  49.4 2.3 %collective-permute-done.15.b_ref = bf16[8,1024]{1,0:T(8,128)(2,1)S(1)} collective-permute-done((bf16[8,1024]{1,0:T(8,128)(2,1)S(1)}, bf16[8,1024]{1,0:T(8,128)(2,1)S(1)}, u32[]{:S(2)}, u32[]{:S(2)}) %collective-permute-start.15) | collective-permute-done | bytes 16416 | tf_op jit(solution)/shard_map/ppermute | solution.py:38
  51.7 0.6 %shard_map.76 = (f32[8,1024]{1,0:T(8,128)S(1)}, bf16[8,1024]{1,0:T(8,128)(2,1)}) custom-call(f32[8,1024]{1,0:T(8,128)S(1)} %get-tuple-element.48.a_ref, bf16[8,1024]{1,0:T(8,128)(2,1)S(1)} %collective-permute-done.15.b_ref), custom_call_target="tpu_custom_call" | custom-call | flops 115000000 | bytes 65536 | tf_op jit(solution)/shard_map/pallas_call | solution.py:26
  52.3 1.2 %collective-permute-done.16.b_ref = f32[8,1024]{1,0:T(8,128)S(1)} collective-permute-done((f32[8,1024]{1,0:T(8,128)S(1)}, f32[8,1024]{1,0:T(8,128)S(1)}, u32[]{:S(2)}, u32[]{:S(2)}) %collective-permute-start.16) | collective-permute-done | bytes 32800 | tf_op jit(solution)/shard_map/ppermute | solution.py:38
  53.5 1.8 %shard_map.77 = bf16[8,2048]{1,0:T(8,128)(2,1)} custom-call(f32[8,1024]{1,0:T(8,128)S(1)} %get-tuple-element.50.a_ref, f32[8,1024]{1,0:T(8,128)S(1)} %collective-permute-done.16.b_ref, bf16[2048,1024]{1,0:T(8,128)(2,1)S(1)} %get-tuple-element.31.basis_ref), custom_call_target="tpu_custom_call" | custom-call | flops 1150000000 | bytes 65536 | tf_op jit(solution)/shard_map/pallas_call | solution.py:26
  (36 shorter events, 0.2 us)
Async XLA Ops:
  2.5 16.1 %slice-start.4 = ((s8[16777216]{0:T(1024)(128)(4,1)}), s8[4194304]{0:T(1024)(128)(4,1)S(1)}, s32[]{:S(2)}) async-start(s8[16777216]{0:T(1024)(128)(4,1)} %bitcast.2), calls=%async_computation.4 | async-start | bytes 8388608
  2.5 16.1 %slice-start.8 = ((s8[16777216]{0:T(1024)(128)(4,1)}), s8[4194304]{0:T(1024)(128)(4,1)S(1)}, s32[]{:S(2)}) async-start(s8[16777216]{0:T(1024)(128)(4,1)} %bitcast.4), calls=%async_computation.8 | async-start | bytes 8388608
  2.5 16.1 %slice-start.5 = ((s8[16777216]{0:T(1024)(128)(4,1)}), s8[4194304]{0:T(1024)(128)(4,1)S(1)}, s32[]{:S(2)}) async-start(s8[16777216]{0:T(1024)(128)(4,1)} %bitcast.2), calls=%async_computation.5 | async-start | bytes 8388608
  2.5 16.1 %slice-start.6 = ((s8[16777216]{0:T(1024)(128)(4,1)}), s8[4194304]{0:T(1024)(128)(4,1)S(1)}, s32[]{:S(2)}) async-start(s8[16777216]{0:T(1024)(128)(4,1)} %bitcast.2), calls=%async_computation.6 | async-start | bytes 8388608
  2.5 16.1 %slice-start.7 = ((s8[16777216]{0:T(1024)(128)(4,1)}), s8[4194304]{0:T(1024)(128)(4,1)S(1)}, s32[]{:S(2)}) async-start(s8[16777216]{0:T(1024)(128)(4,1)} %bitcast.2), calls=%async_computation.7 | async-start | bytes 8388608
  2.6 16.1 %slice-start.9 = ((s8[16777216]{0:T(1024)(128)(4,1)}), s8[4194304]{0:T(1024)(128)(4,1)S(1)}, s32[]{:S(2)}) async-start(s8[16777216]{0:T(1024)(128)(4,1)} %bitcast.4), calls=%async_computation.9 | async-start | bytes 8388608
  2.6 16.1 %slice-start.10 = ((s8[16777216]{0:T(1024)(128)(4,1)}), s8[4194304]{0:T(1024)(128)(4,1)S(1)}, s32[]{:S(2)}) async-start(s8[16777216]{0:T(1024)(128)(4,1)} %bitcast.4), calls=%async_computation.10 | async-start | bytes 8388608
  2.6 16.1 %slice-start.11 = ((s8[16777216]{0:T(1024)(128)(4,1)}), s8[4194304]{0:T(1024)(128)(4,1)S(1)}, s32[]{:S(2)}) async-start(s8[16777216]{0:T(1024)(128)(4,1)} %bitcast.4), calls=%async_computation.11 | async-start | bytes 8388608
  2.6 1.4 %collective-permute-start = (f32[8,1024]{1,0:T(8,128)S(1)}, f32[8,1024]{1,0:T(8,128)S(1)}, u32[]{:S(2)}, u32[]{:S(2)}) collective-permute-start(f32[8,1024]{1,0:T(8,128)S(1)} %get-tuple-element.28.a_ref), channel_id=1, source_target_pairs={{0,4},{4,0},{8,12},{12,8},{1,5},{5,1},{9,13},{13,9},{2,6},{6,2},{1... | collective-permute-start | bytes 98312 | tf_op jit(solution)/shard_map/ppermute | solution.py:38
  4.0 4.5 %collective-permute-start.1 = (bf16[8,1024]{1,0:T(8,128)(2,1)S(1)}, bf16[8,1024]{1,0:T(8,128)(2,1)S(1)}, u32[]{:S(2)}, u32[]{:S(2)}) collective-permute-start(bf16[8,1024]{1,0:T(8,128)(2,1)S(1)} %get-tuple-element.30), channel_id=1, source_target_pairs={{0,8},{4,12},{8,0},{12,4},{1,9},{5,13},{9,1},{13,5},{2,10},{6,14},... | collective-permute-start | bytes 49160 | tf_op jit(solution)/shard_map/ppermute | solution.py:38
  8.5 3.8 %collective-permute-start.2 = (bf16[8,1024]{1,0:T(8,128)(2,1)S(1)}, bf16[8,1024]{1,0:T(8,128)(2,1)S(1)}, u32[]{:S(2)}, u32[]{:S(2)}) collective-permute-start(bf16[8,1024]{1,0:T(8,128)(2,1)S(1)} %shard_map.57.a_ref), channel_id=1, source_target_pairs={{0,1},{1,0},{2,3},{3,2},{4,5},{5,4},{6,7},{7,6},{8,9},{9,8},{10,11... | collective-permute-start | bytes 49160 | tf_op jit(solution)/shard_map/ppermute | solution.py:38
  12.4 4.9 %collective-permute-start.3 = (bf16[16,1024]{1,0:T(8,128)(2,1)S(1)}, bf16[16,1024]{1,0:T(8,128)(2,1)S(1)}, u32[]{:S(2)}, u32[]{:S(2)}) collective-permute-start(bf16[16,1024]{1,0:T(8,128)(2,1)S(1)} %shard_map.58.a_ref), channel_id=1, source_target_pairs={{0,2},{1,3},{2,0},{3,1},{4,6},{5,7},{6,4},{7,5},{8,10},{9,11},{10,... | collective-permute-start | bytes 98312 | tf_op jit(solution)/shard_map/ppermute | solution.py:38
  21.7 2.1 %collective-permute-start.4 = (bf16[32,2048]{1,0:T(8,128)(2,1)S(1)}, bf16[32,2048]{1,0:T(8,128)(2,1)S(1)}, u32[]{:S(2)}, u32[]{:S(2)}) collective-permute-start(bf16[32,2048]{1,0:T(8,128)(2,1)S(1)} %get-tuple-element.34), channel_id=1, source_target_pairs={{0,4},{4,0},{8,12},{12,8},{1,5},{5,1},{9,13},{13,9},{2,6},{6,2},{1... | collective-permute-start | bytes 393224 | tf_op jit(solution)/shard_map/ppermute | solution.py:38
  23.3 2.2 %collective-permute-start.8 = (bf16[32,1024]{1,0:T(8,128)(2,1)S(1)}, bf16[32,1024]{1,0:T(8,128)(2,1)S(1)}, u32[]{:S(2)}, u32[]{:S(2)}) collective-permute-start(bf16[32,1024]{1,0:T(8,128)(2,1)S(1)} %get-tuple-element.40), channel_id=1, source_target_pairs={{0,4},{4,0},{8,12},{12,8},{1,5},{5,1},{9,13},{13,9},{2,6},{6,2},{1... | collective-permute-start | bytes 196616 | tf_op jit(solution)/shard_map/ppermute | solution.py:38
  25.5 2.2 %collective-permute-start.5 = (bf16[32,1024]{1,0:T(8,128)(2,1)S(1)}, bf16[32,1024]{1,0:T(8,128)(2,1)S(1)}, u32[]{:S(2)}, u32[]{:S(2)}) collective-permute-start(bf16[32,1024]{1,0:T(8,128)(2,1)S(1)} %get-tuple-element.37), channel_id=1, source_target_pairs={{0,4},{4,0},{8,12},{12,8},{1,5},{5,1},{9,13},{13,9},{2,6},{6,2},{1... | collective-permute-start | bytes 196616 | tf_op jit(solution)/shard_map/ppermute | solution.py:38
  25.5 9.6 %slice-start = ((s8[16777216]{0:T(1024)(128)(4,1)}), s8[4194304]{0:T(1024)(128)(4,1)S(1)}, s32[]{:S(2)}) async-start(s8[16777216]{0:T(1024)(128)(4,1)} %bitcast), calls=%async_computation | async-start | bytes 8388608
  25.5 9.6 %slice-start.1 = ((s8[16777216]{0:T(1024)(128)(4,1)}), s8[4194304]{0:T(1024)(128)(4,1)S(1)}, s32[]{:S(2)}) async-start(s8[16777216]{0:T(1024)(128)(4,1)} %bitcast), calls=%async_computation.1 | async-start | bytes 8388608
  25.5 8.3 %collective-permute-start.9 = (bf16[32,1024]{1,0:T(8,128)(2,1)S(1)}, bf16[32,1024]{1,0:T(8,128)(2,1)S(1)}, u32[]{:S(2)}, u32[]{:S(2)}) collective-permute-start(bf16[32,1024]{1,0:T(8,128)(2,1)S(1)} %get-tuple-element.42), channel_id=1, source_target_pairs={{0,8},{4,12},{8,0},{12,4},{1,9},{5,13},{9,1},{13,5},{2,10},{6,14},... | collective-permute-start | bytes 196616 | tf_op jit(solution)/shard_map/ppermute | solution.py:38
  27.4 6.3 %collective-permute-start.11 = (bf16[32,2048]{1,0:T(8,128)(2,1)S(1)}, bf16[32,2048]{1,0:T(8,128)(2,1)S(1)}, u32[]{:S(2)}, u32[]{:S(2)}) collective-permute-start(bf16[32,2048]{1,0:T(8,128)(2,1)S(1)} %get-tuple-element.35.refs_1_), channel_id=1, source_target_pairs={{0,8},{4,12},{8,0},{12,4},{1,9},{5,13},{9,1},{13,5},{2,10},{6,14},... | collective-permute-start | bytes 393224 | tf_op jit(solution)/shard_map/ppermute | solution.py:38
  27.6 7.5 %slice-start.2 = ((s8[16777216]{0:T(1024)(128)(4,1)}), s8[4194304]{0:T(1024)(128)(4,1)S(1)}, s32[]{:S(2)}) async-start(s8[16777216]{0:T(1024)(128)(4,1)} %bitcast), calls=%async_computation.2 | async-start | bytes 8388608
  27.6 7.5 %slice-start.3 = ((s8[16777216]{0:T(1024)(128)(4,1)}), s8[4194304]{0:T(1024)(128)(4,1)S(1)}, s32[]{:S(2)}) async-start(s8[16777216]{0:T(1024)(128)(4,1)} %bitcast), calls=%async_computation.3 | async-start | bytes 8388608
  27.7 6.8 %collective-permute-start.6 = (bf16[32,1024]{1,0:T(8,128)(2,1)S(1)}, bf16[32,1024]{1,0:T(8,128)(2,1)S(1)}, u32[]{:S(2)}, u32[]{:S(2)}) collective-permute-start(bf16[32,1024]{1,0:T(8,128)(2,1)S(1)} %get-tuple-element.39), channel_id=1, source_target_pairs={{0,8},{4,12},{8,0},{12,4},{1,9},{5,13},{9,1},{13,5},{2,10},{6,14},... | collective-permute-start | bytes 196616 | tf_op jit(solution)/shard_map/ppermute | solution.py:38
  33.8 1.3 %collective-permute-start.12 = (bf16[32,1024]{1,0:T(8,128)(2,1)S(1)}, bf16[32,1024]{1,0:T(8,128)(2,1)S(1)}, u32[]{:S(2)}, u32[]{:S(2)}) collective-permute-start(bf16[32,1024]{1,0:T(8,128)(2,1)S(1)} %shard_map.69.refs_0_), channel_id=1, source_target_pairs={{0,4},{4,0},{8,12},{12,8},{1,5},{5,1},{9,13},{13,9},{2,6},{6,2},{1... | collective-permute-start | bytes 196616 | tf_op jit(solution)/shard_map/ppermute | solution.py:38
  33.9 2.8 %collective-permute-start.10 = (bf16[32,512]{1,0:T(8,128)(2,1)S(1)}, bf16[32,512]{1,0:T(8,128)(2,1)S(1)}, u32[]{:S(2)}, u32[]{:S(2)}) collective-permute-start(bf16[32,512]{1,0:T(8,128)(2,1)S(1)} %shard_map.68.refs_0_), channel_id=1, source_target_pairs={{0,4},{4,0},{8,12},{12,8},{1,5},{5,1},{9,13},{13,9},{2,6},{6,2},{1... | collective-permute-start | bytes 98312 | tf_op jit(solution)/shard_map/ppermute | solution.py:38
  34.5 3.5 %collective-permute-start.7 = (bf16[32,512]{1,0:T(8,128)(2,1)S(1)}, bf16[32,512]{1,0:T(8,128)(2,1)S(1)}, u32[]{:S(2)}, u32[]{:S(2)}) collective-permute-start(bf16[32,512]{1,0:T(8,128)(2,1)S(1)} %shard_map.66.refs_0_), channel_id=1, source_target_pairs={{0,4},{4,0},{8,12},{12,8},{1,5},{5,1},{9,13},{13,9},{2,6},{6,2},{1... | collective-permute-start | bytes 98312 | tf_op jit(solution)/shard_map/ppermute | solution.py:38
  39.3 4.8 %collective-permute-start.13 = (bf16[16,1024]{1,0:T(8,128)(2,1)S(1)}, bf16[16,1024]{1,0:T(8,128)(2,1)S(1)}, u32[]{:S(2)}, u32[]{:S(2)}) collective-permute-start(bf16[16,1024]{1,0:T(8,128)(2,1)S(1)} %get-tuple-element.45), channel_id=1, source_target_pairs={{0,2},{1,3},{2,0},{3,1},{4,6},{5,7},{6,4},{7,5},{8,10},{9,11},{10,... | collective-permute-start | bytes 98312 | tf_op jit(solution)/shard_map/ppermute | solution.py:38
  44.1 3.8 %collective-permute-start.14 = (bf16[8,1024]{1,0:T(8,128)(2,1)S(1)}, bf16[8,1024]{1,0:T(8,128)(2,1)S(1)}, u32[]{:S(2)}, u32[]{:S(2)}) collective-permute-start(bf16[8,1024]{1,0:T(8,128)(2,1)S(1)} %get-tuple-element.47), channel_id=1, source_target_pairs={{0,1},{1,0},{2,3},{3,2},{4,5},{5,4},{6,7},{7,6},{8,9},{9,8},{10,11... | collective-permute-start | bytes 49160 | tf_op jit(solution)/shard_map/ppermute | solution.py:38
  47.9 3.8 %collective-permute-start.15 = (bf16[8,1024]{1,0:T(8,128)(2,1)S(1)}, bf16[8,1024]{1,0:T(8,128)(2,1)S(1)}, u32[]{:S(2)}, u32[]{:S(2)}) collective-permute-start(bf16[8,1024]{1,0:T(8,128)(2,1)S(1)} %get-tuple-element.49), channel_id=1, source_target_pairs={{0,8},{4,12},{8,0},{12,4},{1,9},{5,13},{9,1},{13,5},{2,10},{6,14},... | collective-permute-start | bytes 49160 | tf_op jit(solution)/shard_map/ppermute | solution.py:38
  52.3 1.2 %collective-permute-start.16 = (f32[8,1024]{1,0:T(8,128)S(1)}, f32[8,1024]{1,0:T(8,128)S(1)}, u32[]{:S(2)}, u32[]{:S(2)}) collective-permute-start(f32[8,1024]{1,0:T(8,128)S(1)} %get-tuple-element.50.a_ref), channel_id=1, source_target_pairs={{0,4},{4,0},{8,12},{12,8},{1,5},{5,1},{9,13},{13,9},{2,6},{6,2},{1... | collective-permute-start | bytes 98312 | tf_op jit(solution)/shard_map/ppermute | solution.py:38

commit v3 on v2

--- a/solution.py
+++ b/solution.py
@@ -14,8 +14,10 @@
 LIMIT = 2 * 1024 * 1024
 PIECES = 4
 WAIT = 30
-SUM = 6
-PAIR = 1
+SUMS = (0.3, 0.3, 0.3)
+PAIR = 6
+HIDDEN = (5, 0.1, 0.1)
+DOWN = 3
 VMEM = pl.BlockSpec(memory_space=pltpu.VMEM)
 HBM = pl.BlockSpec(memory_space=pltpu.HBM)
 sds = jax.ShapeDtypeStruct
@@ -73,10 +75,13 @@
         out_ref[...] = part if p == 0 else out_ref[...] + part
 
 
-def add_body(a_ref, b_ref, *out_refs):
+def add_body(a_ref, b_ref, *refs, outs=1):
     total = a_ref[...] + b_ref[...].astype(F32)
-    for out_ref in out_refs:
+    for out_ref in refs[-outs:]:
         out_ref[...] = total.astype(out_ref.dtype)
+
+
+add_two_body = functools.partial(add_body, outs=2)
 
 
 def half_body(a_ref, b_ref, keep_ref, send_ref):
@@ -91,7 +96,8 @@
     out_ref[rows:] = b_ref[...]
 
 
-def hidden_body(a_ref, b_ref, out_ref):
+def hidden_body(a_ref, b_ref, *refs):
+    out_ref = refs[-1]
     half = out_ref.shape[1]
     gate = a_ref[:, :half] + b_ref[:, :half].astype(F32)
     up = a_ref[:, half:] + b_ref[:, half:].astype(F32)
@@ -169,10 +175,10 @@
         scratch=[pltpu.VMEM(tokens.shape, BF16), pltpu.SemaphoreType.DMA((PIECES + 1,))],
         fixed=(0, 1),
     )
-    codes, send = call(add_body, both(codes.shape), WAIT, codes, swap(codes, "dp", 1, dp))
+    codes, send = call(add_two_body, both(codes.shape), WAIT, codes, swap(codes, "dp", 1, dp))
     mask = 2
     while 2 * mask < dp:
-        codes, send = call(add_body, both(codes.shape), 0.1, codes, swap(send, "dp", mask, dp))
+        codes, send = call(add_two_body, both(codes.shape), 0.1, codes, swap(send, "dp", mask, dp))
         mask *= 2
     codes = call(add_body, sds(codes.shape, BF16), 0.1, codes, swap(send, "dp", mask, dp))
     mask = 1
@@ -188,8 +194,7 @@
     for share in shares:
         spans.append((at, ff * share // sum(shares)))
         at += spans[-1][1]
-    sums = []
-    after = []
+    pairs, kept, sums = [], [], []
     for q, (start, span) in enumerate(spans):
         keep, send = call(
             functools.partial(pair_body, start=start),
@@ -198,24 +203,26 @@
             restored,
             gate_weight,
             up_weight,
-            *after,
+            *kept[-1:],
+            *[send for _, send in sums[-1:]],
         )
-        sums.append((keep, swap(send, "dp", 1, dp)))
-        after = [keep]
+        kept.append(keep)
+        pairs.append((keep, swap(send, "dp", 1, dp)))
         if q > 0:
-            sums[q - 1] = call(add_body, both((rows, spans[q - 1][1])), SUM, *sums[q - 1])
-            after.append(sums[q - 1][1])
-    sums[-1] = call(add_body, both((rows, spans[-1][1])), SUM, *sums[-1])
+            sums.append(call(add_two_body, both((rows, spans[q - 1][1])), SUMS[q - 1], *pairs[q - 1], keep))
+    sums.append(call(add_two_body, both((rows, spans[-1][1])), SUMS[-1], *pairs[-1], sums[-1][1]))
     acc = None
-    for (start, span), (total, send) in zip(spans, sums):
+    own = None
+    for q, ((start, span), (total, send)) in enumerate(zip(spans, sums)):
         mask = 2
         while 2 * mask < dp:
-            total, send = call(add_body, both(total.shape), 0.1, total, swap(send, "dp", mask, dp))
+            total, send = call(add_two_body, both(total.shape), 0.1, total, swap(send, "dp", mask, dp))
             mask *= 2
         half = span // 2
-        own = call(hidden_body, sds((rows, half), BF16), 0.1, total, swap(send, "dp", mask, dp))
+        order = [sums[-1][1]] if q == 0 else [acc] if q == 1 else [own]
+        own = call(hidden_body, sds((rows, half), BF16), HIDDEN[q], total, swap(send, "dp", mask, dp), *order)
         away = swap(own, "dp", 1, dp)
-        time = 3 * span / ff
+        time = DOWN * span / ff
         shape = sds((rows, width), F32)
         if start + span < ff:
             body = functools.partial(down_body, start=start, half=half, own=1, away=1, first=acc is None)
@@ -241,11 +248,12 @@
             half_body, [sds((top, R), F32), sds((top, R), BF16)], 0.1, codes, swap(send, "tensor", mask, tensor)
         )
         mask //= 2
-    codes, send = call(add_body, both(codes.shape), 0.1, codes, swap(send, "tensor", 1, tensor))
+    codes, send = call(add_two_body, both(codes.shape), 0.1, codes, swap(send, "tensor", 1, tensor))
     mask = dp // 2
-    while mask > 1:
-        codes, send = call(add_body, both(codes.shape), 0.1, codes, swap(send, "dp", mask, dp))
+    while mask > 2:
+        codes, send = call(add_two_body, both(codes.shape), 0.1, codes, swap(send, "dp", mask, dp))
         mask //= 2
+    codes = call(add_body, sds(codes.shape, F32), 0.1, codes, swap(send, "dp", 2, dp))
     return call(final_body, sds((local, width), BF16), 1, codes, swap(codes, "dp", 1, dp), basis)
 
 

time: 55.5 us -> 54 us (0.973)
  waiting for transfers between devices: 18.7 us -> 17.6 us
  Pallas kernels: 16.7 us -> 16.1 us
    ppermute x17, waiting for transfers between devices: 18.7 us -> 17.6 us  [swap(): return lax.ppermute(value, axis, [(i, i ^ mask) for i in range(size)])]
    pallas_call x23, Pallas kernels: 16.7 us -> 16.1 us  [call(): pl.pallas_call(body, out_shape=out, in_specs=[HBM if i in fixed else VMEM...]
  transfers between devices with their start and end apart: 17 -> 17, of which waited for: 10 -> 12; matrix products, arithmetic and copies ran while one was open for 0% -> 0% of each run, Pallas kernels for 11% -> 11%
where the time goes in v3:
time: 54 us; the launch traced here: 53.8 us
  starting transfers between devices  19.6 us (36%)
  waiting for transfers between devices  17.6 us (33%)
  Pallas kernels  16.1 us (30%)
    ppermute x17, starting transfers between devices, swap(): return lax.ppermute(value, axis, [(i, i ^ mask) for i in range(size)])  19.6 us
    ppermute x17, waiting for transfers between devices, swap(): return lax.ppermute(value, axis, [(i, i ^ mask) for i in range(size)])  17.6 us
    pallas_call x23, Pallas kernels, call(): pl.pallas_call(body, out_shape=out, in_specs=[HBM if i in fixed else VMEM...  16.1 us
  transfers between devices with their start and end apart: 17, of which 12 were waited for; matrix products, arithmetic and copies ran while one was open for 0% of the time, Pallas kernels for 11%

profile of v3, /device:TPU:0, one launch (start us, length us, event | category | flops | bytes accessed | tf_op | source)
XLA Modules:
  0.0 53.8 jit_solution(17123724764745395573)
XLA Ops:
  0.0 2.5 %shard_map.55 = (f32[8,1024]{1,0:T(8,128)S(1)}, bf16[2048,1024]{1,0:T(8,128)(2,1)S(1)}) custom-call(bf16[8,2048]{1,0:T(8,128)(2,1)} %x_ref.1, bf16[2048,1024]{1,0:T(8,128)(2,1)} %basis_ref.1), custom_call_target="tpu_custom_call" | custom-call | flops 1150000000 | bytes 65536 | tf_op jit(solution)/shard_map/pallas_call | solution.py:28
  2.5 0.0 slice-start.4
  2.5 0.0 slice-start.8
  2.5 0.0 slice-start.6
  2.5 0.0 slice-start.7
  2.6 0.0 slice-start.10
  2.6 0.0 slice-start.11
  2.6 0.5 collective-permute-start
  3.1 0.9 %collective-permute-done.b_ref = f32[8,1024]{1,0:T(8,128)S(1)} collective-permute-done((f32[8,1024]{1,0:T(8,128)S(1)}, f32[8,1024]{1,0:T(8,128)S(1)}, u32[]{:S(2)}, u32[]{:S(2)}) %collective-permute-start) | collective-permute-done | bytes 32800 | tf_op jit(solution)/shard_map/ppermute | solution.py:40
  4.0 2.8 %collective-permute-start.1 = (bf16[8,1024]{1,0:T(8,128)(2,1)S(1)}, bf16[8,1024]{1,0:T(8,128)(2,1)S(1)}, u32[]{:S(2)}, u32[]{:S(2)}) collective-permute-start(bf16[8,1024]{1,0:T(8,128)(2,1)S(1)} %get-tuple-element.29), channel_id=1, source_target_pairs={{0,8},{4,12},{8,0},{12,4},{1,9},{5,13},{9,1},{13,5},{2,10},{6,14},... | collective-permute-start | bytes 49160 | tf_op jit(solution)/shard_map/ppermute | solution.py:40
  6.8 1.7 %collective-permute-done.1.b_ref = bf16[8,1024]{1,0:T(8,128)(2,1)S(1)} collective-permute-done((bf16[8,1024]{1,0:T(8,128)(2,1)S(1)}, bf16[8,1024]{1,0:T(8,128)(2,1)S(1)}, u32[]{:S(2)}, u32[]{:S(2)}) %collective-permute-start.1) | collective-permute-done | bytes 16416 | tf_op jit(solution)/shard_map/ppermute | solution.py:40
  8.5 2.1 %collective-permute-start.2 = (bf16[8,1024]{1,0:T(8,128)(2,1)S(1)}, bf16[8,1024]{1,0:T(8,128)(2,1)S(1)}, u32[]{:S(2)}, u32[]{:S(2)}) collective-permute-start(bf16[8,1024]{1,0:T(8,128)(2,1)S(1)} %shard_map.57.a_ref), channel_id=1, source_target_pairs={{0,1},{1,0},{2,3},{3,2},{4,5},{5,4},{6,7},{7,6},{8,9},{9,8},{10,11... | collective-permute-start | bytes 49160 | tf_op jit(solution)/shard_map/ppermute | solution.py:40
  10.6 1.7 %collective-permute-done.2.b_ref = bf16[8,1024]{1,0:T(8,128)(2,1)S(1)} collective-permute-done((bf16[8,1024]{1,0:T(8,128)(2,1)S(1)}, bf16[8,1024]{1,0:T(8,128)(2,1)S(1)}, u32[]{:S(2)}, u32[]{:S(2)}) %collective-permute-start.2) | collective-permute-done | bytes 16416 | tf_op jit(solution)/shard_map/ppermute | solution.py:40
  12.4 3.0 %collective-permute-start.3 = (bf16[16,1024]{1,0:T(8,128)(2,1)S(1)}, bf16[16,1024]{1,0:T(8,128)(2,1)S(1)}, u32[]{:S(2)}, u32[]{:S(2)}) collective-permute-start(bf16[16,1024]{1,0:T(8,128)(2,1)S(1)} %shard_map.58.a_ref), channel_id=1, source_target_pairs={{0,2},{1,3},{2,0},{3,1},{4,6},{5,7},{6,4},{7,5},{8,10},{9,11},{10,... | collective-permute-start | bytes 98312 | tf_op jit(solution)/shard_map/ppermute | solution.py:40
  15.4 1.9 %collective-permute-done.3.b_ref = bf16[16,1024]{1,0:T(8,128)(2,1)S(1)} collective-permute-done((bf16[16,1024]{1,0:T(8,128)(2,1)S(1)}, bf16[16,1024]{1,0:T(8,128)(2,1)S(1)}, u32[]{:S(2)}, u32[]{:S(2)}) %collective-permute-start.3) | collective-permute-done | bytes 32800 | tf_op jit(solution)/shard_map/ppermute | solution.py:40
  17.3 1.3 %shard_map.60.x_ref = bf16[32,2048]{1,0:T(8,128)(2,1)S(1)} custom-call(bf16[32,1024]{1,0:T(8,128)(2,1)S(1)} %shard_map.59.codes_ref, bf16[2048,1024]{1,0:T(8,128)(2,1)S(1)} %get-tuple-element.30.basis_ref), custom_call_target="tpu_custom_call" | custom-call | flops 575000000 | bytes 65536 | tf_op jit(solution)/shard_map/pallas_call | solution.py:28
  18.6 0.0 slice-done.4
  18.7 3.0 %shard_map.61 = (f32[32,2048]{1,0:T(8,128)S(1)}, bf16[32,2048]{1,0:T(8,128)(2,1)S(1)}) custom-call(bf16[32,2048]{1,0:T(8,128)(2,1)S(1)} %shard_map.60.x_ref, bf16[2048,4096]{1,0:T(8,128)(2,1)S(1)} %bitcast.3, bf16[2048,4096]{1,0:T(8,128)(2,1)S(1)} %bitcast.5), custom_call_target="tpu_custom_call" | custom-call | flops 3449999872 | bytes 65536 | tf_op jit(solution)/shard_map/pallas_call | solution.py:28
  21.7 1.6 %shard_map.62 = (f32[32,1024]{1,0:T(8,128)S(1)}, bf16[32,1024]{1,0:T(8,128)(2,1)S(1)}) custom-call(bf16[32,2048]{1,0:T(8,128)(2,1)S(1)} %shard_map.60.x_ref, bf16[2048,4096]{1,0:T(8,128)(2,1)S(1)} %bitcast.3, bf16[2048,4096]{1,0:T(8,128)(2,1)S(1)} %bitcast.5, f32[32,2048]{1,0:T(8,128)S(1)} %get-tuple-element.31.refs_0_.a_ref), custom_call_target="tpu_custom_call" | custom-call | flops 1724999936 | bytes 65536 | tf_op jit(solution)/shard_map/pallas_call | solution.py:28
  23.3 0.5 collective-permute-start.6
  23.9 1.9 %collective-permute-start.9 = (bf16[32,2048]{1,0:T(8,128)(2,1)S(1)}, bf16[32,2048]{1,0:T(8,128)(2,1)S(1)}, u32[]{:S(2)}, u32[]{:S(2)}) collective-permute-start(bf16[32,2048]{1,0:T(8,128)(2,1)S(1)} %get-tuple-element.34.refs_1_), channel_id=1, source_target_pairs={{0,8},{4,12},{8,0},{12,4},{1,9},{5,13},{9,1},{13,5},{2,10},{6,14},... | collective-permute-start | bytes 393224 | tf_op jit(solution)/shard_map/ppermute | solution.py:40
  25.8 1.6 %shard_map.64 = (f32[32,1024]{1,0:T(8,128)S(1)}, bf16[32,1024]{1,0:T(8,128)(2,1)S(1)}) custom-call(bf16[32,2048]{1,0:T(8,128)(2,1)S(1)} %shard_map.60.x_ref, bf16[2048,4096]{1,0:T(8,128)(2,1)S(1)} %bitcast.3, bf16[2048,4096]{1,0:T(8,128)(2,1)S(1)} %bitcast.5, f32[32,1024]{1,0:T(8,128)S(1)} %get-tuple-element.32.refs_0_.a_ref, ...), custom_call_target="tpu_custom_call" | custom-call | flops 1724999936 | bytes 65536 | tf_op jit(solution)/shard_map/pallas_call | solution.py:28
  27.4 0.0 collective-permute-start.5
  27.4 0.0 collective-permute-done.6.b_ref
  27.4 1.2 %collective-permute-done.5.b_ref = bf16[32,1024]{1,0:T(8,128)(2,1)S(1)} collective-permute-done((bf16[32,1024]{1,0:T(8,128)(2,1)S(1)}, bf16[32,1024]{1,0:T(8,128)(2,1)S(1)}, u32[]{:S(2)}, u32[]{:S(2)}) %collective-permute-start.5) | collective-permute-done | bytes 65568 | tf_op jit(solution)/shard_map/ppermute | solution.py:40
  28.6 0.8 %collective-permute-done.9.b_ref = bf16[32,2048]{1,0:T(8,128)(2,1)S(1)} collective-permute-done((bf16[32,2048]{1,0:T(8,128)(2,1)S(1)}, bf16[32,2048]{1,0:T(8,128)(2,1)S(1)}, u32[]{:S(2)}, u32[]{:S(2)}) %collective-permute-start.9) | collective-permute-done | bytes 131104 | tf_op jit(solution)/shard_map/ppermute | solution.py:40
  29.5 0.1 shard_map.67.refs_0_
  29.5 0.1 collective-permute-start.10
  29.6 1.8 %collective-permute-start.8 = (bf16[32,1024]{1,0:T(8,128)(2,1)S(1)}, bf16[32,1024]{1,0:T(8,128)(2,1)S(1)}, u32[]{:S(2)}, u32[]{:S(2)}) collective-permute-start(bf16[32,1024]{1,0:T(8,128)(2,1)S(1)} %get-tuple-element.38.refs_0_), channel_id=1, source_target_pairs={{0,8},{4,12},{8,0},{12,4},{1,9},{5,13},{9,1},{13,5},{2,10},{6,14},... | collective-permute-start | bytes 196616 | tf_op jit(solution)/shard_map/ppermute | solution.py:40
  31.4 0.3 collective-permute-start.7
  31.7 0.2 slice-done.3
  31.9 1.6 %shard_map.68.refs_0_.refs_3_ = f32[32,2048]{1,0:T(8,128)S(1)} custom-call(bf16[32,1024]{1,0:T(8,128)(2,1)S(1)} %shard_map.67.refs_0_, bf16[32,1024]{1,0:T(8,128)(2,1)S(1)} %collective-permute-done.10.refs_1_, bf16[4096,2048]{1,0:T(8,128)(2,1)S(1)} %bitcast.1), custom_call_target="tpu_custom_call" | custom-call | flops 1724999936 | bytes 65536 | tf_op jit(solution)/shard_map/pallas_call | solution.py:28
  33.4 0.7 %collective-permute-done.8.b_ref = bf16[32,1024]{1,0:T(8,128)(2,1)S(1)} collective-permute-done((bf16[32,1024]{1,0:T(8,128)(2,1)S(1)}, bf16[32,1024]{1,0:T(8,128)(2,1)S(1)}, u32[]{:S(2)}, u32[]{:S(2)}) %collective-permute-start.8) | collective-permute-done | bytes 65568 | tf_op jit(solution)/shard_map/ppermute | solution.py:40
  34.1 0.1 collective-permute-start.12
  34.2 1.4 %collective-permute-done.7.b_ref = bf16[32,1024]{1,0:T(8,128)(2,1)S(1)} collective-permute-done((bf16[32,1024]{1,0:T(8,128)(2,1)S(1)}, bf16[32,1024]{1,0:T(8,128)(2,1)S(1)}, u32[]{:S(2)}, u32[]{:S(2)}) %collective-permute-start.7) | collective-permute-done | bytes 65568 | tf_op jit(solution)/shard_map/ppermute | solution.py:40
  35.7 0.1 collective-permute-start.11
  35.8 0.8 %shard_map.71.refs_2_ = f32[32,2048]{1,0:T(8,128)S(1)} custom-call(bf16[32,512]{1,0:T(8,128)(2,1)S(1)} %shard_map.69.refs_0_, bf16[32,512]{1,0:T(8,128)(2,1)S(1)} %collective-permute-done.12.refs_1_, bf16[4096,2048]{1,0:T(8,128)(2,1)S(1)} %bitcast.1, f32[32,2048]{1,0:T(8,128)S(1)} %shard_map.68.refs_0_.refs_3_), custom_call_target="tpu_custom_call" | custom-call | flops 862499968 | bytes 65536 | tf_op jit(solution)/shard_map/pallas_call | solution.py:28
  36.6 0.5 shard_map.72.acc_ref
  37.1 0.0 collective-permute-done.11.h_ref
  37.1 1.2 %shard_map.73 = (f32[16,1024]{1,0:T(8,128)S(1)}, bf16[16,1024]{1,0:T(8,128)(2,1)S(1)}) custom-call(bf16[32,512]{1,0:T(8,128)(2,1)S(1)} %collective-permute-done.11.h_ref, bf16[4096,2048]{1,0:T(8,128)(2,1)S(1)} %bitcast.1, f32[32,2048]{1,0:T(8,128)S(1)} %shard_map.72.acc_ref, bf16[2048,1024]{1,0:T(8,128)(2,1)S(1)} %get-tuple-element.30.basis_ref), custom_call_target="tpu_custom_call" | custom-call | flops 1150000000 | bytes 65536 | tf_op jit(solution)/shard_map/pallas_call | solution.py:28
  38.3 2.7 %collective-permute-start.13 = (bf16[16,1024]{1,0:T(8,128)(2,1)S(1)}, bf16[16,1024]{1,0:T(8,128)(2,1)S(1)}, u32[]{:S(2)}, u32[]{:S(2)}) collective-permute-start(bf16[16,1024]{1,0:T(8,128)(2,1)S(1)} %get-tuple-element.44), channel_id=1, source_target_pairs={{0,2},{1,3},{2,0},{3,1},{4,6},{5,7},{6,4},{7,5},{8,10},{9,11},{10,... | collective-permute-start | bytes 98312 | tf_op jit(solution)/shard_map/ppermute | solution.py:40
  41.0 2.1 %collective-permute-done.13.b_ref = bf16[16,1024]{1,0:T(8,128)(2,1)S(1)} collective-permute-done((bf16[16,1024]{1,0:T(8,128)(2,1)S(1)}, bf16[16,1024]{1,0:T(8,128)(2,1)S(1)}, u32[]{:S(2)}, u32[]{:S(2)}) %collective-permute-start.13) | collective-permute-done | bytes 32800 | tf_op jit(solution)/shard_map/ppermute | solution.py:40
  43.2 1.8 %collective-permute-start.14 = (bf16[8,1024]{1,0:T(8,128)(2,1)S(1)}, bf16[8,1024]{1,0:T(8,128)(2,1)S(1)}, u32[]{:S(2)}, u32[]{:S(2)}) collective-permute-start(bf16[8,1024]{1,0:T(8,128)(2,1)S(1)} %get-tuple-element.46), channel_id=1, source_target_pairs={{0,1},{1,0},{2,3},{3,2},{4,5},{5,4},{6,7},{7,6},{8,9},{9,8},{10,11... | collective-permute-start | bytes 49160 | tf_op jit(solution)/shard_map/ppermute | solution.py:40
  44.9 2.0 %collective-permute-done.14.b_ref = bf16[8,1024]{1,0:T(8,128)(2,1)S(1)} collective-permute-done((bf16[8,1024]{1,0:T(8,128)(2,1)S(1)}, bf16[8,1024]{1,0:T(8,128)(2,1)S(1)}, u32[]{:S(2)}, u32[]{:S(2)}) %collective-permute-start.14) | collective-permute-done | bytes 16416 | tf_op jit(solution)/shard_map/ppermute | solution.py:40
  47.0 1.9 %collective-permute-start.15 = (bf16[8,1024]{1,0:T(8,128)(2,1)S(1)}, bf16[8,1024]{1,0:T(8,128)(2,1)S(1)}, u32[]{:S(2)}, u32[]{:S(2)}) collective-permute-start(bf16[8,1024]{1,0:T(8,128)(2,1)S(1)} %get-tuple-element.48), channel_id=1, source_target_pairs={{0,8},{4,12},{8,0},{12,4},{1,9},{5,13},{9,1},{13,5},{2,10},{6,14},... | collective-permute-start | bytes 49160 | tf_op jit(solution)/shard_map/ppermute | solution.py:40
  48.8 1.9 %collective-permute-done.15.b_ref = bf16[8,1024]{1,0:T(8,128)(2,1)S(1)} collective-permute-done((bf16[8,1024]{1,0:T(8,128)(2,1)S(1)}, bf16[8,1024]{1,0:T(8,128)(2,1)S(1)}, u32[]{:S(2)}, u32[]{:S(2)}) %collective-permute-start.15) | collective-permute-done | bytes 16416 | tf_op jit(solution)/shard_map/ppermute | solution.py:40
  50.8 1.2 %collective-permute-done.16.b_ref = f32[8,1024]{1,0:T(8,128)S(1)} collective-permute-done((f32[8,1024]{1,0:T(8,128)S(1)}, f32[8,1024]{1,0:T(8,128)S(1)}, u32[]{:S(2)}, u32[]{:S(2)}) %collective-permute-start.16) | collective-permute-done | bytes 32800 | tf_op jit(solution)/shard_map/ppermute | solution.py:40
  52.0 1.8 %shard_map.77 = bf16[8,2048]{1,0:T(8,128)(2,1)} custom-call(f32[8,1024]{1,0:T(8,128)S(1)} %shard_map.76.a_ref, f32[8,1024]{1,0:T(8,128)S(1)} %collective-permute-done.16.b_ref, bf16[2048,1024]{1,0:T(8,128)(2,1)S(1)} %get-tuple-element.30.basis_ref), custom_call_target="tpu_custom_call" | custom-call | flops 1150000000 | bytes 65536 | tf_op jit(solution)/shard_map/pallas_call | solution.py:28
  (36 shorter events, 0.2 us)
Async XLA Ops:
  2.5 16.1 %slice-start.4 = ((s8[16777216]{0:T(1024)(128)(4,1)}), s8[4194304]{0:T(1024)(128)(4,1)S(1)}, s32[]{:S(2)}) async-start(s8[16777216]{0:T(1024)(128)(4,1)} %bitcast.2), calls=%async_computation.4 | async-start | bytes 8388608
  2.5 16.1 %slice-start.8 = ((s8[16777216]{0:T(1024)(128)(4,1)}), s8[4194304]{0:T(1024)(128)(4,1)S(1)}, s32[]{:S(2)}) async-start(s8[16777216]{0:T(1024)(128)(4,1)} %bitcast.4), calls=%async_computation.8 | async-start | bytes 8388608
  2.5 16.1 %slice-start.5 = ((s8[16777216]{0:T(1024)(128)(4,1)}), s8[4194304]{0:T(1024)(128)(4,1)S(1)}, s32[]{:S(2)}) async-start(s8[16777216]{0:T(1024)(128)(4,1)} %bitcast.2), calls=%async_computation.5 | async-start | bytes 8388608
  2.5 16.1 %slice-start.6 = ((s8[16777216]{0:T(1024)(128)(4,1)}), s8[4194304]{0:T(1024)(128)(4,1)S(1)}, s32[]{:S(2)}) async-start(s8[16777216]{0:T(1024)(128)(4,1)} %bitcast.2), calls=%async_computation.6 | async-start | bytes 8388608
  2.5 16.1 %slice-start.7 = ((s8[16777216]{0:T(1024)(128)(4,1)}), s8[4194304]{0:T(1024)(128)(4,1)S(1)}, s32[]{:S(2)}) async-start(s8[16777216]{0:T(1024)(128)(4,1)} %bitcast.2), calls=%async_computation.7 | async-start | bytes 8388608
  2.6 16.1 %slice-start.9 = ((s8[16777216]{0:T(1024)(128)(4,1)}), s8[4194304]{0:T(1024)(128)(4,1)S(1)}, s32[]{:S(2)}) async-start(s8[16777216]{0:T(1024)(128)(4,1)} %bitcast.4), calls=%async_computation.9 | async-start | bytes 8388608
  2.6 16.1 %slice-start.10 = ((s8[16777216]{0:T(1024)(128)(4,1)}), s8[4194304]{0:T(1024)(128)(4,1)S(1)}, s32[]{:S(2)}) async-start(s8[16777216]{0:T(1024)(128)(4,1)} %bitcast.4), calls=%async_computation.10 | async-start | bytes 8388608
  2.6 16.1 %slice-start.11 = ((s8[16777216]{0:T(1024)(128)(4,1)}), s8[4194304]{0:T(1024)(128)(4,1)S(1)}, s32[]{:S(2)}) async-start(s8[16777216]{0:T(1024)(128)(4,1)} %bitcast.4), calls=%async_computation.11 | async-start | bytes 8388608
  2.6 1.4 %collective-permute-start = (f32[8,1024]{1,0:T(8,128)S(1)}, f32[8,1024]{1,0:T(8,128)S(1)}, u32[]{:S(2)}, u32[]{:S(2)}) collective-permute-start(f32[8,1024]{1,0:T(8,128)S(1)} %get-tuple-element.27.a_ref), channel_id=1, source_target_pairs={{0,4},{4,0},{8,12},{12,8},{1,5},{5,1},{9,13},{13,9},{2,6},{6,2},{1... | collective-permute-start | bytes 98312 | tf_op jit(solution)/shard_map/ppermute | solution.py:40
  4.0 4.5 %collective-permute-start.1 = (bf16[8,1024]{1,0:T(8,128)(2,1)S(1)}, bf16[8,1024]{1,0:T(8,128)(2,1)S(1)}, u32[]{:S(2)}, u32[]{:S(2)}) collective-permute-start(bf16[8,1024]{1,0:T(8,128)(2,1)S(1)} %get-tuple-element.29), channel_id=1, source_target_pairs={{0,8},{4,12},{8,0},{12,4},{1,9},{5,13},{9,1},{13,5},{2,10},{6,14},... | collective-permute-start | bytes 49160 | tf_op jit(solution)/shard_map/ppermute | solution.py:40
  8.5 3.8 %collective-permute-start.2 = (bf16[8,1024]{1,0:T(8,128)(2,1)S(1)}, bf16[8,1024]{1,0:T(8,128)(2,1)S(1)}, u32[]{:S(2)}, u32[]{:S(2)}) collective-permute-start(bf16[8,1024]{1,0:T(8,128)(2,1)S(1)} %shard_map.57.a_ref), channel_id=1, source_target_pairs={{0,1},{1,0},{2,3},{3,2},{4,5},{5,4},{6,7},{7,6},{8,9},{9,8},{10,11... | collective-permute-start | bytes 49160 | tf_op jit(solution)/shard_map/ppermute | solution.py:40
  12.4 4.9 %collective-permute-start.3 = (bf16[16,1024]{1,0:T(8,128)(2,1)S(1)}, bf16[16,1024]{1,0:T(8,128)(2,1)S(1)}, u32[]{:S(2)}, u32[]{:S(2)}) collective-permute-start(bf16[16,1024]{1,0:T(8,128)(2,1)S(1)} %shard_map.58.a_ref), channel_id=1, source_target_pairs={{0,2},{1,3},{2,0},{3,1},{4,6},{5,7},{6,4},{7,5},{8,10},{9,11},{10,... | collective-permute-start | bytes 98312 | tf_op jit(solution)/shard_map/ppermute | solution.py:40
  21.7 2.1 %collective-permute-start.4 = (bf16[32,2048]{1,0:T(8,128)(2,1)S(1)}, bf16[32,2048]{1,0:T(8,128)(2,1)S(1)}, u32[]{:S(2)}, u32[]{:S(2)}) collective-permute-start(bf16[32,2048]{1,0:T(8,128)(2,1)S(1)} %get-tuple-element.33), channel_id=1, source_target_pairs={{0,4},{4,0},{8,12},{12,8},{1,5},{5,1},{9,13},{13,9},{2,6},{6,2},{1... | collective-permute-start | bytes 393224 | tf_op jit(solution)/shard_map/ppermute | solution.py:40
  23.3 4.0 %collective-permute-start.6 = (bf16[32,1024]{1,0:T(8,128)(2,1)S(1)}, bf16[32,1024]{1,0:T(8,128)(2,1)S(1)}, u32[]{:S(2)}, u32[]{:S(2)}) collective-permute-start(bf16[32,1024]{1,0:T(8,128)(2,1)S(1)} %get-tuple-element.37), channel_id=1, source_target_pairs={{0,4},{4,0},{8,12},{12,8},{1,5},{5,1},{9,13},{13,9},{2,6},{6,2},{1... | collective-permute-start | bytes 196616 | tf_op jit(solution)/shard_map/ppermute | solution.py:40
  23.9 5.6 %collective-permute-start.9 = (bf16[32,2048]{1,0:T(8,128)(2,1)S(1)}, bf16[32,2048]{1,0:T(8,128)(2,1)S(1)}, u32[]{:S(2)}, u32[]{:S(2)}) collective-permute-start(bf16[32,2048]{1,0:T(8,128)(2,1)S(1)} %get-tuple-element.34.refs_1_), channel_id=1, source_target_pairs={{0,8},{4,12},{8,0},{12,4},{1,9},{5,13},{9,1},{13,5},{2,10},{6,14},... | collective-permute-start | bytes 393224 | tf_op jit(solution)/shard_map/ppermute | solution.py:40
  25.8 5.9 %slice-start = ((s8[16777216]{0:T(1024)(128)(4,1)}), s8[4194304]{0:T(1024)(128)(4,1)S(1)}, s32[]{:S(2)}) async-start(s8[16777216]{0:T(1024)(128)(4,1)} %bitcast), calls=%async_computation | async-start | bytes 8388608
  25.8 5.9 %slice-start.1 = ((s8[16777216]{0:T(1024)(128)(4,1)}), s8[4194304]{0:T(1024)(128)(4,1)S(1)}, s32[]{:S(2)}) async-start(s8[16777216]{0:T(1024)(128)(4,1)} %bitcast), calls=%async_computation.1 | async-start | bytes 8388608
  25.8 5.9 %slice-start.2 = ((s8[16777216]{0:T(1024)(128)(4,1)}), s8[4194304]{0:T(1024)(128)(4,1)S(1)}, s32[]{:S(2)}) async-start(s8[16777216]{0:T(1024)(128)(4,1)} %bitcast), calls=%async_computation.2 | async-start | bytes 8388608
  27.4 1.3 %collective-permute-start.5 = (bf16[32,1024]{1,0:T(8,128)(2,1)S(1)}, bf16[32,1024]{1,0:T(8,128)(2,1)S(1)}, u32[]{:S(2)}, u32[]{:S(2)}) collective-permute-start(bf16[32,1024]{1,0:T(8,128)(2,1)S(1)} %get-tuple-element.36), channel_id=1, source_target_pairs={{0,4},{4,0},{8,12},{12,8},{1,5},{5,1},{9,13},{13,9},{2,6},{6,2},{1... | collective-permute-start | bytes 196616 | tf_op jit(solution)/shard_map/ppermute | solution.py:40
  29.5 2.4 %slice-start.3 = ((s8[16777216]{0:T(1024)(128)(4,1)}), s8[4194304]{0:T(1024)(128)(4,1)S(1)}, s32[]{:S(2)}) async-start(s8[16777216]{0:T(1024)(128)(4,1)} %bitcast), calls=%async_computation.3 | async-start | bytes 8388608
  29.5 2.2 %collective-permute-start.10 = (bf16[32,1024]{1,0:T(8,128)(2,1)S(1)}, bf16[32,1024]{1,0:T(8,128)(2,1)S(1)}, u32[]{:S(2)}, u32[]{:S(2)}) collective-permute-start(bf16[32,1024]{1,0:T(8,128)(2,1)S(1)} %shard_map.67.refs_0_), channel_id=1, source_target_pairs={{0,4},{4,0},{8,12},{12,8},{1,5},{5,1},{9,13},{13,9},{2,6},{6,2},{1... | collective-permute-start | bytes 196616 | tf_op jit(solution)/shard_map/ppermute | solution.py:40
  29.6 4.5 %collective-permute-start.8 = (bf16[32,1024]{1,0:T(8,128)(2,1)S(1)}, bf16[32,1024]{1,0:T(8,128)(2,1)S(1)}, u32[]{:S(2)}, u32[]{:S(2)}) collective-permute-start(bf16[32,1024]{1,0:T(8,128)(2,1)S(1)} %get-tuple-element.38.refs_0_), channel_id=1, source_target_pairs={{0,8},{4,12},{8,0},{12,4},{1,9},{5,13},{9,1},{13,5},{2,10},{6,14},... | collective-permute-start | bytes 196616 | tf_op jit(solution)/shard_map/ppermute | solution.py:40
  31.4 4.3 %collective-permute-start.7 = (bf16[32,1024]{1,0:T(8,128)(2,1)S(1)}, bf16[32,1024]{1,0:T(8,128)(2,1)S(1)}, u32[]{:S(2)}, u32[]{:S(2)}) collective-permute-start(bf16[32,1024]{1,0:T(8,128)(2,1)S(1)} %get-tuple-element.40.refs_0_), channel_id=1, source_target_pairs={{0,8},{4,12},{8,0},{12,4},{1,9},{5,13},{9,1},{13,5},{2,10},{6,14},... | collective-permute-start | bytes 196616 | tf_op jit(solution)/shard_map/ppermute | solution.py:40
  34.1 1.6 %collective-permute-start.12 = (bf16[32,512]{1,0:T(8,128)(2,1)S(1)}, bf16[32,512]{1,0:T(8,128)(2,1)S(1)}, u32[]{:S(2)}, u32[]{:S(2)}) collective-permute-start(bf16[32,512]{1,0:T(8,128)(2,1)S(1)} %shard_map.69.refs_0_), channel_id=1, source_target_pairs={{0,4},{4,0},{8,12},{12,8},{1,5},{5,1},{9,13},{13,9},{2,6},{6,2},{1... | collective-permute-start | bytes 98312 | tf_op jit(solution)/shard_map/ppermute | solution.py:40
  35.7 1.4 %collective-permute-start.11 = (bf16[32,512]{1,0:T(8,128)(2,1)S(1)}, bf16[32,512]{1,0:T(8,128)(2,1)S(1)}, u32[]{:S(2)}, u32[]{:S(2)}) collective-permute-start(bf16[32,512]{1,0:T(8,128)(2,1)S(1)} %shard_map.70.refs_0_), channel_id=1, source_target_pairs={{0,4},{4,0},{8,12},{12,8},{1,5},{5,1},{9,13},{13,9},{2,6},{6,2},{1... | collective-permute-start | bytes 98312 | tf_op jit(solution)/shard_map/ppermute | solution.py:40
  38.3 4.8 %collective-permute-start.13 = (bf16[16,1024]{1,0:T(8,128)(2,1)S(1)}, bf16[16,1024]{1,0:T(8,128)(2,1)S(1)}, u32[]{:S(2)}, u32[]{:S(2)}) collective-permute-start(bf16[16,1024]{1,0:T(8,128)(2,1)S(1)} %get-tuple-element.44), channel_id=1, source_target_pairs={{0,2},{1,3},{2,0},{3,1},{4,6},{5,7},{6,4},{7,5},{8,10},{9,11},{10,... | collective-permute-start | bytes 98312 | tf_op jit(solution)/shard_map/ppermute | solution.py:40
  43.2 3.8 %collective-permute-start.14 = (bf16[8,1024]{1,0:T(8,128)(2,1)S(1)}, bf16[8,1024]{1,0:T(8,128)(2,1)S(1)}, u32[]{:S(2)}, u32[]{:S(2)}) collective-permute-start(bf16[8,1024]{1,0:T(8,128)(2,1)S(1)} %get-tuple-element.46), channel_id=1, source_target_pairs={{0,1},{1,0},{2,3},{3,2},{4,5},{5,4},{6,7},{7,6},{8,9},{9,8},{10,11... | collective-permute-start | bytes 49160 | tf_op jit(solution)/shard_map/ppermute | solution.py:40
  47.0 3.8 %collective-permute-start.15 = (bf16[8,1024]{1,0:T(8,128)(2,1)S(1)}, bf16[8,1024]{1,0:T(8,128)(2,1)S(1)}, u32[]{:S(2)}, u32[]{:S(2)}) collective-permute-start(bf16[8,1024]{1,0:T(8,128)(2,1)S(1)} %get-tuple-element.48), channel_id=1, source_target_pairs={{0,8},{4,12},{8,0},{12,4},{1,9},{5,13},{9,1},{13,5},{2,10},{6,14},... | collective-permute-start | bytes 49160 | tf_op jit(solution)/shard_map/ppermute | solution.py:40
  50.8 1.2 %collective-permute-start.16 = (f32[8,1024]{1,0:T(8,128)S(1)}, f32[8,1024]{1,0:T(8,128)S(1)}, u32[]{:S(2)}, u32[]{:S(2)}) collective-permute-start(f32[8,1024]{1,0:T(8,128)S(1)} %shard_map.76.a_ref), channel_id=1, source_target_pairs={{0,4},{4,0},{8,12},{12,8},{1,5},{5,1},{9,13},{13,9},{2,6},{6,2},{1... | collective-permute-start | bytes 98312 | tf_op jit(solution)/shard_map/ppermute | solution.py:40

commit v4 on v3

--- a/solution.py
+++ b/solution.py
@@ -14,10 +14,10 @@
 LIMIT = 2 * 1024 * 1024
 PIECES = 4
 WAIT = 30
-SUMS = (0.3, 0.3, 0.3)
-PAIR = 6
-HIDDEN = (5, 0.1, 0.1)
-DOWN = 3
+SUMS = (0.1, 0.1, 0.1)
+PAIRS = (3, 1.5, 1.5)
+HIDDEN = (3, 0.1, 0.1)
+DOWN = (0.1, 0.1, 0.1)
 VMEM = pl.BlockSpec(memory_space=pltpu.VMEM)
 HBM = pl.BlockSpec(memory_space=pltpu.HBM)
 sds = jax.ShapeDtypeStruct
@@ -132,23 +132,22 @@
             out_ref[:, half + t : half + t + tile] = dot(x_ref[...], up_ref[:, at]).astype(out_ref.dtype)
 
 
-def down_body(*refs, start, half, own, away, first):
-    h_refs, (weight_ref, *acc, out_ref) = refs[: own + away], refs[own + away :]
+def down_body(*refs, parts, first=False):
+    h_refs, (weight_ref, *acc, out_ref) = refs[: len(parts)], refs[len(parts) :]
     core = core_index()
-    which = ([core] if own else []) + ([1 - core] if away else [])
     width = out_ref.shape[1]
     tile = tile_of(width, 512)
     for t in range(0, width, tile):
         total = None if first else acc[0][:, t : t + tile]
-        for h_ref, w in zip(h_refs, which):
-            at = pl.ds(pl.multiple_of(start + w * half, 16), half)
+        for h_ref, (away, start, half) in zip(h_refs, parts):
+            at = pl.ds(pl.multiple_of(start + (1 - core if away else core) * half, 16), half)
             part = dot(h_ref[...], weight_ref[at, t : t + tile])
             total = part if total is None else total + part
         out_ref[:, t : t + tile] = total.astype(out_ref.dtype)
 
 
-def last_body(h_ref, weight_ref, acc_ref, basis_ref, keep_ref, send_ref, rows_ref, *, start, half):
-    down_body(h_ref, weight_ref, acc_ref, rows_ref, start=start, half=half, own=0, away=1, first=False)
+def last_body(h_ref, weight_ref, acc_ref, basis_ref, keep_ref, send_ref, rows_ref, *, parts):
+    down_body(h_ref, weight_ref, acc_ref, rows_ref, parts=parts)
     top = keep_ref.shape[0]
     tile = tile_of(R, 512)
     for t in range(0, R, tile):
@@ -199,7 +198,7 @@
         keep, send = call(
             functools.partial(pair_body, start=start),
             both((rows, span)),
-            PAIR * span / ff,
+            PAIRS[q],
             restored,
             gate_weight,
             up_weight,
@@ -211,35 +210,34 @@
         if q > 0:
             sums.append(call(add_two_body, both((rows, spans[q - 1][1])), SUMS[q - 1], *pairs[q - 1], keep))
     sums.append(call(add_two_body, both((rows, spans[-1][1])), SUMS[-1], *pairs[-1], sums[-1][1]))
-    acc = None
-    own = None
+    acc, early, own, late = None, None, None, []
     for q, ((start, span), (total, send)) in enumerate(zip(spans, sums)):
         mask = 2
         while 2 * mask < dp:
             total, send = call(add_two_body, both(total.shape), 0.1, total, swap(send, "dp", mask, dp))
             mask *= 2
         half = span // 2
-        order = [sums[-1][1]] if q == 0 else [acc] if q == 1 else [own]
+        order = [sums[-1][1]] if q == 0 else [early] if q == 1 else [own]
         own = call(hidden_body, sds((rows, half), BF16), HIDDEN[q], total, swap(send, "dp", mask, dp), *order)
         away = swap(own, "dp", 1, dp)
-        time = DOWN * span / ff
-        shape = sds((rows, width), F32)
-        if start + span < ff:
-            body = functools.partial(down_body, start=start, half=half, own=1, away=1, first=acc is None)
-            acc = call(body, shape, time, own, away, down_weight, *([] if acc is None else [acc]))
-        else:
-            body = functools.partial(down_body, start=start, half=half, own=1, away=0, first=False)
-            acc = call(body, shape, time / 2, own, down_weight, acc)
-            codes, send = call(
-                functools.partial(last_body, start=start, half=half),
-                [sds((rows // 2, R), F32), sds((rows // 2, R), BF16)],
-                1,
-                away,
-                down_weight,
-                acc,
-                basis,
-                scratch=[pltpu.VMEM((rows, width), BF16)],
-            )
+        blocks = late + [(own, (0, start, half))]
+        body = functools.partial(down_body, parts=tuple(part for _, part in blocks), first=acc is None)
+        acc = call(
+            body, sds((rows, width), F32), DOWN[q], *[h for h, _ in blocks], down_weight, *([] if acc is None else [acc])
+        )
+        early = acc if early is None else early
+        late = [(away, (1, start, half))]
+    ((away, part),) = late
+    codes, send = call(
+        functools.partial(last_body, parts=(part,)),
+        [sds((rows // 2, R), F32), sds((rows // 2, R), BF16)],
+        1,
+        away,
+        down_weight,
+        acc,
+        basis,
+        scratch=[pltpu.VMEM((rows, width), BF16)],
+    )
 
     mask = tensor // 2
     while mask > 1:

time: 54 us -> 52.5 us (0.972)
  waiting for transfers between devices: 17.6 us -> 15.1 us
  local copies, waits for them, and re-layouts: 0.24 us -> 2.09 us
  starting transfers between devices: 19.6 us -> 18.8 us
    ppermute x17, waiting for transfers between devices: 17.6 us -> 15.1 us  [swap(): return lax.ppermute(value, axis, [(i, i ^ mask) for i in range(size)])]
    unnamed x24, local copies, waits for them, and re-layouts: 0.24 us -> 2.09 us
    ppermute x17, starting transfers between devices: 19.6 us -> 18.8 us  [swap(): return lax.ppermute(value, axis, [(i, i ^ mask) for i in range(size)])]
  transfers between devices with their start and end apart: 17 -> 17, of which waited for: 12 -> 10; matrix products, arithmetic and copies ran while one was open for 0% -> 0% of each run, Pallas kernels for 11% -> 12%
where the time goes in v4:
time: 52.5 us; the launch traced here: 52.4 us
  starting transfers between devices  18.8 us (36%)
  Pallas kernels  16.1 us (31%)
  waiting for transfers between devices  15.1 us (29%)
  local copies, waits for them, and re-layouts  2.09 us (4%)
    ppermute x17, starting transfers between devices, swap(): return lax.ppermute(value, axis, [(i, i ^ mask) for i in range(size)])  18.8 us
    pallas_call x23, Pallas kernels, call(): pl.pallas_call(body, out_shape=out, in_specs=[HBM if i in fixed else VMEM...  16.1 us
    ppermute x17, waiting for transfers between devices, swap(): return lax.ppermute(value, axis, [(i, i ^ mask) for i in range(size)])  15.1 us
    unnamed x24, local copies, waits for them, and re-layouts  2.09 us
  transfers between devices with their start and end apart: 17, of which 10 were waited for; matrix products, arithmetic and copies ran while one was open for 0% of the time, Pallas kernels for 12%

profile of v4, /device:TPU:0, one launch (start us, length us, event | category | flops | bytes accessed | tf_op | source)
XLA Modules:
  0.0 52.4 jit_solution(15660664243514652129)
XLA Ops:
  0.0 2.5 %shard_map.55 = (f32[8,1024]{1,0:T(8,128)S(1)}, bf16[2048,1024]{1,0:T(8,128)(2,1)S(1)}) custom-call(bf16[8,2048]{1,0:T(8,128)(2,1)} %x_ref.1, bf16[2048,1024]{1,0:T(8,128)(2,1)} %basis_ref.1), custom_call_target="tpu_custom_call" | custom-call | flops 1150000000 | bytes 65536 | tf_op jit(solution)/shard_map/pallas_call | solution.py:28
  2.5 0.0 slice-start.4
  2.5 0.0 slice-start.8
  2.5 0.0 slice-start.5
  2.5 0.0 slice-start.6
  2.6 0.0 slice-start.9
  2.6 0.5 collective-permute-start
  3.1 0.9 %collective-permute-done.b_ref = f32[8,1024]{1,0:T(8,128)S(1)} collective-permute-done((f32[8,1024]{1,0:T(8,128)S(1)}, f32[8,1024]{1,0:T(8,128)S(1)}, u32[]{:S(2)}, u32[]{:S(2)}) %collective-permute-start) | collective-permute-done | bytes 32800 | tf_op jit(solution)/shard_map/ppermute | solution.py:40
  4.0 2.8 %collective-permute-start.1 = (bf16[8,1024]{1,0:T(8,128)(2,1)S(1)}, bf16[8,1024]{1,0:T(8,128)(2,1)S(1)}, u32[]{:S(2)}, u32[]{:S(2)}) collective-permute-start(bf16[8,1024]{1,0:T(8,128)(2,1)S(1)} %get-tuple-element.29), channel_id=1, source_target_pairs={{0,8},{4,12},{8,0},{12,4},{1,9},{5,13},{9,1},{13,5},{2,10},{6,14},... | collective-permute-start | bytes 49160 | tf_op jit(solution)/shard_map/ppermute | solution.py:40
  6.8 1.7 %collective-permute-done.1.b_ref = bf16[8,1024]{1,0:T(8,128)(2,1)S(1)} collective-permute-done((bf16[8,1024]{1,0:T(8,128)(2,1)S(1)}, bf16[8,1024]{1,0:T(8,128)(2,1)S(1)}, u32[]{:S(2)}, u32[]{:S(2)}) %collective-permute-start.1) | collective-permute-done | bytes 16416 | tf_op jit(solution)/shard_map/ppermute | solution.py:40
  8.5 2.1 %collective-permute-start.2 = (bf16[8,1024]{1,0:T(8,128)(2,1)S(1)}, bf16[8,1024]{1,0:T(8,128)(2,1)S(1)}, u32[]{:S(2)}, u32[]{:S(2)}) collective-permute-start(bf16[8,1024]{1,0:T(8,128)(2,1)S(1)} %shard_map.57.a_ref), channel_id=1, source_target_pairs={{0,1},{1,0},{2,3},{3,2},{4,5},{5,4},{6,7},{7,6},{8,9},{9,8},{10,11... | collective-permute-start | bytes 49160 | tf_op jit(solution)/shard_map/ppermute | solution.py:40
  10.6 1.7 %collective-permute-done.2.b_ref = bf16[8,1024]{1,0:T(8,128)(2,1)S(1)} collective-permute-done((bf16[8,1024]{1,0:T(8,128)(2,1)S(1)}, bf16[8,1024]{1,0:T(8,128)(2,1)S(1)}, u32[]{:S(2)}, u32[]{:S(2)}) %collective-permute-start.2) | collective-permute-done | bytes 16416 | tf_op jit(solution)/shard_map/ppermute | solution.py:40
  12.4 3.0 %collective-permute-start.3 = (bf16[16,1024]{1,0:T(8,128)(2,1)S(1)}, bf16[16,1024]{1,0:T(8,128)(2,1)S(1)}, u32[]{:S(2)}, u32[]{:S(2)}) collective-permute-start(bf16[16,1024]{1,0:T(8,128)(2,1)S(1)} %shard_map.58.a_ref), channel_id=1, source_target_pairs={{0,2},{1,3},{2,0},{3,1},{4,6},{5,7},{6,4},{7,5},{8,10},{9,11},{10,... | collective-permute-start | bytes 98312 | tf_op jit(solution)/shard_map/ppermute | solution.py:40
  15.4 1.9 %collective-permute-done.3.b_ref = bf16[16,1024]{1,0:T(8,128)(2,1)S(1)} collective-permute-done((bf16[16,1024]{1,0:T(8,128)(2,1)S(1)}, bf16[16,1024]{1,0:T(8,128)(2,1)S(1)}, u32[]{:S(2)}, u32[]{:S(2)}) %collective-permute-start.3) | collective-permute-done | bytes 32800 | tf_op jit(solution)/shard_map/ppermute | solution.py:40
  17.3 1.3 %shard_map.60.x_ref = bf16[32,2048]{1,0:T(8,128)(2,1)S(1)} custom-call(bf16[32,1024]{1,0:T(8,128)(2,1)S(1)} %shard_map.59.codes_ref, bf16[2048,1024]{1,0:T(8,128)(2,1)S(1)} %get-tuple-element.30.basis_ref), custom_call_target="tpu_custom_call" | custom-call | flops 575000000 | bytes 65536 | tf_op jit(solution)/shard_map/pallas_call | solution.py:28
  18.6 0.0 slice-done.4
  18.7 3.0 %shard_map.61 = (f32[32,2048]{1,0:T(8,128)S(1)}, bf16[32,2048]{1,0:T(8,128)(2,1)S(1)}) custom-call(bf16[32,2048]{1,0:T(8,128)(2,1)S(1)} %shard_map.60.x_ref, bf16[2048,4096]{1,0:T(8,128)(2,1)S(1)} %bitcast.3, bf16[2048,4096]{1,0:T(8,128)(2,1)S(1)} %bitcast.5), custom_call_target="tpu_custom_call" | custom-call | flops 3449999872 | bytes 65536 | tf_op jit(solution)/shard_map/pallas_call | solution.py:28
  21.7 1.6 %shard_map.62 = (f32[32,1024]{1,0:T(8,128)S(1)}, bf16[32,1024]{1,0:T(8,128)(2,1)S(1)}) custom-call(bf16[32,2048]{1,0:T(8,128)(2,1)S(1)} %shard_map.60.x_ref, bf16[2048,4096]{1,0:T(8,128)(2,1)S(1)} %bitcast.3, bf16[2048,4096]{1,0:T(8,128)(2,1)S(1)} %bitcast.5, f32[32,2048]{1,0:T(8,128)S(1)} %get-tuple-element.31.refs_0_.a_ref), custom_call_target="tpu_custom_call" | custom-call | flops 1724999936 | bytes 65536 | tf_op jit(solution)/shard_map/pallas_call | solution.py:28
  23.3 0.5 collective-permute-start.6
  23.9 0.0 slice-start
  23.9 0.0 slice-start.1
  23.9 0.0 slice-start.2
  23.9 1.9 %collective-permute-start.9 = (bf16[32,2048]{1,0:T(8,128)(2,1)S(1)}, bf16[32,2048]{1,0:T(8,128)(2,1)S(1)}, u32[]{:S(2)}, u32[]{:S(2)}) collective-permute-start(bf16[32,2048]{1,0:T(8,128)(2,1)S(1)} %get-tuple-element.34.refs_1_), channel_id=1, source_target_pairs={{0,8},{4,12},{8,0},{12,4},{1,9},{5,13},{9,1},{13,5},{2,10},{6,14},... | collective-permute-start | bytes 393224 | tf_op jit(solution)/shard_map/ppermute | solution.py:40
  25.8 1.6 %shard_map.64 = (f32[32,1024]{1,0:T(8,128)S(1)}, bf16[32,1024]{1,0:T(8,128)(2,1)S(1)}) custom-call(bf16[32,2048]{1,0:T(8,128)(2,1)S(1)} %shard_map.60.x_ref, bf16[2048,4096]{1,0:T(8,128)(2,1)S(1)} %bitcast.3, bf16[2048,4096]{1,0:T(8,128)(2,1)S(1)} %bitcast.5, f32[32,1024]{1,0:T(8,128)S(1)} %get-tuple-element.32.refs_0_.a_ref, ...), custom_call_target="tpu_custom_call" | custom-call | flops 1724999936 | bytes 65536 | tf_op jit(solution)/shard_map/pallas_call | solution.py:28
  27.4 0.0 collective-permute-done.6.b_ref
  27.4 0.3 collective-permute-start.8
  27.7 1.0 %collective-permute-done.5.b_ref = bf16[32,1024]{1,0:T(8,128)(2,1)S(1)} collective-permute-done((bf16[32,1024]{1,0:T(8,128)(2,1)S(1)}, bf16[32,1024]{1,0:T(8,128)(2,1)S(1)}, u32[]{:S(2)}, u32[]{:S(2)}) %collective-permute-start.5) | collective-permute-done | bytes 65568 | tf_op jit(solution)/shard_map/ppermute | solution.py:40
  28.7 0.9 %collective-permute-start.7 = (bf16[32,1024]{1,0:T(8,128)(2,1)S(1)}, bf16[32,1024]{1,0:T(8,128)(2,1)S(1)}, u32[]{:S(2)}, u32[]{:S(2)}) collective-permute-start(bf16[32,1024]{1,0:T(8,128)(2,1)S(1)} %get-tuple-element.40.refs_0_), channel_id=1, source_target_pairs={{0,8},{4,12},{8,0},{12,4},{1,9},{5,13},{9,1},{13,5},{2,10},{6,14},... | collective-permute-start | bytes 196616 | tf_op jit(solution)/shard_map/ppermute | solution.py:40
  29.6 0.1 shard_map.67.refs_0_
  29.7 0.1 collective-permute-start.12
  29.8 2.0 %slice-done.3 = s8[4194304]{0:T(1024)(128)(4,1)S(1)} async-done(((s8[16777216]{0:T(1024)(128)(4,1)}), s8[4194304]{0:T(1024)(128)(4,1)S(1)}, s32[]{:S(2)}) %slice-start.3) | async-done | bytes 4194328
  31.8 0.8 %shard_map.68.refs_0_.refs_3_ = f32[32,2048]{1,0:T(8,128)S(1)} custom-call(bf16[32,1024]{1,0:T(8,128)(2,1)S(1)} %shard_map.67.refs_0_, bf16[4096,2048]{1,0:T(8,128)(2,1)S(1)} %bitcast.1), custom_call_target="tpu_custom_call" | custom-call | flops 115000000 | bytes 65536 | tf_op jit(solution)/shard_map/pallas_call | solution.py:28
  32.7 0.1 collective-permute-start.11
  32.8 0.6 %collective-permute-done.7.b_ref = bf16[32,1024]{1,0:T(8,128)(2,1)S(1)} collective-permute-done((bf16[32,1024]{1,0:T(8,128)(2,1)S(1)}, bf16[32,1024]{1,0:T(8,128)(2,1)S(1)}, u32[]{:S(2)}, u32[]{:S(2)}) %collective-permute-start.7) | collective-permute-done | bytes 65568 | tf_op jit(solution)/shard_map/ppermute | solution.py:40
  33.4 0.1 collective-permute-start.10
  33.5 1.2 %shard_map.71.refs_3_ = f32[32,2048]{1,0:T(8,128)S(1)} custom-call(bf16[32,1024]{1,0:T(8,128)(2,1)S(1)} %collective-permute-done.12.refs_0_, bf16[32,512]{1,0:T(8,128)(2,1)S(1)} %shard_map.69.refs_0_.refs_1_, bf16[4096,2048]{1,0:T(8,128)(2,1)S(1)} %bitcast.1, f32[32,2048]{1,0:T(8,128)S(1)} %shard_map.68.refs_0_.refs_3_), custom_call_target="tpu_custom_call" | custom-call | flops 115000000 | bytes 65536 | tf_op jit(solution)/shard_map/pallas_call | solution.py:28
  34.7 0.0 collective-permute-done.11.refs_0_
  34.7 0.8 %shard_map.72.acc_ref = f32[32,2048]{1,0:T(8,128)S(1)} custom-call(bf16[32,512]{1,0:T(8,128)(2,1)S(1)} %collective-permute-done.11.refs_0_, bf16[32,512]{1,0:T(8,128)(2,1)S(1)} %shard_map.70.refs_1_, bf16[4096,2048]{1,0:T(8,128)(2,1)S(1)} %bitcast.1, f32[32,2048]{1,0:T(8,128)S(1)} %shard_map.71.refs_3_), custom_call_target="tpu_custom_call" | custom-call | flops 115000000 | bytes 65536 | tf_op jit(solution)/shard_map/pallas_call | solution.py:28
  35.6 0.0 collective-permute-done.10.h_ref
  35.6 1.2 %shard_map.73 = (f32[16,1024]{1,0:T(8,128)S(1)}, bf16[16,1024]{1,0:T(8,128)(2,1)S(1)}) custom-call(bf16[32,512]{1,0:T(8,128)(2,1)S(1)} %collective-permute-done.10.h_ref, bf16[4096,2048]{1,0:T(8,128)(2,1)S(1)} %bitcast.1, f32[32,2048]{1,0:T(8,128)S(1)} %shard_map.72.acc_ref, bf16[2048,1024]{1,0:T(8,128)(2,1)S(1)} %get-tuple-element.30.basis_ref), custom_call_target="tpu_custom_call" | custom-call | flops 1150000000 | bytes 65536 | tf_op jit(solution)/shard_map/pallas_call | solution.py:28
  36.8 2.6 %collective-permute-start.13 = (bf16[16,1024]{1,0:T(8,128)(2,1)S(1)}, bf16[16,1024]{1,0:T(8,128)(2,1)S(1)}, u32[]{:S(2)}, u32[]{:S(2)}) collective-permute-start(bf16[16,1024]{1,0:T(8,128)(2,1)S(1)} %get-tuple-element.44), channel_id=1, source_target_pairs={{0,2},{1,3},{2,0},{3,1},{4,6},{5,7},{6,4},{7,5},{8,10},{9,11},{10,... | collective-permute-start | bytes 98312 | tf_op jit(solution)/shard_map/ppermute | solution.py:40
  39.4 2.2 %collective-permute-done.13.b_ref = bf16[16,1024]{1,0:T(8,128)(2,1)S(1)} collective-permute-done((bf16[16,1024]{1,0:T(8,128)(2,1)S(1)}, bf16[16,1024]{1,0:T(8,128)(2,1)S(1)}, u32[]{:S(2)}, u32[]{:S(2)}) %collective-permute-start.13) | collective-permute-done | bytes 32800 | tf_op jit(solution)/shard_map/ppermute | solution.py:40
  41.6 1.7 %collective-permute-start.14 = (bf16[8,1024]{1,0:T(8,128)(2,1)S(1)}, bf16[8,1024]{1,0:T(8,128)(2,1)S(1)}, u32[]{:S(2)}, u32[]{:S(2)}) collective-permute-start(bf16[8,1024]{1,0:T(8,128)(2,1)S(1)} %get-tuple-element.46), channel_id=1, source_target_pairs={{0,1},{1,0},{2,3},{3,2},{4,5},{5,4},{6,7},{7,6},{8,9},{9,8},{10,11... | collective-permute-start | bytes 49160 | tf_op jit(solution)/shard_map/ppermute | solution.py:40
  43.3 2.1 %collective-permute-done.14.b_ref = bf16[8,1024]{1,0:T(8,128)(2,1)S(1)} collective-permute-done((bf16[8,1024]{1,0:T(8,128)(2,1)S(1)}, bf16[8,1024]{1,0:T(8,128)(2,1)S(1)}, u32[]{:S(2)}, u32[]{:S(2)}) %collective-permute-start.14) | collective-permute-done | bytes 16416 | tf_op jit(solution)/shard_map/ppermute | solution.py:40
  45.4 2.2 %collective-permute-start.15 = (bf16[8,1024]{1,0:T(8,128)(2,1)S(1)}, bf16[8,1024]{1,0:T(8,128)(2,1)S(1)}, u32[]{:S(2)}, u32[]{:S(2)}) collective-permute-start(bf16[8,1024]{1,0:T(8,128)(2,1)S(1)} %get-tuple-element.48), channel_id=1, source_target_pairs={{0,8},{4,12},{8,0},{12,4},{1,9},{5,13},{9,1},{13,5},{2,10},{6,14},... | collective-permute-start | bytes 49160 | tf_op jit(solution)/shard_map/ppermute | solution.py:40
  47.6 1.7 %collective-permute-done.15.b_ref = bf16[8,1024]{1,0:T(8,128)(2,1)S(1)} collective-permute-done((bf16[8,1024]{1,0:T(8,128)(2,1)S(1)}, bf16[8,1024]{1,0:T(8,128)(2,1)S(1)}, u32[]{:S(2)}, u32[]{:S(2)}) %collective-permute-start.15) | collective-permute-done | bytes 16416 | tf_op jit(solution)/shard_map/ppermute | solution.py:40
  49.3 1.2 %collective-permute-done.16.b_ref = f32[8,1024]{1,0:T(8,128)S(1)} collective-permute-done((f32[8,1024]{1,0:T(8,128)S(1)}, f32[8,1024]{1,0:T(8,128)S(1)}, u32[]{:S(2)}, u32[]{:S(2)}) %collective-permute-start.16) | collective-permute-done | bytes 32800 | tf_op jit(solution)/shard_map/ppermute | solution.py:40
  50.5 1.8 %shard_map.77 = bf16[8,2048]{1,0:T(8,128)(2,1)} custom-call(f32[8,1024]{1,0:T(8,128)S(1)} %shard_map.76.a_ref, f32[8,1024]{1,0:T(8,128)S(1)} %collective-permute-done.16.b_ref, bf16[2048,1024]{1,0:T(8,128)(2,1)S(1)} %get-tuple-element.30.basis_ref), custom_call_target="tpu_custom_call" | custom-call | flops 1150000000 | bytes 65536 | tf_op jit(solution)/shard_map/pallas_call | solution.py:28
  (36 shorter events, 0.3 us)
Async XLA Ops:
  2.5 16.1 %slice-start.4 = ((s8[16777216]{0:T(1024)(128)(4,1)}), s8[4194304]{0:T(1024)(128)(4,1)S(1)}, s32[]{:S(2)}) async-start(s8[16777216]{0:T(1024)(128)(4,1)} %bitcast.2), calls=%async_computation.4 | async-start | bytes 8388608
  2.5 16.1 %slice-start.8 = ((s8[16777216]{0:T(1024)(128)(4,1)}), s8[4194304]{0:T(1024)(128)(4,1)S(1)}, s32[]{:S(2)}) async-start(s8[16777216]{0:T(1024)(128)(4,1)} %bitcast.4), calls=%async_computation.8 | async-start | bytes 8388608
  2.5 16.1 %slice-start.5 = ((s8[16777216]{0:T(1024)(128)(4,1)}), s8[4194304]{0:T(1024)(128)(4,1)S(1)}, s32[]{:S(2)}) async-start(s8[16777216]{0:T(1024)(128)(4,1)} %bitcast.2), calls=%async_computation.5 | async-start | bytes 8388608
  2.5 16.1 %slice-start.6 = ((s8[16777216]{0:T(1024)(128)(4,1)}), s8[4194304]{0:T(1024)(128)(4,1)S(1)}, s32[]{:S(2)}) async-start(s8[16777216]{0:T(1024)(128)(4,1)} %bitcast.2), calls=%async_computation.6 | async-start | bytes 8388608
  2.5 16.1 %slice-start.7 = ((s8[16777216]{0:T(1024)(128)(4,1)}), s8[4194304]{0:T(1024)(128)(4,1)S(1)}, s32[]{:S(2)}) async-start(s8[16777216]{0:T(1024)(128)(4,1)} %bitcast.2), calls=%async_computation.7 | async-start | bytes 8388608
  2.6 16.1 %slice-start.9 = ((s8[16777216]{0:T(1024)(128)(4,1)}), s8[4194304]{0:T(1024)(128)(4,1)S(1)}, s32[]{:S(2)}) async-start(s8[16777216]{0:T(1024)(128)(4,1)} %bitcast.4), calls=%async_computation.9 | async-start | bytes 8388608
  2.6 16.1 %slice-start.10 = ((s8[16777216]{0:T(1024)(128)(4,1)}), s8[4194304]{0:T(1024)(128)(4,1)S(1)}, s32[]{:S(2)}) async-start(s8[16777216]{0:T(1024)(128)(4,1)} %bitcast.4), calls=%async_computation.10 | async-start | bytes 8388608
  2.6 16.1 %slice-start.11 = ((s8[16777216]{0:T(1024)(128)(4,1)}), s8[4194304]{0:T(1024)(128)(4,1)S(1)}, s32[]{:S(2)}) async-start(s8[16777216]{0:T(1024)(128)(4,1)} %bitcast.4), calls=%async_computation.11 | async-start | bytes 8388608
  2.6 1.4 %collective-permute-start = (f32[8,1024]{1,0:T(8,128)S(1)}, f32[8,1024]{1,0:T(8,128)S(1)}, u32[]{:S(2)}, u32[]{:S(2)}) collective-permute-start(f32[8,1024]{1,0:T(8,128)S(1)} %get-tuple-element.27.a_ref), channel_id=1, source_target_pairs={{0,4},{4,0},{8,12},{12,8},{1,5},{5,1},{9,13},{13,9},{2,6},{6,2},{1... | collective-permute-start | bytes 98312 | tf_op jit(solution)/shard_map/ppermute | solution.py:40
  4.0 4.5 %collective-permute-start.1 = (bf16[8,1024]{1,0:T(8,128)(2,1)S(1)}, bf16[8,1024]{1,0:T(8,128)(2,1)S(1)}, u32[]{:S(2)}, u32[]{:S(2)}) collective-permute-start(bf16[8,1024]{1,0:T(8,128)(2,1)S(1)} %get-tuple-element.29), channel_id=1, source_target_pairs={{0,8},{4,12},{8,0},{12,4},{1,9},{5,13},{9,1},{13,5},{2,10},{6,14},... | collective-permute-start | bytes 49160 | tf_op jit(solution)/shard_map/ppermute | solution.py:40
  8.5 3.8 %collective-permute-start.2 = (bf16[8,1024]{1,0:T(8,128)(2,1)S(1)}, bf16[8,1024]{1,0:T(8,128)(2,1)S(1)}, u32[]{:S(2)}, u32[]{:S(2)}) collective-permute-start(bf16[8,1024]{1,0:T(8,128)(2,1)S(1)} %shard_map.57.a_ref), channel_id=1, source_target_pairs={{0,1},{1,0},{2,3},{3,2},{4,5},{5,4},{6,7},{7,6},{8,9},{9,8},{10,11... | collective-permute-start | bytes 49160 | tf_op jit(solution)/shard_map/ppermute | solution.py:40
  12.4 4.9 %collective-permute-start.3 = (bf16[16,1024]{1,0:T(8,128)(2,1)S(1)}, bf16[16,1024]{1,0:T(8,128)(2,1)S(1)}, u32[]{:S(2)}, u32[]{:S(2)}) collective-permute-start(bf16[16,1024]{1,0:T(8,128)(2,1)S(1)} %shard_map.58.a_ref), channel_id=1, source_target_pairs={{0,2},{1,3},{2,0},{3,1},{4,6},{5,7},{6,4},{7,5},{8,10},{9,11},{10,... | collective-permute-start | bytes 98312 | tf_op jit(solution)/shard_map/ppermute | solution.py:40
  21.7 2.1 %collective-permute-start.4 = (bf16[32,2048]{1,0:T(8,128)(2,1)S(1)}, bf16[32,2048]{1,0:T(8,128)(2,1)S(1)}, u32[]{:S(2)}, u32[]{:S(2)}) collective-permute-start(bf16[32,2048]{1,0:T(8,128)(2,1)S(1)} %get-tuple-element.33), channel_id=1, source_target_pairs={{0,4},{4,0},{8,12},{12,8},{1,5},{5,1},{9,13},{13,9},{2,6},{6,2},{1... | collective-permute-start | bytes 393224 | tf_op jit(solution)/shard_map/ppermute | solution.py:40
  23.3 4.1 %collective-permute-start.6 = (bf16[32,1024]{1,0:T(8,128)(2,1)S(1)}, bf16[32,1024]{1,0:T(8,128)(2,1)S(1)}, u32[]{:S(2)}, u32[]{:S(2)}) collective-permute-start(bf16[32,1024]{1,0:T(8,128)(2,1)S(1)} %get-tuple-element.37), channel_id=1, source_target_pairs={{0,4},{4,0},{8,12},{12,8},{1,5},{5,1},{9,13},{13,9},{2,6},{6,2},{1... | collective-permute-start | bytes 196616 | tf_op jit(solution)/shard_map/ppermute | solution.py:40
  23.9 5.9 %slice-start = ((s8[16777216]{0:T(1024)(128)(4,1)}), s8[4194304]{0:T(1024)(128)(4,1)S(1)}, s32[]{:S(2)}) async-start(s8[16777216]{0:T(1024)(128)(4,1)} %bitcast), calls=%async_computation | async-start | bytes 8388608
  23.9 5.9 %slice-start.1 = ((s8[16777216]{0:T(1024)(128)(4,1)}), s8[4194304]{0:T(1024)(128)(4,1)S(1)}, s32[]{:S(2)}) async-start(s8[16777216]{0:T(1024)(128)(4,1)} %bitcast), calls=%async_computation.1 | async-start | bytes 8388608
  23.9 5.9 %slice-start.2 = ((s8[16777216]{0:T(1024)(128)(4,1)}), s8[4194304]{0:T(1024)(128)(4,1)S(1)}, s32[]{:S(2)}) async-start(s8[16777216]{0:T(1024)(128)(4,1)} %bitcast), calls=%async_computation.2 | async-start | bytes 8388608
  23.9 5.7 %collective-permute-start.9 = (bf16[32,2048]{1,0:T(8,128)(2,1)S(1)}, bf16[32,2048]{1,0:T(8,128)(2,1)S(1)}, u32[]{:S(2)}, u32[]{:S(2)}) collective-permute-start(bf16[32,2048]{1,0:T(8,128)(2,1)S(1)} %get-tuple-element.34.refs_1_), channel_id=1, source_target_pairs={{0,8},{4,12},{8,0},{12,4},{1,9},{5,13},{9,1},{13,5},{2,10},{6,14},... | collective-permute-start | bytes 393224 | tf_op jit(solution)/shard_map/ppermute | solution.py:40
  27.4 1.3 %collective-permute-start.5 = (bf16[32,1024]{1,0:T(8,128)(2,1)S(1)}, bf16[32,1024]{1,0:T(8,128)(2,1)S(1)}, u32[]{:S(2)}, u32[]{:S(2)}) collective-permute-start(bf16[32,1024]{1,0:T(8,128)(2,1)S(1)} %get-tuple-element.36), channel_id=1, source_target_pairs={{0,4},{4,0},{8,12},{12,8},{1,5},{5,1},{9,13},{13,9},{2,6},{6,2},{1... | collective-permute-start | bytes 196616 | tf_op jit(solution)/shard_map/ppermute | solution.py:40
  27.4 5.2 %collective-permute-start.8 = (bf16[32,1024]{1,0:T(8,128)(2,1)S(1)}, bf16[32,1024]{1,0:T(8,128)(2,1)S(1)}, u32[]{:S(2)}, u32[]{:S(2)}) collective-permute-start(bf16[32,1024]{1,0:T(8,128)(2,1)S(1)} %get-tuple-element.38.refs_0_), channel_id=1, source_target_pairs={{0,8},{4,12},{8,0},{12,4},{1,9},{5,13},{9,1},{13,5},{2,10},{6,14},... | collective-permute-start | bytes 196616 | tf_op jit(solution)/shard_map/ppermute | solution.py:40
  28.7 4.7 %collective-permute-start.7 = (bf16[32,1024]{1,0:T(8,128)(2,1)S(1)}, bf16[32,1024]{1,0:T(8,128)(2,1)S(1)}, u32[]{:S(2)}, u32[]{:S(2)}) collective-permute-start(bf16[32,1024]{1,0:T(8,128)(2,1)S(1)} %get-tuple-element.40.refs_0_), channel_id=1, source_target_pairs={{0,8},{4,12},{8,0},{12,4},{1,9},{5,13},{9,1},{13,5},{2,10},{6,14},... | collective-permute-start | bytes 196616 | tf_op jit(solution)/shard_map/ppermute | solution.py:40
  29.6 2.2 %slice-start.3 = ((s8[16777216]{0:T(1024)(128)(4,1)}), s8[4194304]{0:T(1024)(128)(4,1)S(1)}, s32[]{:S(2)}) async-start(s8[16777216]{0:T(1024)(128)(4,1)} %bitcast), calls=%async_computation.3 | async-start | bytes 8388608
  29.7 3.8 %collective-permute-start.12 = (bf16[32,1024]{1,0:T(8,128)(2,1)S(1)}, bf16[32,1024]{1,0:T(8,128)(2,1)S(1)}, u32[]{:S(2)}, u32[]{:S(2)}) collective-permute-start(bf16[32,1024]{1,0:T(8,128)(2,1)S(1)} %shard_map.67.refs_0_), channel_id=1, source_target_pairs={{0,4},{4,0},{8,12},{12,8},{1,5},{5,1},{9,13},{13,9},{2,6},{6,2},{1... | collective-permute-start | bytes 196616 | tf_op jit(solution)/shard_map/ppermute | solution.py:40
  32.7 2.0 %collective-permute-start.11 = (bf16[32,512]{1,0:T(8,128)(2,1)S(1)}, bf16[32,512]{1,0:T(8,128)(2,1)S(1)}, u32[]{:S(2)}, u32[]{:S(2)}) collective-permute-start(bf16[32,512]{1,0:T(8,128)(2,1)S(1)} %shard_map.69.refs_0_.refs_1_), channel_id=1, source_target_pairs={{0,4},{4,0},{8,12},{12,8},{1,5},{5,1},{9,13},{13,9},{2,6},{6,2},{1... | collective-permute-start | bytes 98312 | tf_op jit(solution)/shard_map/ppermute | solution.py:40
  33.4 2.1 %collective-permute-start.10 = (bf16[32,512]{1,0:T(8,128)(2,1)S(1)}, bf16[32,512]{1,0:T(8,128)(2,1)S(1)}, u32[]{:S(2)}, u32[]{:S(2)}) collective-permute-start(bf16[32,512]{1,0:T(8,128)(2,1)S(1)} %shard_map.70.refs_1_), channel_id=1, source_target_pairs={{0,4},{4,0},{8,12},{12,8},{1,5},{5,1},{9,13},{13,9},{2,6},{6,2},{1... | collective-permute-start | bytes 98312 | tf_op jit(solution)/shard_map/ppermute | solution.py:40
  36.8 4.8 %collective-permute-start.13 = (bf16[16,1024]{1,0:T(8,128)(2,1)S(1)}, bf16[16,1024]{1,0:T(8,128)(2,1)S(1)}, u32[]{:S(2)}, u32[]{:S(2)}) collective-permute-start(bf16[16,1024]{1,0:T(8,128)(2,1)S(1)} %get-tuple-element.44), channel_id=1, source_target_pairs={{0,2},{1,3},{2,0},{3,1},{4,6},{5,7},{6,4},{7,5},{8,10},{9,11},{10,... | collective-permute-start | bytes 98312 | tf_op jit(solution)/shard_map/ppermute | solution.py:40
  41.6 3.8 %collective-permute-start.14 = (bf16[8,1024]{1,0:T(8,128)(2,1)S(1)}, bf16[8,1024]{1,0:T(8,128)(2,1)S(1)}, u32[]{:S(2)}, u32[]{:S(2)}) collective-permute-start(bf16[8,1024]{1,0:T(8,128)(2,1)S(1)} %get-tuple-element.46), channel_id=1, source_target_pairs={{0,1},{1,0},{2,3},{3,2},{4,5},{5,4},{6,7},{7,6},{8,9},{9,8},{10,11... | collective-permute-start | bytes 49160 | tf_op jit(solution)/shard_map/ppermute | solution.py:40
  45.4 3.9 %collective-permute-start.15 = (bf16[8,1024]{1,0:T(8,128)(2,1)S(1)}, bf16[8,1024]{1,0:T(8,128)(2,1)S(1)}, u32[]{:S(2)}, u32[]{:S(2)}) collective-permute-start(bf16[8,1024]{1,0:T(8,128)(2,1)S(1)} %get-tuple-element.48), channel_id=1, source_target_pairs={{0,8},{4,12},{8,0},{12,4},{1,9},{5,13},{9,1},{13,5},{2,10},{6,14},... | collective-permute-start | bytes 49160 | tf_op jit(solution)/shard_map/ppermute | solution.py:40
  49.3 1.2 %collective-permute-start.16 = (f32[8,1024]{1,0:T(8,128)S(1)}, f32[8,1024]{1,0:T(8,128)S(1)}, u32[]{:S(2)}, u32[]{:S(2)}) collective-permute-start(f32[8,1024]{1,0:T(8,128)S(1)} %shard_map.76.a_ref), channel_id=1, source_target_pairs={{0,4},{4,0},{8,12},{12,8},{1,5},{5,1},{9,13},{13,9},{2,6},{6,2},{1... | collective-permute-start | bytes 98312 | tf_op jit(solution)/shard_map/ppermute | solution.py:40

commit v5 on v4

--- a/solution.py
+++ b/solution.py
@@ -14,9 +14,10 @@
 LIMIT = 2 * 1024 * 1024
 PIECES = 4
 WAIT = 30
-SUMS = (0.1, 0.1, 0.1)
+TURN = 1
+SUMS = (0.1, 1, 0.1)
 PAIRS = (3, 1.5, 1.5)
-HIDDEN = (3, 0.1, 0.1)
+HIDDEN = (2, 0.1, 0.1)
 DOWN = (0.1, 0.1, 0.1)
 VMEM = pl.BlockSpec(memory_space=pltpu.VMEM)
 HBM = pl.BlockSpec(memory_space=pltpu.HBM)
@@ -49,10 +50,6 @@
 
 def dot(a, b):
     return jnp.dot(a, b, preferred_element_type=F32)
-
-
-def dot_t(a, b):
-    return lax.dot_general(a, b, (((1,), (1,)), ((), ())), preferred_element_type=F32)
 
 
 def core_index():
@@ -104,20 +101,28 @@
     out_ref[...] = (gate / (1 + jnp.exp(-gate)) * up).astype(BF16)
 
 
-def decode(codes, basis_ref, out_ref):
+def turn_body(basis_ref, *refs):
+    out_ref = refs[-1]
+    width = basis_ref.shape[0]
+    tile = tile_of(width, 256)
+    for t in range(0, width, tile):
+        out_ref[:, t : t + tile] = basis_ref[t : t + tile, :].T
+
+
+def decode(codes, turned_ref, out_ref):
     factor = (D / R) ** 0.5
-    width = basis_ref.shape[0]
+    width = turned_ref.shape[1]
     tile = tile_of(width, 512)
     for t in range(0, width, tile):
-        out_ref[:, t : t + tile] = (factor * dot_t(codes, basis_ref[t : t + tile, :])).astype(BF16)
-
-
-def restore_body(codes_ref, basis_ref, out_ref):
-    decode(codes_ref[...], basis_ref, out_ref)
-
-
-def final_body(a_ref, b_ref, basis_ref, out_ref):
-    decode((a_ref[...] + b_ref[...]).astype(BF16), basis_ref, out_ref)
+        out_ref[:, t : t + tile] = (factor * dot(codes, turned_ref[:, t : t + tile])).astype(BF16)
+
+
+def restore_body(codes_ref, turned_ref, out_ref):
+    decode(codes_ref[...], turned_ref, out_ref)
+
+
+def final_body(a_ref, b_ref, turned_ref, out_ref):
+    decode((a_ref[...] + b_ref[...]).astype(BF16), turned_ref, out_ref)
 
 
 def pair_body(x_ref, gate_ref, up_ref, *refs, start):
@@ -182,11 +187,13 @@
     codes = call(add_body, sds(codes.shape, BF16), 0.1, codes, swap(send, "dp", mask, dp))
     mask = 1
     while mask < tensor:
+        if 2 * mask == tensor:
+            turned = call(turn_body, sds((R, width), BF16), TURN, basis, codes)
         codes = call(
             join_body, sds((2 * codes.shape[0], R), BF16), 0.1, codes, swap(codes, "tensor", mask, tensor)
         )
         mask *= 2
-    restored = call(restore_body, sds((rows, width), BF16), 0.5, codes, basis)
+    restored = call(restore_body, sds((rows, width), BF16), 0.5, codes, turned)
 
     shares = SHARES if ff % 1024 == 0 else (1, 1)
     spans, at = [], 0
@@ -252,7 +259,7 @@
         codes, send = call(add_two_body, both(codes.shape), 0.1, codes, swap(send, "dp", mask, dp))
         mask //= 2
     codes = call(add_body, sds(codes.shape, F32), 0.1, codes, swap(send, "dp", 2, dp))
-    return call(final_body, sds((local, width), BF16), 1, codes, swap(codes, "dp", 1, dp), basis)
+    return call(final_body, sds((local, width), BF16), 1, codes, swap(codes, "dp", 1, dp), turned)
 
 
 SHARES = (2, 1, 1)

time: 52.5 us -> 51.4 us (0.979)
  waiting for transfers between devices: 15.1 us -> 17 us
  local copies, waits for them, and re-layouts: 2.09 us -> 0.28 us
  starting transfers between devices: 18.8 us -> 17.3 us
    ppermute x17, waiting for transfers between devices: 15.1 us -> 17 us  [swap(): return lax.ppermute(value, axis, [(i, i ^ mask) for i in range(size)])]
    unnamed x24 -> x28, local copies, waits for them, and re-layouts: 2.09 us -> 0.28 us
    ppermute x17, starting transfers between devices: 18.8 us -> 17.3 us  [swap(): return lax.ppermute(value, axis, [(i, i ^ mask) for i in range(size)])]
    pallas_call x23 -> x24, Pallas kernels: 16.1 us -> 16.3 us  [call(): pl.pallas_call(body, out_shape=out, in_specs=[HBM if i in fixed else VMEM...]
  transfers between devices with their start and end apart: 17 -> 17, of which waited for: 10 -> 11; matrix products, arithmetic and copies ran while one was open for 0% -> 0% of each run, Pallas kernels for 12% -> 14%
where the time goes in v5:
time: 51.4 us; the launch traced here: 51.3 us
  starting transfers between devices  17.3 us (34%)
  waiting for transfers between devices  17 us (33%)
  Pallas kernels  16.3 us (32%)
    ppermute x17, starting transfers between devices, swap(): return lax.ppermute(value, axis, [(i, i ^ mask) for i in range(size)])  17.3 us
    ppermute x17, waiting for transfers between devices, swap(): return lax.ppermute(value, axis, [(i, i ^ mask) for i in range(size)])  17 us
    pallas_call x24, Pallas kernels, call(): pl.pallas_call(body, out_shape=out, in_specs=[HBM if i in fixed else VMEM...  16.3 us
  transfers between devices with their start and end apart: 17, of which 11 were waited for; matrix products, arithmetic and copies ran while one was open for 0% of the time, Pallas kernels for 14%

profile of v5, /device:TPU:0, one launch (start us, length us, event | category | flops | bytes accessed | tf_op | source)
XLA Modules:
  0.0 51.3 jit_solution(8281647947570375009)
XLA Ops:
  0.0 2.5 %shard_map.55 = (f32[8,1024]{1,0:T(8,128)S(1)}, bf16[2048,1024]{1,0:T(8,128)(2,1)S(1)}) custom-call(bf16[8,2048]{1,0:T(8,128)(2,1)} %x_ref.1, bf16[2048,1024]{1,0:T(8,128)(2,1)} %basis_ref.1), custom_call_target="tpu_custom_call" | custom-call | flops 1150000000 | bytes 65536 | tf_op jit(solution)/shard_map/pallas_call | solution.py:29
  2.5 0.0 slice-start.4
  2.5 0.0 slice-start.8
  2.6 0.5 %collective-permute-start = (f32[8,1024]{1,0:T(8,128)S(1)}, f32[8,1024]{1,0:T(8,128)S(1)}, u32[]{:S(2)}, u32[]{:S(2)}) collective-permute-start(f32[8,1024]{1,0:T(8,128)S(1)} %get-tuple-element.27.a_ref), channel_id=1, source_target_pairs={{0,4},{4,0},{8,12},{12,8},{1,5},{5,1},{9,13},{13,9},{2,6},{6,2},{1... | collective-permute-start | bytes 98312 | tf_op jit(solution)/shard_map/ppermute | solution.py:41
  3.1 0.9 %collective-permute-done.b_ref = f32[8,1024]{1,0:T(8,128)S(1)} collective-permute-done((f32[8,1024]{1,0:T(8,128)S(1)}, f32[8,1024]{1,0:T(8,128)S(1)}, u32[]{:S(2)}, u32[]{:S(2)}) %collective-permute-start) | collective-permute-done | bytes 32800 | tf_op jit(solution)/shard_map/ppermute | solution.py:41
  4.0 2.8 %collective-permute-start.1 = (bf16[8,1024]{1,0:T(8,128)(2,1)S(1)}, bf16[8,1024]{1,0:T(8,128)(2,1)S(1)}, u32[]{:S(2)}, u32[]{:S(2)}) collective-permute-start(bf16[8,1024]{1,0:T(8,128)(2,1)S(1)} %get-tuple-element.29), channel_id=1, source_target_pairs={{0,8},{4,12},{8,0},{12,4},{1,9},{5,13},{9,1},{13,5},{2,10},{6,14},... | collective-permute-start | bytes 49160 | tf_op jit(solution)/shard_map/ppermute | solution.py:41
  6.8 1.7 %collective-permute-done.1.b_ref = bf16[8,1024]{1,0:T(8,128)(2,1)S(1)} collective-permute-done((bf16[8,1024]{1,0:T(8,128)(2,1)S(1)}, bf16[8,1024]{1,0:T(8,128)(2,1)S(1)}, u32[]{:S(2)}, u32[]{:S(2)}) %collective-permute-start.1) | collective-permute-done | bytes 16416 | tf_op jit(solution)/shard_map/ppermute | solution.py:41
  8.5 2.1 %collective-permute-start.2 = (bf16[8,1024]{1,0:T(8,128)(2,1)S(1)}, bf16[8,1024]{1,0:T(8,128)(2,1)S(1)}, u32[]{:S(2)}, u32[]{:S(2)}) collective-permute-start(bf16[8,1024]{1,0:T(8,128)(2,1)S(1)} %shard_map.57.a_ref), channel_id=1, source_target_pairs={{0,1},{1,0},{2,3},{3,2},{4,5},{5,4},{6,7},{7,6},{8,9},{9,8},{10,11... | collective-permute-start | bytes 49160 | tf_op jit(solution)/shard_map/ppermute | solution.py:41
  10.6 1.7 %collective-permute-done.2.b_ref = bf16[8,1024]{1,0:T(8,128)(2,1)S(1)} collective-permute-done((bf16[8,1024]{1,0:T(8,128)(2,1)S(1)}, bf16[8,1024]{1,0:T(8,128)(2,1)S(1)}, u32[]{:S(2)}, u32[]{:S(2)}) %collective-permute-start.2) | collective-permute-done | bytes 16416 | tf_op jit(solution)/shard_map/ppermute | solution.py:41
  12.4 3.0 %collective-permute-start.3 = (bf16[16,1024]{1,0:T(8,128)(2,1)S(1)}, bf16[16,1024]{1,0:T(8,128)(2,1)S(1)}, u32[]{:S(2)}, u32[]{:S(2)}) collective-permute-start(bf16[16,1024]{1,0:T(8,128)(2,1)S(1)} %shard_map.58.a_ref.refs_0_), channel_id=1, source_target_pairs={{0,2},{1,3},{2,0},{3,1},{4,6},{5,7},{6,4},{7,5},{8,10},{9,11},{10,... | collective-permute-start | bytes 98312 | tf_op jit(solution)/shard_map/ppermute | solution.py:41
  15.4 1.2 %shard_map.60.turned_ref = bf16[1024,2048]{1,0:T(8,128)(2,1)S(1)} custom-call(bf16[2048,1024]{1,0:T(8,128)(2,1)S(1)} %get-tuple-element.30.basis_ref, bf16[16,1024]{1,0:T(8,128)(2,1)S(1)} %shard_map.58.a_ref.refs_0_), custom_call_target="tpu_custom_call" | custom-call | flops 1150000000 | bytes 65536 | tf_op jit(solution)/shard_map/pallas_call | solution.py:29
  16.6 0.7 %collective-permute-done.3.b_ref = bf16[16,1024]{1,0:T(8,128)(2,1)S(1)} collective-permute-done((bf16[16,1024]{1,0:T(8,128)(2,1)S(1)}, bf16[16,1024]{1,0:T(8,128)(2,1)S(1)}, u32[]{:S(2)}, u32[]{:S(2)}) %collective-permute-start.3) | collective-permute-done | bytes 32800 | tf_op jit(solution)/shard_map/ppermute | solution.py:41
  17.3 0.8 %shard_map.61.x_ref = bf16[32,2048]{1,0:T(8,128)(2,1)S(1)} custom-call(bf16[32,1024]{1,0:T(8,128)(2,1)S(1)} %shard_map.59.codes_ref, bf16[1024,2048]{1,0:T(8,128)(2,1)S(1)} %shard_map.60.turned_ref), custom_call_target="tpu_custom_call" | custom-call | flops 575000000 | bytes 65536 | tf_op jit(solution)/shard_map/pallas_call | solution.py:29
  18.1 0.0 slice-done.8
  18.2 3.0 %shard_map.62 = (f32[32,2048]{1,0:T(8,128)S(1)}, bf16[32,2048]{1,0:T(8,128)(2,1)S(1)}) custom-call(bf16[32,2048]{1,0:T(8,128)(2,1)S(1)} %shard_map.61.x_ref, bf16[2048,4096]{1,0:T(8,128)(2,1)S(1)} %bitcast.3, bf16[2048,4096]{1,0:T(8,128)(2,1)S(1)} %bitcast.5), custom_call_target="tpu_custom_call" | custom-call | flops 3449999872 | bytes 65536 | tf_op jit(solution)/shard_map/pallas_call | solution.py:29
  21.3 1.6 %shard_map.63 = (f32[32,1024]{1,0:T(8,128)S(1)}, bf16[32,1024]{1,0:T(8,128)(2,1)S(1)}) custom-call(bf16[32,2048]{1,0:T(8,128)(2,1)S(1)} %shard_map.61.x_ref, bf16[2048,4096]{1,0:T(8,128)(2,1)S(1)} %bitcast.3, bf16[2048,4096]{1,0:T(8,128)(2,1)S(1)} %bitcast.5, f32[32,2048]{1,0:T(8,128)S(1)} %get-tuple-element.31.refs_0_.a_ref), custom_call_target="tpu_custom_call" | custom-call | flops 1724999936 | bytes 65536 | tf_op jit(solution)/shard_map/pallas_call | solution.py:29
  22.8 0.5 %collective-permute-start.6 = (bf16[32,1024]{1,0:T(8,128)(2,1)S(1)}, bf16[32,1024]{1,0:T(8,128)(2,1)S(1)}, u32[]{:S(2)}, u32[]{:S(2)}) collective-permute-start(bf16[32,1024]{1,0:T(8,128)(2,1)S(1)} %get-tuple-element.37), channel_id=1, source_target_pairs={{0,4},{4,0},{8,12},{12,8},{1,5},{5,1},{9,13},{13,9},{2,6},{6,2},{1... | collective-permute-start | bytes 196616 | tf_op jit(solution)/shard_map/ppermute | solution.py:41
  23.4 0.0 slice-start
  23.4 0.0 slice-start.1
  23.4 1.9 %collective-permute-start.9 = (bf16[32,2048]{1,0:T(8,128)(2,1)S(1)}, bf16[32,2048]{1,0:T(8,128)(2,1)S(1)}, u32[]{:S(2)}, u32[]{:S(2)}) collective-permute-start(bf16[32,2048]{1,0:T(8,128)(2,1)S(1)} %get-tuple-element.34.refs_1_), channel_id=1, source_target_pairs={{0,8},{4,12},{8,0},{12,4},{1,9},{5,13},{9,1},{13,5},{2,10},{6,14},... | collective-permute-start | bytes 393224 | tf_op jit(solution)/shard_map/ppermute | solution.py:41
  25.3 1.6 %shard_map.65 = (f32[32,1024]{1,0:T(8,128)S(1)}, bf16[32,1024]{1,0:T(8,128)(2,1)S(1)}) custom-call(bf16[32,2048]{1,0:T(8,128)(2,1)S(1)} %shard_map.61.x_ref, bf16[2048,4096]{1,0:T(8,128)(2,1)S(1)} %bitcast.3, bf16[2048,4096]{1,0:T(8,128)(2,1)S(1)} %bitcast.5, f32[32,1024]{1,0:T(8,128)S(1)} %get-tuple-element.32.refs_0_.a_ref, ...), custom_call_target="tpu_custom_call" | custom-call | flops 1724999936 | bytes 65536 | tf_op jit(solution)/shard_map/pallas_call | solution.py:29
  26.9 0.0 collective-permute-done.6.b_ref
  26.9 0.0 slice-start.3
  26.9 0.3 collective-permute-start.8
  27.2 0.9 %collective-permute-done.5.b_ref = bf16[32,1024]{1,0:T(8,128)(2,1)S(1)} collective-permute-done((bf16[32,1024]{1,0:T(8,128)(2,1)S(1)}, bf16[32,1024]{1,0:T(8,128)(2,1)S(1)}, u32[]{:S(2)}, u32[]{:S(2)}) %collective-permute-start.5) | collective-permute-done | bytes 65568 | tf_op jit(solution)/shard_map/ppermute | solution.py:41
  28.2 1.0 %collective-permute-start.7 = (bf16[32,1024]{1,0:T(8,128)(2,1)S(1)}, bf16[32,1024]{1,0:T(8,128)(2,1)S(1)}, u32[]{:S(2)}, u32[]{:S(2)}) collective-permute-start(bf16[32,1024]{1,0:T(8,128)(2,1)S(1)} %get-tuple-element.40.refs_0_), channel_id=1, source_target_pairs={{0,8},{4,12},{8,0},{12,4},{1,9},{5,13},{9,1},{13,5},{2,10},{6,14},... | collective-permute-start | bytes 196616 | tf_op jit(solution)/shard_map/ppermute | solution.py:41
  29.1 0.1 shard_map.68.refs_0_
  29.2 0.1 collective-permute-start.12
  29.3 0.2 slice-done.3
  29.5 0.8 %shard_map.69.refs_0_.refs_3_ = f32[32,2048]{1,0:T(8,128)S(1)} custom-call(bf16[32,1024]{1,0:T(8,128)(2,1)S(1)} %shard_map.68.refs_0_, bf16[4096,2048]{1,0:T(8,128)(2,1)S(1)} %bitcast.1), custom_call_target="tpu_custom_call" | custom-call | flops 115000000 | bytes 65536 | tf_op jit(solution)/shard_map/pallas_call | solution.py:29
  30.3 1.6 %collective-permute-done.8.b_ref = bf16[32,1024]{1,0:T(8,128)(2,1)S(1)} collective-permute-done((bf16[32,1024]{1,0:T(8,128)(2,1)S(1)}, bf16[32,1024]{1,0:T(8,128)(2,1)S(1)}, u32[]{:S(2)}, u32[]{:S(2)}) %collective-permute-start.8) | collective-permute-done | bytes 65568 | tf_op jit(solution)/shard_map/ppermute | solution.py:41
  31.9 0.1 collective-permute-start.11
  32.0 0.9 %collective-permute-done.7.b_ref = bf16[32,1024]{1,0:T(8,128)(2,1)S(1)} collective-permute-done((bf16[32,1024]{1,0:T(8,128)(2,1)S(1)}, bf16[32,1024]{1,0:T(8,128)(2,1)S(1)}, u32[]{:S(2)}, u32[]{:S(2)}) %collective-permute-start.7) | collective-permute-done | bytes 65568 | tf_op jit(solution)/shard_map/ppermute | solution.py:41
  32.9 0.1 collective-permute-start.10
  33.0 1.2 %shard_map.72.refs_3_ = f32[32,2048]{1,0:T(8,128)S(1)} custom-call(bf16[32,1024]{1,0:T(8,128)(2,1)S(1)} %collective-permute-done.12.refs_0_, bf16[32,512]{1,0:T(8,128)(2,1)S(1)} %shard_map.70.refs_0_.refs_1_, bf16[4096,2048]{1,0:T(8,128)(2,1)S(1)} %bitcast.1, f32[32,2048]{1,0:T(8,128)S(1)} %shard_map.69.refs_0_.refs_3_), custom_call_target="tpu_custom_call" | custom-call | flops 115000000 | bytes 65536 | tf_op jit(solution)/shard_map/pallas_call | solution.py:29
  34.2 0.0 collective-permute-done.11.refs_0_
  34.3 0.8 %shard_map.73.acc_ref = f32[32,2048]{1,0:T(8,128)S(1)} custom-call(bf16[32,512]{1,0:T(8,128)(2,1)S(1)} %collective-permute-done.11.refs_0_, bf16[32,512]{1,0:T(8,128)(2,1)S(1)} %shard_map.71.refs_1_, bf16[4096,2048]{1,0:T(8,128)(2,1)S(1)} %bitcast.1, f32[32,2048]{1,0:T(8,128)S(1)} %shard_map.72.refs_3_), custom_call_target="tpu_custom_call" | custom-call | flops 115000000 | bytes 65536 | tf_op jit(solution)/shard_map/pallas_call | solution.py:29
  35.1 0.0 collective-permute-done.10.h_ref
  35.1 0.0 copy-done.1
  35.1 1.2 %shard_map.74 = (f32[16,1024]{1,0:T(8,128)S(1)}, bf16[16,1024]{1,0:T(8,128)(2,1)S(1)}) custom-call(bf16[32,512]{1,0:T(8,128)(2,1)S(1)} %collective-permute-done.10.h_ref, bf16[4096,2048]{1,0:T(8,128)(2,1)S(1)} %bitcast.1, f32[32,2048]{1,0:T(8,128)S(1)} %shard_map.73.acc_ref, bf16[2048,1024]{1,0:T(8,128)(2,1)S(1)} %copy-done.1), custom_call_target="tpu_custom_call" | custom-call | flops 1150000000 | bytes 65536 | tf_op jit(solution)/shard_map/pallas_call | solution.py:29
  36.3 2.6 %collective-permute-start.13 = (bf16[16,1024]{1,0:T(8,128)(2,1)S(1)}, bf16[16,1024]{1,0:T(8,128)(2,1)S(1)}, u32[]{:S(2)}, u32[]{:S(2)}) collective-permute-start(bf16[16,1024]{1,0:T(8,128)(2,1)S(1)} %get-tuple-element.44), channel_id=1, source_target_pairs={{0,2},{1,3},{2,0},{3,1},{4,6},{5,7},{6,4},{7,5},{8,10},{9,11},{10,... | collective-permute-start | bytes 98312 | tf_op jit(solution)/shard_map/ppermute | solution.py:41
  38.9 2.2 %collective-permute-done.13.b_ref = bf16[16,1024]{1,0:T(8,128)(2,1)S(1)} collective-permute-done((bf16[16,1024]{1,0:T(8,128)(2,1)S(1)}, bf16[16,1024]{1,0:T(8,128)(2,1)S(1)}, u32[]{:S(2)}, u32[]{:S(2)}) %collective-permute-start.13) | collective-permute-done | bytes 32800 | tf_op jit(solution)/shard_map/ppermute | solution.py:41
  41.2 1.7 %collective-permute-start.14 = (bf16[8,1024]{1,0:T(8,128)(2,1)S(1)}, bf16[8,1024]{1,0:T(8,128)(2,1)S(1)}, u32[]{:S(2)}, u32[]{:S(2)}) collective-permute-start(bf16[8,1024]{1,0:T(8,128)(2,1)S(1)} %get-tuple-element.46), channel_id=1, source_target_pairs={{0,1},{1,0},{2,3},{3,2},{4,5},{5,4},{6,7},{7,6},{8,9},{9,8},{10,11... | collective-permute-start | bytes 49160 | tf_op jit(solution)/shard_map/ppermute | solution.py:41
  42.8 2.1 %collective-permute-done.14.b_ref = bf16[8,1024]{1,0:T(8,128)(2,1)S(1)} collective-permute-done((bf16[8,1024]{1,0:T(8,128)(2,1)S(1)}, bf16[8,1024]{1,0:T(8,128)(2,1)S(1)}, u32[]{:S(2)}, u32[]{:S(2)}) %collective-permute-start.14) | collective-permute-done | bytes 16416 | tf_op jit(solution)/shard_map/ppermute | solution.py:41
  45.0 0.7 %collective-permute-start.15 = (bf16[8,1024]{1,0:T(8,128)(2,1)S(1)}, bf16[8,1024]{1,0:T(8,128)(2,1)S(1)}, u32[]{:S(2)}, u32[]{:S(2)}) collective-permute-start(bf16[8,1024]{1,0:T(8,128)(2,1)S(1)} %get-tuple-element.48), channel_id=1, source_target_pairs={{0,8},{4,12},{8,0},{12,4},{1,9},{5,13},{9,1},{13,5},{2,10},{6,14},... | collective-permute-start | bytes 49160 | tf_op jit(solution)/shard_map/ppermute | solution.py:41
  45.7 3.1 %collective-permute-done.15.b_ref = bf16[8,1024]{1,0:T(8,128)(2,1)S(1)} collective-permute-done((bf16[8,1024]{1,0:T(8,128)(2,1)S(1)}, bf16[8,1024]{1,0:T(8,128)(2,1)S(1)}, u32[]{:S(2)}, u32[]{:S(2)}) %collective-permute-start.15) | collective-permute-done | bytes 16416 | tf_op jit(solution)/shard_map/ppermute | solution.py:41
  48.8 1.2 %collective-permute-done.16.b_ref = f32[8,1024]{1,0:T(8,128)S(1)} collective-permute-done((f32[8,1024]{1,0:T(8,128)S(1)}, f32[8,1024]{1,0:T(8,128)S(1)}, u32[]{:S(2)}, u32[]{:S(2)}) %collective-permute-start.16) | collective-permute-done | bytes 32800 | tf_op jit(solution)/shard_map/ppermute | solution.py:41
  50.0 1.3 %shard_map.78 = bf16[8,2048]{1,0:T(8,128)(2,1)} custom-call(f32[8,1024]{1,0:T(8,128)S(1)} %shard_map.77.a_ref, f32[8,1024]{1,0:T(8,128)S(1)} %collective-permute-done.16.b_ref, bf16[1024,2048]{1,0:T(8,128)(2,1)S(1)} %shard_map.60.turned_ref), custom_call_target="tpu_custom_call" | custom-call | flops 1150000000 | bytes 65536 | tf_op jit(solution)/shard_map/pallas_call | solution.py:29
  (41 shorter events, 0.3 us)
Async XLA Ops:
  2.5 12.9 %copy-start = (bf16[2048,1024]{1,0:T(8,128)(2,1)}, bf16[2048,1024]{1,0:T(8,128)(2,1)S(1)}, u32[]{:S(2)}) copy-start(bf16[2048,1024]{1,0:T(8,128)(2,1)S(1)} %get-tuple-element.30.basis_ref) | copy-start | bytes 12582916
  2.5 15.6 %slice-start.4 = ((s8[16777216]{0:T(1024)(128)(4,1)}), s8[4194304]{0:T(1024)(128)(4,1)S(1)}, s32[]{:S(2)}) async-start(s8[16777216]{0:T(1024)(128)(4,1)} %bitcast.2), calls=%async_computation.4 | async-start | bytes 8388608
  2.5 15.6 %slice-start.8 = ((s8[16777216]{0:T(1024)(128)(4,1)}), s8[4194304]{0:T(1024)(128)(4,1)S(1)}, s32[]{:S(2)}) async-start(s8[16777216]{0:T(1024)(128)(4,1)} %bitcast.4), calls=%async_computation.8 | async-start | bytes 8388608
  2.5 15.6 %slice-start.5 = ((s8[16777216]{0:T(1024)(128)(4,1)}), s8[4194304]{0:T(1024)(128)(4,1)S(1)}, s32[]{:S(2)}) async-start(s8[16777216]{0:T(1024)(128)(4,1)} %bitcast.2), calls=%async_computation.5 | async-start | bytes 8388608
  2.5 15.6 %slice-start.6 = ((s8[16777216]{0:T(1024)(128)(4,1)}), s8[4194304]{0:T(1024)(128)(4,1)S(1)}, s32[]{:S(2)}) async-start(s8[16777216]{0:T(1024)(128)(4,1)} %bitcast.2), calls=%async_computation.6 | async-start | bytes 8388608
  2.5 15.6 %slice-start.7 = ((s8[16777216]{0:T(1024)(128)(4,1)}), s8[4194304]{0:T(1024)(128)(4,1)S(1)}, s32[]{:S(2)}) async-start(s8[16777216]{0:T(1024)(128)(4,1)} %bitcast.2), calls=%async_computation.7 | async-start | bytes 8388608
  2.6 15.6 %slice-start.9 = ((s8[16777216]{0:T(1024)(128)(4,1)}), s8[4194304]{0:T(1024)(128)(4,1)S(1)}, s32[]{:S(2)}) async-start(s8[16777216]{0:T(1024)(128)(4,1)} %bitcast.4), calls=%async_computation.9 | async-start | bytes 8388608
  2.6 15.6 %slice-start.10 = ((s8[16777216]{0:T(1024)(128)(4,1)}), s8[4194304]{0:T(1024)(128)(4,1)S(1)}, s32[]{:S(2)}) async-start(s8[16777216]{0:T(1024)(128)(4,1)} %bitcast.4), calls=%async_computation.10 | async-start | bytes 8388608
  2.6 15.6 %slice-start.11 = ((s8[16777216]{0:T(1024)(128)(4,1)}), s8[4194304]{0:T(1024)(128)(4,1)S(1)}, s32[]{:S(2)}) async-start(s8[16777216]{0:T(1024)(128)(4,1)} %bitcast.4), calls=%async_computation.11 | async-start | bytes 8388608
  2.6 1.4 %collective-permute-start = (f32[8,1024]{1,0:T(8,128)S(1)}, f32[8,1024]{1,0:T(8,128)S(1)}, u32[]{:S(2)}, u32[]{:S(2)}) collective-permute-start(f32[8,1024]{1,0:T(8,128)S(1)} %get-tuple-element.27.a_ref), channel_id=1, source_target_pairs={{0,4},{4,0},{8,12},{12,8},{1,5},{5,1},{9,13},{13,9},{2,6},{6,2},{1... | collective-permute-start | bytes 98312 | tf_op jit(solution)/shard_map/ppermute | solution.py:41
  4.0 4.5 %collective-permute-start.1 = (bf16[8,1024]{1,0:T(8,128)(2,1)S(1)}, bf16[8,1024]{1,0:T(8,128)(2,1)S(1)}, u32[]{:S(2)}, u32[]{:S(2)}) collective-permute-start(bf16[8,1024]{1,0:T(8,128)(2,1)S(1)} %get-tuple-element.29), channel_id=1, source_target_pairs={{0,8},{4,12},{8,0},{12,4},{1,9},{5,13},{9,1},{13,5},{2,10},{6,14},... | collective-permute-start | bytes 49160 | tf_op jit(solution)/shard_map/ppermute | solution.py:41
  8.5 3.8 %collective-permute-start.2 = (bf16[8,1024]{1,0:T(8,128)(2,1)S(1)}, bf16[8,1024]{1,0:T(8,128)(2,1)S(1)}, u32[]{:S(2)}, u32[]{:S(2)}) collective-permute-start(bf16[8,1024]{1,0:T(8,128)(2,1)S(1)} %shard_map.57.a_ref), channel_id=1, source_target_pairs={{0,1},{1,0},{2,3},{3,2},{4,5},{5,4},{6,7},{7,6},{8,9},{9,8},{10,11... | collective-permute-start | bytes 49160 | tf_op jit(solution)/shard_map/ppermute | solution.py:41
  12.4 4.9 %collective-permute-start.3 = (bf16[16,1024]{1,0:T(8,128)(2,1)S(1)}, bf16[16,1024]{1,0:T(8,128)(2,1)S(1)}, u32[]{:S(2)}, u32[]{:S(2)}) collective-permute-start(bf16[16,1024]{1,0:T(8,128)(2,1)S(1)} %shard_map.58.a_ref.refs_0_), channel_id=1, source_target_pairs={{0,2},{1,3},{2,0},{3,1},{4,6},{5,7},{6,4},{7,5},{8,10},{9,11},{10,... | collective-permute-start | bytes 98312 | tf_op jit(solution)/shard_map/ppermute | solution.py:41
  21.2 2.1 %collective-permute-start.4 = (bf16[32,2048]{1,0:T(8,128)(2,1)S(1)}, bf16[32,2048]{1,0:T(8,128)(2,1)S(1)}, u32[]{:S(2)}, u32[]{:S(2)}) collective-permute-start(bf16[32,2048]{1,0:T(8,128)(2,1)S(1)} %get-tuple-element.33), channel_id=1, source_target_pairs={{0,4},{4,0},{8,12},{12,8},{1,5},{5,1},{9,13},{13,9},{2,6},{6,2},{1... | collective-permute-start | bytes 393224 | tf_op jit(solution)/shard_map/ppermute | solution.py:41
  22.8 4.1 %collective-permute-start.6 = (bf16[32,1024]{1,0:T(8,128)(2,1)S(1)}, bf16[32,1024]{1,0:T(8,128)(2,1)S(1)}, u32[]{:S(2)}, u32[]{:S(2)}) collective-permute-start(bf16[32,1024]{1,0:T(8,128)(2,1)S(1)} %get-tuple-element.37), channel_id=1, source_target_pairs={{0,4},{4,0},{8,12},{12,8},{1,5},{5,1},{9,13},{13,9},{2,6},{6,2},{1... | collective-permute-start | bytes 196616 | tf_op jit(solution)/shard_map/ppermute | solution.py:41
  23.4 5.9 %slice-start = ((s8[16777216]{0:T(1024)(128)(4,1)}), s8[4194304]{0:T(1024)(128)(4,1)S(1)}, s32[]{:S(2)}) async-start(s8[16777216]{0:T(1024)(128)(4,1)} %bitcast), calls=%async_computation | async-start | bytes 8388608
  23.4 5.9 %slice-start.1 = ((s8[16777216]{0:T(1024)(128)(4,1)}), s8[4194304]{0:T(1024)(128)(4,1)S(1)}, s32[]{:S(2)}) async-start(s8[16777216]{0:T(1024)(128)(4,1)} %bitcast), calls=%async_computation.1 | async-start | bytes 8388608
  23.4 5.9 %slice-start.2 = ((s8[16777216]{0:T(1024)(128)(4,1)}), s8[4194304]{0:T(1024)(128)(4,1)S(1)}, s32[]{:S(2)}) async-start(s8[16777216]{0:T(1024)(128)(4,1)} %bitcast), calls=%async_computation.2 | async-start | bytes 8388608
  23.4 5.7 %collective-permute-start.9 = (bf16[32,2048]{1,0:T(8,128)(2,1)S(1)}, bf16[32,2048]{1,0:T(8,128)(2,1)S(1)}, u32[]{:S(2)}, u32[]{:S(2)}) collective-permute-start(bf16[32,2048]{1,0:T(8,128)(2,1)S(1)} %get-tuple-element.34.refs_1_), channel_id=1, source_target_pairs={{0,8},{4,12},{8,0},{12,4},{1,9},{5,13},{9,1},{13,5},{2,10},{6,14},... | collective-permute-start | bytes 393224 | tf_op jit(solution)/shard_map/ppermute | solution.py:41
  26.9 1.3 %collective-permute-start.5 = (bf16[32,1024]{1,0:T(8,128)(2,1)S(1)}, bf16[32,1024]{1,0:T(8,128)(2,1)S(1)}, u32[]{:S(2)}, u32[]{:S(2)}) collective-permute-start(bf16[32,1024]{1,0:T(8,128)(2,1)S(1)} %get-tuple-element.36), channel_id=1, source_target_pairs={{0,4},{4,0},{8,12},{12,8},{1,5},{5,1},{9,13},{13,9},{2,6},{6,2},{1... | collective-permute-start | bytes 196616 | tf_op jit(solution)/shard_map/ppermute | solution.py:41
  26.9 2.6 %slice-start.3 = ((s8[16777216]{0:T(1024)(128)(4,1)}), s8[4194304]{0:T(1024)(128)(4,1)S(1)}, s32[]{:S(2)}) async-start(s8[16777216]{0:T(1024)(128)(4,1)} %bitcast), calls=%async_computation.3 | async-start | bytes 8388608
  26.9 5.0 %collective-permute-start.8 = (bf16[32,1024]{1,0:T(8,128)(2,1)S(1)}, bf16[32,1024]{1,0:T(8,128)(2,1)S(1)}, u32[]{:S(2)}, u32[]{:S(2)}) collective-permute-start(bf16[32,1024]{1,0:T(8,128)(2,1)S(1)} %get-tuple-element.38.refs_0_), channel_id=1, source_target_pairs={{0,8},{4,12},{8,0},{12,4},{1,9},{5,13},{9,1},{13,5},{2,10},{6,14},... | collective-permute-start | bytes 196616 | tf_op jit(solution)/shard_map/ppermute | solution.py:41
  28.2 4.7 %collective-permute-start.7 = (bf16[32,1024]{1,0:T(8,128)(2,1)S(1)}, bf16[32,1024]{1,0:T(8,128)(2,1)S(1)}, u32[]{:S(2)}, u32[]{:S(2)}) collective-permute-start(bf16[32,1024]{1,0:T(8,128)(2,1)S(1)} %get-tuple-element.40.refs_0_), channel_id=1, source_target_pairs={{0,8},{4,12},{8,0},{12,4},{1,9},{5,13},{9,1},{13,5},{2,10},{6,14},... | collective-permute-start | bytes 196616 | tf_op jit(solution)/shard_map/ppermute | solution.py:41
  29.2 3.8 %collective-permute-start.12 = (bf16[32,1024]{1,0:T(8,128)(2,1)S(1)}, bf16[32,1024]{1,0:T(8,128)(2,1)S(1)}, u32[]{:S(2)}, u32[]{:S(2)}) collective-permute-start(bf16[32,1024]{1,0:T(8,128)(2,1)S(1)} %shard_map.68.refs_0_), channel_id=1, source_target_pairs={{0,4},{4,0},{8,12},{12,8},{1,5},{5,1},{9,13},{13,9},{2,6},{6,2},{1... | collective-permute-start | bytes 196616 | tf_op jit(solution)/shard_map/ppermute | solution.py:41
  31.9 2.3 %collective-permute-start.11 = (bf16[32,512]{1,0:T(8,128)(2,1)S(1)}, bf16[32,512]{1,0:T(8,128)(2,1)S(1)}, u32[]{:S(2)}, u32[]{:S(2)}) collective-permute-start(bf16[32,512]{1,0:T(8,128)(2,1)S(1)} %shard_map.70.refs_0_.refs_1_), channel_id=1, source_target_pairs={{0,4},{4,0},{8,12},{12,8},{1,5},{5,1},{9,13},{13,9},{2,6},{6,2},{1... | collective-permute-start | bytes 98312 | tf_op jit(solution)/shard_map/ppermute | solution.py:41
  32.9 2.2 %copy-start.1 = (bf16[2048,1024]{1,0:T(8,128)(2,1)S(1)}, bf16[2048,1024]{1,0:T(8,128)(2,1)}, u32[]{:S(2)}) copy-start(bf16[2048,1024]{1,0:T(8,128)(2,1)} %copy-done) | copy-start | bytes 12582916
  32.9 2.1 %collective-permute-start.10 = (bf16[32,512]{1,0:T(8,128)(2,1)S(1)}, bf16[32,512]{1,0:T(8,128)(2,1)S(1)}, u32[]{:S(2)}, u32[]{:S(2)}) collective-permute-start(bf16[32,512]{1,0:T(8,128)(2,1)S(1)} %shard_map.71.refs_1_), channel_id=1, source_target_pairs={{0,4},{4,0},{8,12},{12,8},{1,5},{5,1},{9,13},{13,9},{2,6},{6,2},{1... | collective-permute-start | bytes 98312 | tf_op jit(solution)/shard_map/ppermute | solution.py:41
  36.3 4.8 %collective-permute-start.13 = (bf16[16,1024]{1,0:T(8,128)(2,1)S(1)}, bf16[16,1024]{1,0:T(8,128)(2,1)S(1)}, u32[]{:S(2)}, u32[]{:S(2)}) collective-permute-start(bf16[16,1024]{1,0:T(8,128)(2,1)S(1)} %get-tuple-element.44), channel_id=1, source_target_pairs={{0,2},{1,3},{2,0},{3,1},{4,6},{5,7},{6,4},{7,5},{8,10},{9,11},{10,... | collective-permute-start | bytes 98312 | tf_op jit(solution)/shard_map/ppermute | solution.py:41
  41.2 3.8 %collective-permute-start.14 = (bf16[8,1024]{1,0:T(8,128)(2,1)S(1)}, bf16[8,1024]{1,0:T(8,128)(2,1)S(1)}, u32[]{:S(2)}, u32[]{:S(2)}) collective-permute-start(bf16[8,1024]{1,0:T(8,128)(2,1)S(1)} %get-tuple-element.46), channel_id=1, source_target_pairs={{0,1},{1,0},{2,3},{3,2},{4,5},{5,4},{6,7},{7,6},{8,9},{9,8},{10,11... | collective-permute-start | bytes 49160 | tf_op jit(solution)/shard_map/ppermute | solution.py:41
  45.0 3.8 %collective-permute-start.15 = (bf16[8,1024]{1,0:T(8,128)(2,1)S(1)}, bf16[8,1024]{1,0:T(8,128)(2,1)S(1)}, u32[]{:S(2)}, u32[]{:S(2)}) collective-permute-start(bf16[8,1024]{1,0:T(8,128)(2,1)S(1)} %get-tuple-element.48), channel_id=1, source_target_pairs={{0,8},{4,12},{8,0},{12,4},{1,9},{5,13},{9,1},{13,5},{2,10},{6,14},... | collective-permute-start | bytes 49160 | tf_op jit(solution)/shard_map/ppermute | solution.py:41
  48.8 1.2 %collective-permute-start.16 = (f32[8,1024]{1,0:T(8,128)S(1)}, f32[8,1024]{1,0:T(8,128)S(1)}, u32[]{:S(2)}, u32[]{:S(2)}) collective-permute-start(f32[8,1024]{1,0:T(8,128)S(1)} %shard_map.77.a_ref), channel_id=1, source_target_pairs={{0,4},{4,0},{8,12},{12,8},{1,5},{5,1},{9,13},{13,9},{2,6},{6,2},{1... | collective-permute-start | bytes 98312 | tf_op jit(solution)/shard_map/ppermute | solution.py:41

commit v6 on v5

--- a/solution.py
+++ b/solution.py
@@ -12,13 +12,13 @@
 F32 = jnp.float32
 BF16 = jnp.bfloat16
 LIMIT = 2 * 1024 * 1024
-PIECES = 4
+PIECES = 8
 WAIT = 30
 TURN = 1
-SUMS = (0.1, 1, 0.1)
-PAIRS = (3, 1.5, 1.5)
-HIDDEN = (2, 0.1, 0.1)
-DOWN = (0.1, 0.1, 0.1)
+SUMS = (0.1, 1, 0.1, 0.1)
+PAIRS = (3, 1.5, 1.5, 0.1)
+HIDDEN = (2, 0.1, 0.1, 0.1)
+DOWN = (0.1, 0.1, 0.1, 0.1)
 VMEM = pl.BlockSpec(memory_space=pltpu.VMEM)
 HBM = pl.BlockSpec(memory_space=pltpu.HBM)
 sds = jax.ShapeDtypeStruct
@@ -195,7 +195,7 @@
         mask *= 2
     restored = call(restore_body, sds((rows, width), BF16), 0.5, codes, turned)
 
-    shares = SHARES if ff % 1024 == 0 else (1, 1)
+    shares = SHARES if ff % (256 * sum(SHARES)) == 0 else (1, 1)
     spans, at = [], 0
     for share in shares:
         spans.append((at, ff * share // sum(shares)))
@@ -216,15 +216,15 @@
         pairs.append((keep, swap(send, "dp", 1, dp)))
         if q > 0:
             sums.append(call(add_two_body, both((rows, spans[q - 1][1])), SUMS[q - 1], *pairs[q - 1], keep))
-    sums.append(call(add_two_body, both((rows, spans[-1][1])), SUMS[-1], *pairs[-1], sums[-1][1]))
-    acc, early, own, late = None, None, None, []
+    sums.append(call(add_two_body, both((rows, spans[-1][1])), SUMS[len(spans) - 1], *pairs[-1], sums[-1][1]))
+    acc, late = None, []
     for q, ((start, span), (total, send)) in enumerate(zip(spans, sums)):
         mask = 2
         while 2 * mask < dp:
             total, send = call(add_two_body, both(total.shape), 0.1, total, swap(send, "dp", mask, dp))
             mask *= 2
         half = span // 2
-        order = [sums[-1][1]] if q == 0 else [early] if q == 1 else [own]
+        order = [sums[-1][1]] if q == 0 else [acc]
         own = call(hidden_body, sds((rows, half), BF16), HIDDEN[q], total, swap(send, "dp", mask, dp), *order)
         away = swap(own, "dp", 1, dp)
         blocks = late + [(own, (0, start, half))]
@@ -232,7 +232,6 @@
         acc = call(
             body, sds((rows, width), F32), DOWN[q], *[h for h, _ in blocks], down_weight, *([] if acc is None else [acc])
         )
-        early = acc if early is None else early
         late = [(away, (1, start, half))]
     ((away, part),) = late
     codes, send = call(
@@ -262,7 +261,7 @@
     return call(final_body, sds((local, width), BF16), 1, codes, swap(codes, "dp", 1, dp), turned)
 
 
-SHARES = (2, 1, 1)
+SHARES = (3, 3, 2)
 
 
 def solution(mesh):

time: 51.4 us -> 51.8 us (level)
  transfers between devices with their start and end apart: 17 -> 17, of which waited for: 11 -> 10; matrix products, arithmetic and copies ran while one was open for 0% -> 0% of each run, Pallas kernels for 14% -> 16%
where the time goes in v6:
time: 51.8 us; the launch traced here: 51.6 us
  waiting for transfers between devices  17.5 us (34%)
  starting transfers between devices  17.3 us (33%)
  Pallas kernels  16.2 us (31%)
    ppermute x17, waiting for transfers between devices, swap(): return lax.ppermute(value, axis, [(i, i ^ mask) for i in range(size)])  17.5 us
    ppermute x17, starting transfers between devices, swap(): return lax.ppermute(value, axis, [(i, i ^ mask) for i in range(size)])  17.3 us
    pallas_call x24, Pallas kernels, call(): pl.pallas_call(body, out_shape=out, in_specs=[HBM if i in fixed else VMEM...  16.2 us
  transfers between devices with their start and end apart: 17, of which 10 were waited for; matrix products, arithmetic and copies ran while one was open for 0% of the time, Pallas kernels for 16%

profile of v6, /device:TPU:0, one launch (start us, length us, event | category | flops | bytes accessed | tf_op | source)
XLA Modules:
  0.0 51.6 jit_solution(9724683581221865000)
XLA Ops:
  0.0 2.4 %shard_map.55 = (f32[8,1024]{1,0:T(8,128)S(1)}, bf16[2048,1024]{1,0:T(8,128)(2,1)S(1)}) custom-call(bf16[8,2048]{1,0:T(8,128)(2,1)} %x_ref.1, bf16[2048,1024]{1,0:T(8,128)(2,1)} %basis_ref.1), custom_call_target="tpu_custom_call" | custom-call | flops 1150000000 | bytes 65536 | tf_op jit(solution)/shard_map/pallas_call | solution.py:29
  2.4 0.0 slice-start.4
  2.5 0.0 slice-start.8
  2.5 0.5 %collective-permute-start = (f32[8,1024]{1,0:T(8,128)S(1)}, f32[8,1024]{1,0:T(8,128)S(1)}, u32[]{:S(2)}, u32[]{:S(2)}) collective-permute-start(f32[8,1024]{1,0:T(8,128)S(1)} %get-tuple-element.27.a_ref), channel_id=1, source_target_pairs={{0,4},{4,0},{8,12},{12,8},{1,5},{5,1},{9,13},{13,9},{2,6},{6,2},{1... | collective-permute-start | bytes 98312 | tf_op jit(solution)/shard_map/ppermute | solution.py:41
  3.1 0.9 %collective-permute-done.b_ref = f32[8,1024]{1,0:T(8,128)S(1)} collective-permute-done((f32[8,1024]{1,0:T(8,128)S(1)}, f32[8,1024]{1,0:T(8,128)S(1)}, u32[]{:S(2)}, u32[]{:S(2)}) %collective-permute-start) | collective-permute-done | bytes 32800 | tf_op jit(solution)/shard_map/ppermute | solution.py:41
  3.9 2.8 %collective-permute-start.1 = (bf16[8,1024]{1,0:T(8,128)(2,1)S(1)}, bf16[8,1024]{1,0:T(8,128)(2,1)S(1)}, u32[]{:S(2)}, u32[]{:S(2)}) collective-permute-start(bf16[8,1024]{1,0:T(8,128)(2,1)S(1)} %get-tuple-element.29), channel_id=1, source_target_pairs={{0,8},{4,12},{8,0},{12,4},{1,9},{5,13},{9,1},{13,5},{2,10},{6,14},... | collective-permute-start | bytes 49160 | tf_op jit(solution)/shard_map/ppermute | solution.py:41
  6.8 1.7 %collective-permute-done.1.b_ref = bf16[8,1024]{1,0:T(8,128)(2,1)S(1)} collective-permute-done((bf16[8,1024]{1,0:T(8,128)(2,1)S(1)}, bf16[8,1024]{1,0:T(8,128)(2,1)S(1)}, u32[]{:S(2)}, u32[]{:S(2)}) %collective-permute-start.1) | collective-permute-done | bytes 16416 | tf_op jit(solution)/shard_map/ppermute | solution.py:41
  8.5 2.1 %collective-permute-start.2 = (bf16[8,1024]{1,0:T(8,128)(2,1)S(1)}, bf16[8,1024]{1,0:T(8,128)(2,1)S(1)}, u32[]{:S(2)}, u32[]{:S(2)}) collective-permute-start(bf16[8,1024]{1,0:T(8,128)(2,1)S(1)} %shard_map.57.a_ref), channel_id=1, source_target_pairs={{0,1},{1,0},{2,3},{3,2},{4,5},{5,4},{6,7},{7,6},{8,9},{9,8},{10,11... | collective-permute-start | bytes 49160 | tf_op jit(solution)/shard_map/ppermute | solution.py:41
  10.6 1.7 %collective-permute-done.2.b_ref = bf16[8,1024]{1,0:T(8,128)(2,1)S(1)} collective-permute-done((bf16[8,1024]{1,0:T(8,128)(2,1)S(1)}, bf16[8,1024]{1,0:T(8,128)(2,1)S(1)}, u32[]{:S(2)}, u32[]{:S(2)}) %collective-permute-start.2) | collective-permute-done | bytes 16416 | tf_op jit(solution)/shard_map/ppermute | solution.py:41
  12.3 3.0 %collective-permute-start.3 = (bf16[16,1024]{1,0:T(8,128)(2,1)S(1)}, bf16[16,1024]{1,0:T(8,128)(2,1)S(1)}, u32[]{:S(2)}, u32[]{:S(2)}) collective-permute-start(bf16[16,1024]{1,0:T(8,128)(2,1)S(1)} %shard_map.58.a_ref.refs_0_), channel_id=1, source_target_pairs={{0,2},{1,3},{2,0},{3,1},{4,6},{5,7},{6,4},{7,5},{8,10},{9,11},{10,... | collective-permute-start | bytes 98312 | tf_op jit(solution)/shard_map/ppermute | solution.py:41
  15.3 1.2 %shard_map.60.turned_ref = bf16[1024,2048]{1,0:T(8,128)(2,1)S(1)} custom-call(bf16[2048,1024]{1,0:T(8,128)(2,1)S(1)} %get-tuple-element.30.basis_ref, bf16[16,1024]{1,0:T(8,128)(2,1)S(1)} %shard_map.58.a_ref.refs_0_), custom_call_target="tpu_custom_call" | custom-call | flops 1150000000 | bytes 65536 | tf_op jit(solution)/shard_map/pallas_call | solution.py:29
  16.6 0.7 %collective-permute-done.3.b_ref = bf16[16,1024]{1,0:T(8,128)(2,1)S(1)} collective-permute-done((bf16[16,1024]{1,0:T(8,128)(2,1)S(1)}, bf16[16,1024]{1,0:T(8,128)(2,1)S(1)}, u32[]{:S(2)}, u32[]{:S(2)}) %collective-permute-start.3) | collective-permute-done | bytes 32800 | tf_op jit(solution)/shard_map/ppermute | solution.py:41
  17.2 0.8 %shard_map.61.x_ref = bf16[32,2048]{1,0:T(8,128)(2,1)S(1)} custom-call(bf16[32,1024]{1,0:T(8,128)(2,1)S(1)} %shard_map.59.codes_ref, bf16[1024,2048]{1,0:T(8,128)(2,1)S(1)} %shard_map.60.turned_ref), custom_call_target="tpu_custom_call" | custom-call | flops 575000000 | bytes 65536 | tf_op jit(solution)/shard_map/pallas_call | solution.py:29
  18.1 0.0 slice-done.8
  18.2 2.3 %shard_map.62 = (f32[32,1536]{1,0:T(8,128)S(1)}, bf16[32,1536]{1,0:T(8,128)(2,1)S(1)}) custom-call(bf16[32,2048]{1,0:T(8,128)(2,1)S(1)} %shard_map.61.x_ref, bf16[2048,4096]{1,0:T(8,128)(2,1)S(1)} %bitcast.3, bf16[2048,4096]{1,0:T(8,128)(2,1)S(1)} %bitcast.5), custom_call_target="tpu_custom_call" | custom-call | flops 3449999872 | bytes 65536 | tf_op jit(solution)/shard_map/pallas_call | solution.py:29
  20.5 0.0 collective-permute-start.4
  20.5 2.3 %shard_map.63 = (f32[32,1536]{1,0:T(8,128)S(1)}, bf16[32,1536]{1,0:T(8,128)(2,1)S(1)}) custom-call(bf16[32,2048]{1,0:T(8,128)(2,1)S(1)} %shard_map.61.x_ref, bf16[2048,4096]{1,0:T(8,128)(2,1)S(1)} %bitcast.3, bf16[2048,4096]{1,0:T(8,128)(2,1)S(1)} %bitcast.5, f32[32,1536]{1,0:T(8,128)S(1)} %get-tuple-element.31.refs_0_.a_ref), custom_call_target="tpu_custom_call" | custom-call | flops 1724999936 | bytes 65536 | tf_op jit(solution)/shard_map/pallas_call | solution.py:29
  22.8 0.5 collective-permute-start.6
  23.3 0.0 slice-start
  23.3 0.0 slice-start.1
  23.3 1.9 %collective-permute-start.8 = (bf16[32,1536]{1,0:T(8,128)(2,1)S(1)}, bf16[32,1536]{1,0:T(8,128)(2,1)S(1)}, u32[]{:S(2)}, u32[]{:S(2)}) collective-permute-start(bf16[32,1536]{1,0:T(8,128)(2,1)S(1)} %get-tuple-element.34.refs_1_), channel_id=1, source_target_pairs={{0,8},{4,12},{8,0},{12,4},{1,9},{5,13},{9,1},{13,5},{2,10},{6,14},... | collective-permute-start | bytes 294920 | tf_op jit(solution)/shard_map/ppermute | solution.py:41
  25.2 1.6 %shard_map.65 = (f32[32,1024]{1,0:T(8,128)S(1)}, bf16[32,1024]{1,0:T(8,128)(2,1)S(1)}) custom-call(bf16[32,2048]{1,0:T(8,128)(2,1)S(1)} %shard_map.61.x_ref, bf16[2048,4096]{1,0:T(8,128)(2,1)S(1)} %bitcast.3, bf16[2048,4096]{1,0:T(8,128)(2,1)S(1)} %bitcast.5, f32[32,1536]{1,0:T(8,128)S(1)} %get-tuple-element.32.refs_0_.a_ref, ...), custom_call_target="tpu_custom_call" | custom-call | flops 1724999936 | bytes 65536 | tf_op jit(solution)/shard_map/pallas_call | solution.py:29
  26.8 0.0 collective-permute-done.6.b_ref
  26.8 0.0 slice-start.3
  26.9 0.3 collective-permute-start.10
  27.1 0.9 %collective-permute-done.5.b_ref = bf16[32,1024]{1,0:T(8,128)(2,1)S(1)} collective-permute-done((bf16[32,1024]{1,0:T(8,128)(2,1)S(1)}, bf16[32,1024]{1,0:T(8,128)(2,1)S(1)}, u32[]{:S(2)}, u32[]{:S(2)}) %collective-permute-start.5) | collective-permute-done | bytes 65568 | tf_op jit(solution)/shard_map/ppermute | solution.py:41
  28.1 1.0 %collective-permute-start.7 = (bf16[32,1024]{1,0:T(8,128)(2,1)S(1)}, bf16[32,1024]{1,0:T(8,128)(2,1)S(1)}, u32[]{:S(2)}, u32[]{:S(2)}) collective-permute-start(bf16[32,1024]{1,0:T(8,128)(2,1)S(1)} %get-tuple-element.40.refs_0_), channel_id=1, source_target_pairs={{0,8},{4,12},{8,0},{12,4},{1,9},{5,13},{9,1},{13,5},{2,10},{6,14},... | collective-permute-start | bytes 196616 | tf_op jit(solution)/shard_map/ppermute | solution.py:41
  29.0 0.1 shard_map.68.refs_0_
  29.1 0.1 collective-permute-start.9
  29.2 0.2 slice-done.3
  29.4 0.6 %shard_map.69.refs_0_.refs_3_ = f32[32,2048]{1,0:T(8,128)S(1)} custom-call(bf16[32,768]{1,0:T(8,128)(2,1)S(1)} %shard_map.68.refs_0_, bf16[4096,2048]{1,0:T(8,128)(2,1)S(1)} %bitcast.1), custom_call_target="tpu_custom_call" | custom-call | flops 115000000 | bytes 65536 | tf_op jit(solution)/shard_map/pallas_call | solution.py:29
  30.0 2.5 %collective-permute-done.10.b_ref = bf16[32,1536]{1,0:T(8,128)(2,1)S(1)} collective-permute-done((bf16[32,1536]{1,0:T(8,128)(2,1)S(1)}, bf16[32,1536]{1,0:T(8,128)(2,1)S(1)}, u32[]{:S(2)}, u32[]{:S(2)}) %collective-permute-start.10) | collective-permute-done | bytes 98336 | tf_op jit(solution)/shard_map/ppermute | solution.py:41
  32.5 0.1 shard_map.70.refs_1_
  32.6 0.1 collective-permute-start.12
  32.7 1.2 %shard_map.71.refs_0_.refs_3_ = f32[32,2048]{1,0:T(8,128)S(1)} custom-call(bf16[32,768]{1,0:T(8,128)(2,1)S(1)} %collective-permute-done.9.refs_0_, bf16[32,768]{1,0:T(8,128)(2,1)S(1)} %shard_map.70.refs_1_, bf16[4096,2048]{1,0:T(8,128)(2,1)S(1)} %bitcast.1, f32[32,2048]{1,0:T(8,128)S(1)} %shard_map.69.refs_0_.refs_3_), custom_call_target="tpu_custom_call" | custom-call | flops 115000000 | bytes 65536 | tf_op jit(solution)/shard_map/pallas_call | solution.py:29
  33.9 0.0 collective-permute-done.7.b_ref
  33.9 0.5 %collective-permute-start.11 = (bf16[32,512]{1,0:T(8,128)(2,1)S(1)}, bf16[32,512]{1,0:T(8,128)(2,1)S(1)}, u32[]{:S(2)}, u32[]{:S(2)}) collective-permute-start(bf16[32,512]{1,0:T(8,128)(2,1)S(1)} %shard_map.72.refs_1_), channel_id=1, source_target_pairs={{0,4},{4,0},{8,12},{12,8},{1,5},{5,1},{9,13},{13,9},{2,6},{6,2},{1... | collective-permute-start | bytes 98312 | tf_op jit(solution)/shard_map/ppermute | solution.py:41
  34.5 1.0 %shard_map.73.acc_ref = f32[32,2048]{1,0:T(8,128)S(1)} custom-call(bf16[32,768]{1,0:T(8,128)(2,1)S(1)} %collective-permute-done.12.refs_0_, bf16[32,512]{1,0:T(8,128)(2,1)S(1)} %shard_map.72.refs_1_, bf16[4096,2048]{1,0:T(8,128)(2,1)S(1)} %bitcast.1, f32[32,2048]{1,0:T(8,128)S(1)} %shard_map.71.refs_0_.refs_3_), custom_call_target="tpu_custom_call" | custom-call | flops 115000000 | bytes 65536 | tf_op jit(solution)/shard_map/pallas_call | solution.py:29
  35.5 0.0 collective-permute-done.11.h_ref
  35.5 1.2 %shard_map.74 = (f32[16,1024]{1,0:T(8,128)S(1)}, bf16[16,1024]{1,0:T(8,128)(2,1)S(1)}) custom-call(bf16[32,512]{1,0:T(8,128)(2,1)S(1)} %collective-permute-done.11.h_ref, bf16[4096,2048]{1,0:T(8,128)(2,1)S(1)} %bitcast.1, f32[32,2048]{1,0:T(8,128)S(1)} %shard_map.73.acc_ref, bf16[2048,1024]{1,0:T(8,128)(2,1)S(1)} %copy-done.1), custom_call_target="tpu_custom_call" | custom-call | flops 1150000000 | bytes 65536 | tf_op jit(solution)/shard_map/pallas_call | solution.py:29
  36.7 2.6 %collective-permute-start.13 = (bf16[16,1024]{1,0:T(8,128)(2,1)S(1)}, bf16[16,1024]{1,0:T(8,128)(2,1)S(1)}, u32[]{:S(2)}, u32[]{:S(2)}) collective-permute-start(bf16[16,1024]{1,0:T(8,128)(2,1)S(1)} %get-tuple-element.44), channel_id=1, source_target_pairs={{0,2},{1,3},{2,0},{3,1},{4,6},{5,7},{6,4},{7,5},{8,10},{9,11},{10,... | collective-permute-start | bytes 98312 | tf_op jit(solution)/shard_map/ppermute | solution.py:41
  39.3 2.2 %collective-permute-done.13.b_ref = bf16[16,1024]{1,0:T(8,128)(2,1)S(1)} collective-permute-done((bf16[16,1024]{1,0:T(8,128)(2,1)S(1)}, bf16[16,1024]{1,0:T(8,128)(2,1)S(1)}, u32[]{:S(2)}, u32[]{:S(2)}) %collective-permute-start.13) | collective-permute-done | bytes 32800 | tf_op jit(solution)/shard_map/ppermute | solution.py:41
  41.5 1.6 %collective-permute-start.14 = (bf16[8,1024]{1,0:T(8,128)(2,1)S(1)}, bf16[8,1024]{1,0:T(8,128)(2,1)S(1)}, u32[]{:S(2)}, u32[]{:S(2)}) collective-permute-start(bf16[8,1024]{1,0:T(8,128)(2,1)S(1)} %get-tuple-element.46), channel_id=1, source_target_pairs={{0,1},{1,0},{2,3},{3,2},{4,5},{5,4},{6,7},{7,6},{8,9},{9,8},{10,11... | collective-permute-start | bytes 49160 | tf_op jit(solution)/shard_map/ppermute | solution.py:41
  43.2 2.2 %collective-permute-done.14.b_ref = bf16[8,1024]{1,0:T(8,128)(2,1)S(1)} collective-permute-done((bf16[8,1024]{1,0:T(8,128)(2,1)S(1)}, bf16[8,1024]{1,0:T(8,128)(2,1)S(1)}, u32[]{:S(2)}, u32[]{:S(2)}) %collective-permute-start.14) | collective-permute-done | bytes 16416 | tf_op jit(solution)/shard_map/ppermute | solution.py:41
  45.3 0.3 collective-permute-start.15
  45.6 3.5 %collective-permute-done.15.b_ref = bf16[8,1024]{1,0:T(8,128)(2,1)S(1)} collective-permute-done((bf16[8,1024]{1,0:T(8,128)(2,1)S(1)}, bf16[8,1024]{1,0:T(8,128)(2,1)S(1)}, u32[]{:S(2)}, u32[]{:S(2)}) %collective-permute-start.15) | collective-permute-done | bytes 16416 | tf_op jit(solution)/shard_map/ppermute | solution.py:41
  49.2 1.2 %collective-permute-done.16.b_ref = f32[8,1024]{1,0:T(8,128)S(1)} collective-permute-done((f32[8,1024]{1,0:T(8,128)S(1)}, f32[8,1024]{1,0:T(8,128)S(1)}, u32[]{:S(2)}, u32[]{:S(2)}) %collective-permute-start.16) | collective-permute-done | bytes 32800 | tf_op jit(solution)/shard_map/ppermute | solution.py:41
  50.4 1.3 %shard_map.78 = bf16[8,2048]{1,0:T(8,128)(2,1)} custom-call(f32[8,1024]{1,0:T(8,128)S(1)} %shard_map.77.a_ref, f32[8,1024]{1,0:T(8,128)S(1)} %collective-permute-done.16.b_ref, bf16[1024,2048]{1,0:T(8,128)(2,1)S(1)} %shard_map.60.turned_ref), custom_call_target="tpu_custom_call" | custom-call | flops 1150000000 | bytes 65536 | tf_op jit(solution)/shard_map/pallas_call | solution.py:29
  (41 shorter events, 0.2 us)
Async XLA Ops:
  2.4 12.9 %copy-start = (bf16[2048,1024]{1,0:T(8,128)(2,1)}, bf16[2048,1024]{1,0:T(8,128)(2,1)S(1)}, u32[]{:S(2)}) copy-start(bf16[2048,1024]{1,0:T(8,128)(2,1)S(1)} %get-tuple-element.30.basis_ref) | copy-start | bytes 12582916
  2.4 15.6 %slice-start.4 = ((s8[16777216]{0:T(1024)(128)(4,1)}), s8[4194304]{0:T(1024)(128)(4,1)S(1)}, s32[]{:S(2)}) async-start(s8[16777216]{0:T(1024)(128)(4,1)} %bitcast.2), calls=%async_computation.4 | async-start | bytes 8388608
  2.5 15.6 %slice-start.8 = ((s8[16777216]{0:T(1024)(128)(4,1)}), s8[4194304]{0:T(1024)(128)(4,1)S(1)}, s32[]{:S(2)}) async-start(s8[16777216]{0:T(1024)(128)(4,1)} %bitcast.4), calls=%async_computation.8 | async-start | bytes 8388608
  2.5 15.6 %slice-start.5 = ((s8[16777216]{0:T(1024)(128)(4,1)}), s8[4194304]{0:T(1024)(128)(4,1)S(1)}, s32[]{:S(2)}) async-start(s8[16777216]{0:T(1024)(128)(4,1)} %bitcast.2), calls=%async_computation.5 | async-start | bytes 8388608
  2.5 15.6 %slice-start.6 = ((s8[16777216]{0:T(1024)(128)(4,1)}), s8[4194304]{0:T(1024)(128)(4,1)S(1)}, s32[]{:S(2)}) async-start(s8[16777216]{0:T(1024)(128)(4,1)} %bitcast.2), calls=%async_computation.6 | async-start | bytes 8388608
  2.5 15.6 %slice-start.7 = ((s8[16777216]{0:T(1024)(128)(4,1)}), s8[4194304]{0:T(1024)(128)(4,1)S(1)}, s32[]{:S(2)}) async-start(s8[16777216]{0:T(1024)(128)(4,1)} %bitcast.2), calls=%async_computation.7 | async-start | bytes 8388608
  2.5 15.6 %slice-start.9 = ((s8[16777216]{0:T(1024)(128)(4,1)}), s8[4194304]{0:T(1024)(128)(4,1)S(1)}, s32[]{:S(2)}) async-start(s8[16777216]{0:T(1024)(128)(4,1)} %bitcast.4), calls=%async_computation.9 | async-start | bytes 8388608
  2.5 15.6 %slice-start.10 = ((s8[16777216]{0:T(1024)(128)(4,1)}), s8[4194304]{0:T(1024)(128)(4,1)S(1)}, s32[]{:S(2)}) async-start(s8[16777216]{0:T(1024)(128)(4,1)} %bitcast.4), calls=%async_computation.10 | async-start | bytes 8388608
  2.5 15.6 %slice-start.11 = ((s8[16777216]{0:T(1024)(128)(4,1)}), s8[4194304]{0:T(1024)(128)(4,1)S(1)}, s32[]{:S(2)}) async-start(s8[16777216]{0:T(1024)(128)(4,1)} %bitcast.4), calls=%async_computation.11 | async-start | bytes 8388608
  2.5 1.4 %collective-permute-start = (f32[8,1024]{1,0:T(8,128)S(1)}, f32[8,1024]{1,0:T(8,128)S(1)}, u32[]{:S(2)}, u32[]{:S(2)}) collective-permute-start(f32[8,1024]{1,0:T(8,128)S(1)} %get-tuple-element.27.a_ref), channel_id=1, source_target_pairs={{0,4},{4,0},{8,12},{12,8},{1,5},{5,1},{9,13},{13,9},{2,6},{6,2},{1... | collective-permute-start | bytes 98312 | tf_op jit(solution)/shard_map/ppermute | solution.py:41
  3.9 4.5 %collective-permute-start.1 = (bf16[8,1024]{1,0:T(8,128)(2,1)S(1)}, bf16[8,1024]{1,0:T(8,128)(2,1)S(1)}, u32[]{:S(2)}, u32[]{:S(2)}) collective-permute-start(bf16[8,1024]{1,0:T(8,128)(2,1)S(1)} %get-tuple-element.29), channel_id=1, source_target_pairs={{0,8},{4,12},{8,0},{12,4},{1,9},{5,13},{9,1},{13,5},{2,10},{6,14},... | collective-permute-start | bytes 49160 | tf_op jit(solution)/shard_map/ppermute | solution.py:41
  8.5 3.8 %collective-permute-start.2 = (bf16[8,1024]{1,0:T(8,128)(2,1)S(1)}, bf16[8,1024]{1,0:T(8,128)(2,1)S(1)}, u32[]{:S(2)}, u32[]{:S(2)}) collective-permute-start(bf16[8,1024]{1,0:T(8,128)(2,1)S(1)} %shard_map.57.a_ref), channel_id=1, source_target_pairs={{0,1},{1,0},{2,3},{3,2},{4,5},{5,4},{6,7},{7,6},{8,9},{9,8},{10,11... | collective-permute-start | bytes 49160 | tf_op jit(solution)/shard_map/ppermute | solution.py:41
  12.3 4.9 %collective-permute-start.3 = (bf16[16,1024]{1,0:T(8,128)(2,1)S(1)}, bf16[16,1024]{1,0:T(8,128)(2,1)S(1)}, u32[]{:S(2)}, u32[]{:S(2)}) collective-permute-start(bf16[16,1024]{1,0:T(8,128)(2,1)S(1)} %shard_map.58.a_ref.refs_0_), channel_id=1, source_target_pairs={{0,2},{1,3},{2,0},{3,1},{4,6},{5,7},{6,4},{7,5},{8,10},{9,11},{10,... | collective-permute-start | bytes 98312 | tf_op jit(solution)/shard_map/ppermute | solution.py:41
  20.5 2.8 %collective-permute-start.4 = (bf16[32,1536]{1,0:T(8,128)(2,1)S(1)}, bf16[32,1536]{1,0:T(8,128)(2,1)S(1)}, u32[]{:S(2)}, u32[]{:S(2)}) collective-permute-start(bf16[32,1536]{1,0:T(8,128)(2,1)S(1)} %get-tuple-element.33), channel_id=1, source_target_pairs={{0,4},{4,0},{8,12},{12,8},{1,5},{5,1},{9,13},{13,9},{2,6},{6,2},{1... | collective-permute-start | bytes 294920 | tf_op jit(solution)/shard_map/ppermute | solution.py:41
  22.8 4.0 %collective-permute-start.6 = (bf16[32,1536]{1,0:T(8,128)(2,1)S(1)}, bf16[32,1536]{1,0:T(8,128)(2,1)S(1)}, u32[]{:S(2)}, u32[]{:S(2)}) collective-permute-start(bf16[32,1536]{1,0:T(8,128)(2,1)S(1)} %get-tuple-element.37), channel_id=1, source_target_pairs={{0,4},{4,0},{8,12},{12,8},{1,5},{5,1},{9,13},{13,9},{2,6},{6,2},{1... | collective-permute-start | bytes 294920 | tf_op jit(solution)/shard_map/ppermute | solution.py:41
  23.3 5.9 %slice-start = ((s8[16777216]{0:T(1024)(128)(4,1)}), s8[4194304]{0:T(1024)(128)(4,1)S(1)}, s32[]{:S(2)}) async-start(s8[16777216]{0:T(1024)(128)(4,1)} %bitcast), calls=%async_computation | async-start | bytes 8388608
  23.3 5.9 %slice-start.1 = ((s8[16777216]{0:T(1024)(128)(4,1)}), s8[4194304]{0:T(1024)(128)(4,1)S(1)}, s32[]{:S(2)}) async-start(s8[16777216]{0:T(1024)(128)(4,1)} %bitcast), calls=%async_computation.1 | async-start | bytes 8388608
  23.3 5.9 %slice-start.2 = ((s8[16777216]{0:T(1024)(128)(4,1)}), s8[4194304]{0:T(1024)(128)(4,1)S(1)}, s32[]{:S(2)}) async-start(s8[16777216]{0:T(1024)(128)(4,1)} %bitcast), calls=%async_computation.2 | async-start | bytes 8388608
  23.3 5.7 %collective-permute-start.8 = (bf16[32,1536]{1,0:T(8,128)(2,1)S(1)}, bf16[32,1536]{1,0:T(8,128)(2,1)S(1)}, u32[]{:S(2)}, u32[]{:S(2)}) collective-permute-start(bf16[32,1536]{1,0:T(8,128)(2,1)S(1)} %get-tuple-element.34.refs_1_), channel_id=1, source_target_pairs={{0,8},{4,12},{8,0},{12,4},{1,9},{5,13},{9,1},{13,5},{2,10},{6,14},... | collective-permute-start | bytes 294920 | tf_op jit(solution)/shard_map/ppermute | solution.py:41
  26.8 1.3 %collective-permute-start.5 = (bf16[32,1024]{1,0:T(8,128)(2,1)S(1)}, bf16[32,1024]{1,0:T(8,128)(2,1)S(1)}, u32[]{:S(2)}, u32[]{:S(2)}) collective-permute-start(bf16[32,1024]{1,0:T(8,128)(2,1)S(1)} %get-tuple-element.36), channel_id=1, source_target_pairs={{0,4},{4,0},{8,12},{12,8},{1,5},{5,1},{9,13},{13,9},{2,6},{6,2},{1... | collective-permute-start | bytes 196616 | tf_op jit(solution)/shard_map/ppermute | solution.py:41
  26.8 2.6 %slice-start.3 = ((s8[16777216]{0:T(1024)(128)(4,1)}), s8[4194304]{0:T(1024)(128)(4,1)S(1)}, s32[]{:S(2)}) async-start(s8[16777216]{0:T(1024)(128)(4,1)} %bitcast), calls=%async_computation.3 | async-start | bytes 8388608
  26.9 5.7 %collective-permute-start.10 = (bf16[32,1536]{1,0:T(8,128)(2,1)S(1)}, bf16[32,1536]{1,0:T(8,128)(2,1)S(1)}, u32[]{:S(2)}, u32[]{:S(2)}) collective-permute-start(bf16[32,1536]{1,0:T(8,128)(2,1)S(1)} %get-tuple-element.38.refs_0_), channel_id=1, source_target_pairs={{0,8},{4,12},{8,0},{12,4},{1,9},{5,13},{9,1},{13,5},{2,10},{6,14},... | collective-permute-start | bytes 294920 | tf_op jit(solution)/shard_map/ppermute | solution.py:41
  28.1 5.8 %collective-permute-start.7 = (bf16[32,1024]{1,0:T(8,128)(2,1)S(1)}, bf16[32,1024]{1,0:T(8,128)(2,1)S(1)}, u32[]{:S(2)}, u32[]{:S(2)}) collective-permute-start(bf16[32,1024]{1,0:T(8,128)(2,1)S(1)} %get-tuple-element.40.refs_0_), channel_id=1, source_target_pairs={{0,8},{4,12},{8,0},{12,4},{1,9},{5,13},{9,1},{13,5},{2,10},{6,14},... | collective-permute-start | bytes 196616 | tf_op jit(solution)/shard_map/ppermute | solution.py:41
  29.1 3.6 %collective-permute-start.9 = (bf16[32,768]{1,0:T(8,128)(2,1)S(1)}, bf16[32,768]{1,0:T(8,128)(2,1)S(1)}, u32[]{:S(2)}, u32[]{:S(2)}) collective-permute-start(bf16[32,768]{1,0:T(8,128)(2,1)S(1)} %shard_map.68.refs_0_), channel_id=1, source_target_pairs={{0,4},{4,0},{8,12},{12,8},{1,5},{5,1},{9,13},{13,9},{2,6},{6,2},{1... | collective-permute-start | bytes 147464 | tf_op jit(solution)/shard_map/ppermute | solution.py:41
  32.6 2.9 %copy-start.1 = (bf16[2048,1024]{1,0:T(8,128)(2,1)S(1)}, bf16[2048,1024]{1,0:T(8,128)(2,1)}, u32[]{:S(2)}) copy-start(bf16[2048,1024]{1,0:T(8,128)(2,1)} %copy-done) | copy-start | bytes 12582916
  32.6 1.9 %collective-permute-start.12 = (bf16[32,768]{1,0:T(8,128)(2,1)S(1)}, bf16[32,768]{1,0:T(8,128)(2,1)S(1)}, u32[]{:S(2)}, u32[]{:S(2)}) collective-permute-start(bf16[32,768]{1,0:T(8,128)(2,1)S(1)} %shard_map.70.refs_1_), channel_id=1, source_target_pairs={{0,4},{4,0},{8,12},{12,8},{1,5},{5,1},{9,13},{13,9},{2,6},{6,2},{1... | collective-permute-start | bytes 147464 | tf_op jit(solution)/shard_map/ppermute | solution.py:41
  33.9 1.5 %collective-permute-start.11 = (bf16[32,512]{1,0:T(8,128)(2,1)S(1)}, bf16[32,512]{1,0:T(8,128)(2,1)S(1)}, u32[]{:S(2)}, u32[]{:S(2)}) collective-permute-start(bf16[32,512]{1,0:T(8,128)(2,1)S(1)} %shard_map.72.refs_1_), channel_id=1, source_target_pairs={{0,4},{4,0},{8,12},{12,8},{1,5},{5,1},{9,13},{13,9},{2,6},{6,2},{1... | collective-permute-start | bytes 98312 | tf_op jit(solution)/shard_map/ppermute | solution.py:41
  36.7 4.8 %collective-permute-start.13 = (bf16[16,1024]{1,0:T(8,128)(2,1)S(1)}, bf16[16,1024]{1,0:T(8,128)(2,1)S(1)}, u32[]{:S(2)}, u32[]{:S(2)}) collective-permute-start(bf16[16,1024]{1,0:T(8,128)(2,1)S(1)} %get-tuple-element.44), channel_id=1, source_target_pairs={{0,2},{1,3},{2,0},{3,1},{4,6},{5,7},{6,4},{7,5},{8,10},{9,11},{10,... | collective-permute-start | bytes 98312 | tf_op jit(solution)/shard_map/ppermute | solution.py:41
  41.5 3.8 %collective-permute-start.14 = (bf16[8,1024]{1,0:T(8,128)(2,1)S(1)}, bf16[8,1024]{1,0:T(8,128)(2,1)S(1)}, u32[]{:S(2)}, u32[]{:S(2)}) collective-permute-start(bf16[8,1024]{1,0:T(8,128)(2,1)S(1)} %get-tuple-element.46), channel_id=1, source_target_pairs={{0,1},{1,0},{2,3},{3,2},{4,5},{5,4},{6,7},{7,6},{8,9},{9,8},{10,11... | collective-permute-start | bytes 49160 | tf_op jit(solution)/shard_map/ppermute | solution.py:41
  45.3 3.8 %collective-permute-start.15 = (bf16[8,1024]{1,0:T(8,128)(2,1)S(1)}, bf16[8,1024]{1,0:T(8,128)(2,1)S(1)}, u32[]{:S(2)}, u32[]{:S(2)}) collective-permute-start(bf16[8,1024]{1,0:T(8,128)(2,1)S(1)} %get-tuple-element.48), channel_id=1, source_target_pairs={{0,8},{4,12},{8,0},{12,4},{1,9},{5,13},{9,1},{13,5},{2,10},{6,14},... | collective-permute-start | bytes 49160 | tf_op jit(solution)/shard_map/ppermute | solution.py:41
  49.1 1.2 %collective-permute-start.16 = (f32[8,1024]{1,0:T(8,128)S(1)}, f32[8,1024]{1,0:T(8,128)S(1)}, u32[]{:S(2)}, u32[]{:S(2)}) collective-permute-start(f32[8,1024]{1,0:T(8,128)S(1)} %shard_map.77.a_ref), channel_id=1, source_target_pairs={{0,4},{4,0},{8,12},{12,8},{1,5},{5,1},{9,13},{13,9},{2,6},{6,2},{1... | collective-permute-start | bytes 98312 | tf_op jit(solution)/shard_map/ppermute | solution.py:41

commit v7 on v6

--- a/solution.py
+++ b/solution.py
@@ -261,7 +261,7 @@
     return call(final_body, sds((local, width), BF16), 1, codes, swap(codes, "dp", 1, dp), turned)
 
 
-SHARES = (3, 3, 2)
+SHARES = (4, 1, 3)
 
 
 def solution(mesh):

time: 51.8 us -> 53.7 us (1.037)
  starting transfers between devices: 17.3 us -> 18.6 us
  waiting for transfers between devices: 17.5 us -> 18.2 us
    ppermute x17, starting transfers between devices: 17.3 us -> 18.6 us  [swap(): return lax.ppermute(value, axis, [(i, i ^ mask) for i in range(size)])]
    ppermute x17, waiting for transfers between devices: 17.5 us -> 18.2 us  [swap(): return lax.ppermute(value, axis, [(i, i ^ mask) for i in range(size)])]
  transfers between devices with their start and end apart: 17 -> 17, of which waited for: 10 -> 11; matrix products, arithmetic and copies ran while one was open for 0% -> 0% of each run, Pallas kernels for 16% -> 14%
where the time goes in v7:
time: 53.7 us; the launch traced here: 53.5 us
  starting transfers between devices  18.6 us (35%)
  waiting for transfers between devices  18.2 us (34%)
  Pallas kernels  16.3 us (30%)
    ppermute x17, starting transfers between devices, swap(): return lax.ppermute(value, axis, [(i, i ^ mask) for i in range(size)])  18.6 us
    ppermute x17, waiting for transfers between devices, swap(): return lax.ppermute(value, axis, [(i, i ^ mask) for i in range(size)])  18.2 us
    pallas_call x24, Pallas kernels, call(): pl.pallas_call(body, out_shape=out, in_specs=[HBM if i in fixed else VMEM...  16.3 us
  transfers between devices with their start and end apart: 17, of which 11 were waited for; matrix products, arithmetic and copies ran while one was open for 0% of the time, Pallas kernels for 14%

profile of v7, /device:TPU:0, one launch (start us, length us, event | category | flops | bytes accessed | tf_op | source)
XLA Modules:
  0.0 53.5 jit_solution(14554418429523619614)
XLA Ops:
  0.0 2.4 %shard_map.55 = (f32[8,1024]{1,0:T(8,128)S(1)}, bf16[2048,1024]{1,0:T(8,128)(2,1)S(1)}) custom-call(bf16[8,2048]{1,0:T(8,128)(2,1)} %x_ref.1, bf16[2048,1024]{1,0:T(8,128)(2,1)} %basis_ref.1), custom_call_target="tpu_custom_call" | custom-call | flops 1150000000 | bytes 65536 | tf_op jit(solution)/shard_map/pallas_call | solution.py:29
  2.4 0.0 slice-start.4
  2.5 0.0 slice-start.8
  2.5 0.5 collective-permute-start
  3.1 0.9 %collective-permute-done.b_ref = f32[8,1024]{1,0:T(8,128)S(1)} collective-permute-done((f32[8,1024]{1,0:T(8,128)S(1)}, f32[8,1024]{1,0:T(8,128)S(1)}, u32[]{:S(2)}, u32[]{:S(2)}) %collective-permute-start) | collective-permute-done | bytes 32800 | tf_op jit(solution)/shard_map/ppermute | solution.py:41
  3.9 2.8 %collective-permute-start.1 = (bf16[8,1024]{1,0:T(8,128)(2,1)S(1)}, bf16[8,1024]{1,0:T(8,128)(2,1)S(1)}, u32[]{:S(2)}, u32[]{:S(2)}) collective-permute-start(bf16[8,1024]{1,0:T(8,128)(2,1)S(1)} %get-tuple-element.29), channel_id=1, source_target_pairs={{0,8},{4,12},{8,0},{12,4},{1,9},{5,13},{9,1},{13,5},{2,10},{6,14},... | collective-permute-start | bytes 49160 | tf_op jit(solution)/shard_map/ppermute | solution.py:41
  6.8 1.7 %collective-permute-done.1.b_ref = bf16[8,1024]{1,0:T(8,128)(2,1)S(1)} collective-permute-done((bf16[8,1024]{1,0:T(8,128)(2,1)S(1)}, bf16[8,1024]{1,0:T(8,128)(2,1)S(1)}, u32[]{:S(2)}, u32[]{:S(2)}) %collective-permute-start.1) | collective-permute-done | bytes 16416 | tf_op jit(solution)/shard_map/ppermute | solution.py:41
  8.5 2.1 %collective-permute-start.2 = (bf16[8,1024]{1,0:T(8,128)(2,1)S(1)}, bf16[8,1024]{1,0:T(8,128)(2,1)S(1)}, u32[]{:S(2)}, u32[]{:S(2)}) collective-permute-start(bf16[8,1024]{1,0:T(8,128)(2,1)S(1)} %shard_map.57.a_ref), channel_id=1, source_target_pairs={{0,1},{1,0},{2,3},{3,2},{4,5},{5,4},{6,7},{7,6},{8,9},{9,8},{10,11... | collective-permute-start | bytes 49160 | tf_op jit(solution)/shard_map/ppermute | solution.py:41
  10.6 1.7 %collective-permute-done.2.b_ref = bf16[8,1024]{1,0:T(8,128)(2,1)S(1)} collective-permute-done((bf16[8,1024]{1,0:T(8,128)(2,1)S(1)}, bf16[8,1024]{1,0:T(8,128)(2,1)S(1)}, u32[]{:S(2)}, u32[]{:S(2)}) %collective-permute-start.2) | collective-permute-done | bytes 16416 | tf_op jit(solution)/shard_map/ppermute | solution.py:41
  12.3 3.0 %collective-permute-start.3 = (bf16[16,1024]{1,0:T(8,128)(2,1)S(1)}, bf16[16,1024]{1,0:T(8,128)(2,1)S(1)}, u32[]{:S(2)}, u32[]{:S(2)}) collective-permute-start(bf16[16,1024]{1,0:T(8,128)(2,1)S(1)} %shard_map.58.a_ref.refs_0_), channel_id=1, source_target_pairs={{0,2},{1,3},{2,0},{3,1},{4,6},{5,7},{6,4},{7,5},{8,10},{9,11},{10,... | collective-permute-start | bytes 98312 | tf_op jit(solution)/shard_map/ppermute | solution.py:41
  15.3 1.2 %shard_map.60.turned_ref = bf16[1024,2048]{1,0:T(8,128)(2,1)S(1)} custom-call(bf16[2048,1024]{1,0:T(8,128)(2,1)S(1)} %get-tuple-element.30.basis_ref, bf16[16,1024]{1,0:T(8,128)(2,1)S(1)} %shard_map.58.a_ref.refs_0_), custom_call_target="tpu_custom_call" | custom-call | flops 1150000000 | bytes 65536 | tf_op jit(solution)/shard_map/pallas_call | solution.py:29
  16.6 0.7 %collective-permute-done.3.b_ref = bf16[16,1024]{1,0:T(8,128)(2,1)S(1)} collective-permute-done((bf16[16,1024]{1,0:T(8,128)(2,1)S(1)}, bf16[16,1024]{1,0:T(8,128)(2,1)S(1)}, u32[]{:S(2)}, u32[]{:S(2)}) %collective-permute-start.3) | collective-permute-done | bytes 32800 | tf_op jit(solution)/shard_map/ppermute | solution.py:41
  17.2 0.8 %shard_map.61.x_ref = bf16[32,2048]{1,0:T(8,128)(2,1)S(1)} custom-call(bf16[32,1024]{1,0:T(8,128)(2,1)S(1)} %shard_map.59.codes_ref, bf16[1024,2048]{1,0:T(8,128)(2,1)S(1)} %shard_map.60.turned_ref), custom_call_target="tpu_custom_call" | custom-call | flops 575000000 | bytes 65536 | tf_op jit(solution)/shard_map/pallas_call | solution.py:29
  18.1 0.0 slice-done.8
  18.2 3.0 %shard_map.62 = (f32[32,2048]{1,0:T(8,128)S(1)}, bf16[32,2048]{1,0:T(8,128)(2,1)S(1)}) custom-call(bf16[32,2048]{1,0:T(8,128)(2,1)S(1)} %shard_map.61.x_ref, bf16[2048,4096]{1,0:T(8,128)(2,1)S(1)} %bitcast.3, bf16[2048,4096]{1,0:T(8,128)(2,1)S(1)} %bitcast.5), custom_call_target="tpu_custom_call" | custom-call | flops 3449999872 | bytes 65536 | tf_op jit(solution)/shard_map/pallas_call | solution.py:29
  21.2 0.9 %shard_map.63 = (f32[32,512]{1,0:T(8,128)S(1)}, bf16[32,512]{1,0:T(8,128)(2,1)S(1)}) custom-call(bf16[32,2048]{1,0:T(8,128)(2,1)S(1)} %shard_map.61.x_ref, bf16[2048,4096]{1,0:T(8,128)(2,1)S(1)} %bitcast.3, bf16[2048,4096]{1,0:T(8,128)(2,1)S(1)} %bitcast.5, f32[32,2048]{1,0:T(8,128)S(1)} %get-tuple-element.31.refs_0_.a_ref), custom_call_target="tpu_custom_call" | custom-call | flops 1724999936 | bytes 65536 | tf_op jit(solution)/shard_map/pallas_call | solution.py:29
  22.0 0.5 collective-permute-start.6
  22.6 0.0 slice-start
  22.6 0.0 slice-start.1
  22.6 0.0 slice-start.2
  22.6 1.9 %collective-permute-start.8 = (bf16[32,2048]{1,0:T(8,128)(2,1)S(1)}, bf16[32,2048]{1,0:T(8,128)(2,1)S(1)}, u32[]{:S(2)}, u32[]{:S(2)}) collective-permute-start(bf16[32,2048]{1,0:T(8,128)(2,1)S(1)} %get-tuple-element.34.refs_1_), channel_id=1, source_target_pairs={{0,8},{4,12},{8,0},{12,4},{1,9},{5,13},{9,1},{13,5},{2,10},{6,14},... | collective-permute-start | bytes 393224 | tf_op jit(solution)/shard_map/ppermute | solution.py:41
  24.5 2.3 %shard_map.65 = (f32[32,1536]{1,0:T(8,128)S(1)}, bf16[32,1536]{1,0:T(8,128)(2,1)S(1)}) custom-call(bf16[32,2048]{1,0:T(8,128)(2,1)S(1)} %shard_map.61.x_ref, bf16[2048,4096]{1,0:T(8,128)(2,1)S(1)} %bitcast.3, bf16[2048,4096]{1,0:T(8,128)(2,1)S(1)} %bitcast.5, f32[32,512]{1,0:T(8,128)S(1)} %get-tuple-element.32.refs_0_.a_ref, ...), custom_call_target="tpu_custom_call" | custom-call | flops 1724999936 | bytes 65536 | tf_op jit(solution)/shard_map/pallas_call | solution.py:29
  26.8 0.0 collective-permute-start.5
  26.9 0.0 slice-start.3
  26.9 1.3 %collective-permute-done.5.b_ref = bf16[32,1536]{1,0:T(8,128)(2,1)S(1)} collective-permute-done((bf16[32,1536]{1,0:T(8,128)(2,1)S(1)}, bf16[32,1536]{1,0:T(8,128)(2,1)S(1)}, u32[]{:S(2)}, u32[]{:S(2)}) %collective-permute-start.5) | collective-permute-done | bytes 98336 | tf_op jit(solution)/shard_map/ppermute | solution.py:41
  28.2 0.3 collective-permute-start.7
  28.5 0.1 shard_map.68.refs_0_
  28.5 0.1 collective-permute-start.9
  28.6 1.9 %collective-permute-start.10 = (bf16[32,512]{1,0:T(8,128)(2,1)S(1)}, bf16[32,512]{1,0:T(8,128)(2,1)S(1)}, u32[]{:S(2)}, u32[]{:S(2)}) collective-permute-start(bf16[32,512]{1,0:T(8,128)(2,1)S(1)} %get-tuple-element.38.refs_0_), channel_id=1, source_target_pairs={{0,8},{4,12},{8,0},{12,4},{1,9},{5,13},{9,1},{13,5},{2,10},{6,14},... | collective-permute-start | bytes 98312 | tf_op jit(solution)/shard_map/ppermute | solution.py:41
  30.5 0.8 %shard_map.69.refs_0_.refs_3_ = f32[32,2048]{1,0:T(8,128)S(1)} custom-call(bf16[32,1024]{1,0:T(8,128)(2,1)S(1)} %shard_map.68.refs_0_, bf16[4096,2048]{1,0:T(8,128)(2,1)S(1)} %bitcast.1), custom_call_target="tpu_custom_call" | custom-call | flops 115000000 | bytes 65536 | tf_op jit(solution)/shard_map/pallas_call | solution.py:29
  31.3 2.5 %collective-permute-done.10.b_ref = bf16[32,512]{1,0:T(8,128)(2,1)S(1)} collective-permute-done((bf16[32,512]{1,0:T(8,128)(2,1)S(1)}, bf16[32,512]{1,0:T(8,128)(2,1)S(1)}, u32[]{:S(2)}, u32[]{:S(2)}) %collective-permute-start.10) | collective-permute-done | bytes 32800 | tf_op jit(solution)/shard_map/ppermute | solution.py:41
  33.9 1.0 %shard_map.71.refs_0_.refs_3_ = f32[32,2048]{1,0:T(8,128)S(1)} custom-call(bf16[32,1024]{1,0:T(8,128)(2,1)S(1)} %collective-permute-done.9.refs_0_, bf16[32,256]{1,0:T(8,128)(2,1)S(1)} %shard_map.70.refs_1_, bf16[4096,2048]{1,0:T(8,128)(2,1)S(1)} %bitcast.1, f32[32,2048]{1,0:T(8,128)S(1)} %shard_map.69.refs_0_.refs_3_), custom_call_target="tpu_custom_call" | custom-call | flops 115000000 | bytes 65536 | tf_op jit(solution)/shard_map/pallas_call | solution.py:29
  34.9 0.0 collective-permute-done.7.b_ref
  34.9 0.1 shard_map.72.refs_1_
  34.9 0.1 collective-permute-start.11
  35.0 0.5 collective-permute-start.12
  35.5 0.8 %collective-permute-done.12.refs_0_ = bf16[32,256]{1,0:T(8,128)(2,1)S(1)} collective-permute-done((bf16[32,256]{1,0:T(8,128)(2,1)S(1)}, bf16[32,256]{1,0:T(8,128)(2,1)S(1)}, u32[]{:S(2)}, u32[]{:S(2)}) %collective-permute-start.12) | collective-permute-done | bytes 16416 | tf_op jit(solution)/shard_map/ppermute | solution.py:41
  36.4 0.8 %shard_map.73.acc_ref = f32[32,2048]{1,0:T(8,128)S(1)} custom-call(bf16[32,256]{1,0:T(8,128)(2,1)S(1)} %collective-permute-done.12.refs_0_, bf16[32,768]{1,0:T(8,128)(2,1)S(1)} %shard_map.72.refs_1_, bf16[4096,2048]{1,0:T(8,128)(2,1)S(1)} %bitcast.1, f32[32,2048]{1,0:T(8,128)S(1)} %shard_map.71.refs_0_.refs_3_), custom_call_target="tpu_custom_call" | custom-call | flops 115000000 | bytes 65536 | tf_op jit(solution)/shard_map/pallas_call | solution.py:29
  37.2 0.0 collective-permute-done.11.h_ref
  37.2 1.4 %shard_map.74 = (f32[16,1024]{1,0:T(8,128)S(1)}, bf16[16,1024]{1,0:T(8,128)(2,1)S(1)}) custom-call(bf16[32,768]{1,0:T(8,128)(2,1)S(1)} %collective-permute-done.11.h_ref, bf16[4096,2048]{1,0:T(8,128)(2,1)S(1)} %bitcast.1, f32[32,2048]{1,0:T(8,128)S(1)} %shard_map.73.acc_ref, bf16[2048,1024]{1,0:T(8,128)(2,1)S(1)} %copy-done.1), custom_call_target="tpu_custom_call" | custom-call | flops 1150000000 | bytes 65536 | tf_op jit(solution)/shard_map/pallas_call | solution.py:29
  38.6 2.6 %collective-permute-start.13 = (bf16[16,1024]{1,0:T(8,128)(2,1)S(1)}, bf16[16,1024]{1,0:T(8,128)(2,1)S(1)}, u32[]{:S(2)}, u32[]{:S(2)}) collective-permute-start(bf16[16,1024]{1,0:T(8,128)(2,1)S(1)} %get-tuple-element.44), channel_id=1, source_target_pairs={{0,2},{1,3},{2,0},{3,1},{4,6},{5,7},{6,4},{7,5},{8,10},{9,11},{10,... | collective-permute-start | bytes 98312 | tf_op jit(solution)/shard_map/ppermute | solution.py:41
  41.2 2.2 %collective-permute-done.13.b_ref = bf16[16,1024]{1,0:T(8,128)(2,1)S(1)} collective-permute-done((bf16[16,1024]{1,0:T(8,128)(2,1)S(1)}, bf16[16,1024]{1,0:T(8,128)(2,1)S(1)}, u32[]{:S(2)}, u32[]{:S(2)}) %collective-permute-start.13) | collective-permute-done | bytes 32800 | tf_op jit(solution)/shard_map/ppermute | solution.py:41
  43.4 1.6 %collective-permute-start.14 = (bf16[8,1024]{1,0:T(8,128)(2,1)S(1)}, bf16[8,1024]{1,0:T(8,128)(2,1)S(1)}, u32[]{:S(2)}, u32[]{:S(2)}) collective-permute-start(bf16[8,1024]{1,0:T(8,128)(2,1)S(1)} %get-tuple-element.46), channel_id=1, source_target_pairs={{0,1},{1,0},{2,3},{3,2},{4,5},{5,4},{6,7},{7,6},{8,9},{9,8},{10,11... | collective-permute-start | bytes 49160 | tf_op jit(solution)/shard_map/ppermute | solution.py:41
  45.1 2.2 %collective-permute-done.14.b_ref = bf16[8,1024]{1,0:T(8,128)(2,1)S(1)} collective-permute-done((bf16[8,1024]{1,0:T(8,128)(2,1)S(1)}, bf16[8,1024]{1,0:T(8,128)(2,1)S(1)}, u32[]{:S(2)}, u32[]{:S(2)}) %collective-permute-start.14) | collective-permute-done | bytes 16416 | tf_op jit(solution)/shard_map/ppermute | solution.py:41
  47.2 0.7 %collective-permute-start.15 = (bf16[8,1024]{1,0:T(8,128)(2,1)S(1)}, bf16[8,1024]{1,0:T(8,128)(2,1)S(1)}, u32[]{:S(2)}, u32[]{:S(2)}) collective-permute-start(bf16[8,1024]{1,0:T(8,128)(2,1)S(1)} %get-tuple-element.48), channel_id=1, source_target_pairs={{0,8},{4,12},{8,0},{12,4},{1,9},{5,13},{9,1},{13,5},{2,10},{6,14},... | collective-permute-start | bytes 49160 | tf_op jit(solution)/shard_map/ppermute | solution.py:41
  47.9 3.1 %collective-permute-done.15.b_ref = bf16[8,1024]{1,0:T(8,128)(2,1)S(1)} collective-permute-done((bf16[8,1024]{1,0:T(8,128)(2,1)S(1)}, bf16[8,1024]{1,0:T(8,128)(2,1)S(1)}, u32[]{:S(2)}, u32[]{:S(2)}) %collective-permute-start.15) | collective-permute-done | bytes 16416 | tf_op jit(solution)/shard_map/ppermute | solution.py:41
  51.1 1.2 %collective-permute-done.16.b_ref = f32[8,1024]{1,0:T(8,128)S(1)} collective-permute-done((f32[8,1024]{1,0:T(8,128)S(1)}, f32[8,1024]{1,0:T(8,128)S(1)}, u32[]{:S(2)}, u32[]{:S(2)}) %collective-permute-start.16) | collective-permute-done | bytes 32800 | tf_op jit(solution)/shard_map/ppermute | solution.py:41
  52.3 1.3 %shard_map.78 = bf16[8,2048]{1,0:T(8,128)(2,1)} custom-call(f32[8,1024]{1,0:T(8,128)S(1)} %shard_map.77.a_ref, f32[8,1024]{1,0:T(8,128)S(1)} %collective-permute-done.16.b_ref, bf16[1024,2048]{1,0:T(8,128)(2,1)S(1)} %shard_map.60.turned_ref), custom_call_target="tpu_custom_call" | custom-call | flops 1150000000 | bytes 65536 | tf_op jit(solution)/shard_map/pallas_call | solution.py:29
  (41 shorter events, 0.2 us)
Async XLA Ops:
  2.4 12.9 %copy-start = (bf16[2048,1024]{1,0:T(8,128)(2,1)}, bf16[2048,1024]{1,0:T(8,128)(2,1)S(1)}, u32[]{:S(2)}) copy-start(bf16[2048,1024]{1,0:T(8,128)(2,1)S(1)} %get-tuple-element.30.basis_ref) | copy-start | bytes 12582916
  2.4 15.6 %slice-start.4 = ((s8[16777216]{0:T(1024)(128)(4,1)}), s8[4194304]{0:T(1024)(128)(4,1)S(1)}, s32[]{:S(2)}) async-start(s8[16777216]{0:T(1024)(128)(4,1)} %bitcast.2), calls=%async_computation.4 | async-start | bytes 8388608
  2.5 15.6 %slice-start.8 = ((s8[16777216]{0:T(1024)(128)(4,1)}), s8[4194304]{0:T(1024)(128)(4,1)S(1)}, s32[]{:S(2)}) async-start(s8[16777216]{0:T(1024)(128)(4,1)} %bitcast.4), calls=%async_computation.8 | async-start | bytes 8388608
  2.5 15.6 %slice-start.5 = ((s8[16777216]{0:T(1024)(128)(4,1)}), s8[4194304]{0:T(1024)(128)(4,1)S(1)}, s32[]{:S(2)}) async-start(s8[16777216]{0:T(1024)(128)(4,1)} %bitcast.2), calls=%async_computation.5 | async-start | bytes 8388608
  2.5 15.6 %slice-start.6 = ((s8[16777216]{0:T(1024)(128)(4,1)}), s8[4194304]{0:T(1024)(128)(4,1)S(1)}, s32[]{:S(2)}) async-start(s8[16777216]{0:T(1024)(128)(4,1)} %bitcast.2), calls=%async_computation.6 | async-start | bytes 8388608
  2.5 15.6 %slice-start.7 = ((s8[16777216]{0:T(1024)(128)(4,1)}), s8[4194304]{0:T(1024)(128)(4,1)S(1)}, s32[]{:S(2)}) async-start(s8[16777216]{0:T(1024)(128)(4,1)} %bitcast.2), calls=%async_computation.7 | async-start | bytes 8388608
  2.5 15.6 %slice-start.9 = ((s8[16777216]{0:T(1024)(128)(4,1)}), s8[4194304]{0:T(1024)(128)(4,1)S(1)}, s32[]{:S(2)}) async-start(s8[16777216]{0:T(1024)(128)(4,1)} %bitcast.4), calls=%async_computation.9 | async-start | bytes 8388608
  2.5 15.6 %slice-start.10 = ((s8[16777216]{0:T(1024)(128)(4,1)}), s8[4194304]{0:T(1024)(128)(4,1)S(1)}, s32[]{:S(2)}) async-start(s8[16777216]{0:T(1024)(128)(4,1)} %bitcast.4), calls=%async_computation.10 | async-start | bytes 8388608
  2.5 15.6 %slice-start.11 = ((s8[16777216]{0:T(1024)(128)(4,1)}), s8[4194304]{0:T(1024)(128)(4,1)S(1)}, s32[]{:S(2)}) async-start(s8[16777216]{0:T(1024)(128)(4,1)} %bitcast.4), calls=%async_computation.11 | async-start | bytes 8388608
  2.5 1.4 %collective-permute-start = (f32[8,1024]{1,0:T(8,128)S(1)}, f32[8,1024]{1,0:T(8,128)S(1)}, u32[]{:S(2)}, u32[]{:S(2)}) collective-permute-start(f32[8,1024]{1,0:T(8,128)S(1)} %get-tuple-element.27.a_ref), channel_id=1, source_target_pairs={{0,4},{4,0},{8,12},{12,8},{1,5},{5,1},{9,13},{13,9},{2,6},{6,2},{1... | collective-permute-start | bytes 98312 | tf_op jit(solution)/shard_map/ppermute | solution.py:41
  3.9 4.5 %collective-permute-start.1 = (bf16[8,1024]{1,0:T(8,128)(2,1)S(1)}, bf16[8,1024]{1,0:T(8,128)(2,1)S(1)}, u32[]{:S(2)}, u32[]{:S(2)}) collective-permute-start(bf16[8,1024]{1,0:T(8,128)(2,1)S(1)} %get-tuple-element.29), channel_id=1, source_target_pairs={{0,8},{4,12},{8,0},{12,4},{1,9},{5,13},{9,1},{13,5},{2,10},{6,14},... | collective-permute-start | bytes 49160 | tf_op jit(solution)/shard_map/ppermute | solution.py:41
  8.5 3.8 %collective-permute-start.2 = (bf16[8,1024]{1,0:T(8,128)(2,1)S(1)}, bf16[8,1024]{1,0:T(8,128)(2,1)S(1)}, u32[]{:S(2)}, u32[]{:S(2)}) collective-permute-start(bf16[8,1024]{1,0:T(8,128)(2,1)S(1)} %shard_map.57.a_ref), channel_id=1, source_target_pairs={{0,1},{1,0},{2,3},{3,2},{4,5},{5,4},{6,7},{7,6},{8,9},{9,8},{10,11... | collective-permute-start | bytes 49160 | tf_op jit(solution)/shard_map/ppermute | solution.py:41
  12.3 4.9 %collective-permute-start.3 = (bf16[16,1024]{1,0:T(8,128)(2,1)S(1)}, bf16[16,1024]{1,0:T(8,128)(2,1)S(1)}, u32[]{:S(2)}, u32[]{:S(2)}) collective-permute-start(bf16[16,1024]{1,0:T(8,128)(2,1)S(1)} %shard_map.58.a_ref.refs_0_), channel_id=1, source_target_pairs={{0,2},{1,3},{2,0},{3,1},{4,6},{5,7},{6,4},{7,5},{8,10},{9,11},{10,... | collective-permute-start | bytes 98312 | tf_op jit(solution)/shard_map/ppermute | solution.py:41
  21.2 1.4 %collective-permute-start.4 = (bf16[32,2048]{1,0:T(8,128)(2,1)S(1)}, bf16[32,2048]{1,0:T(8,128)(2,1)S(1)}, u32[]{:S(2)}, u32[]{:S(2)}) collective-permute-start(bf16[32,2048]{1,0:T(8,128)(2,1)S(1)} %get-tuple-element.33), channel_id=1, source_target_pairs={{0,4},{4,0},{8,12},{12,8},{1,5},{5,1},{9,13},{13,9},{2,6},{6,2},{1... | collective-permute-start | bytes 393224 | tf_op jit(solution)/shard_map/ppermute | solution.py:41
  22.0 4.8 %collective-permute-start.6 = (bf16[32,512]{1,0:T(8,128)(2,1)S(1)}, bf16[32,512]{1,0:T(8,128)(2,1)S(1)}, u32[]{:S(2)}, u32[]{:S(2)}) collective-permute-start(bf16[32,512]{1,0:T(8,128)(2,1)S(1)} %get-tuple-element.37), channel_id=1, source_target_pairs={{0,4},{4,0},{8,12},{12,8},{1,5},{5,1},{9,13},{13,9},{2,6},{6,2},{1... | collective-permute-start | bytes 98312 | tf_op jit(solution)/shard_map/ppermute | solution.py:41
  22.6 7.9 %slice-start = ((s8[16777216]{0:T(1024)(128)(4,1)}), s8[4194304]{0:T(1024)(128)(4,1)S(1)}, s32[]{:S(2)}) async-start(s8[16777216]{0:T(1024)(128)(4,1)} %bitcast), calls=%async_computation | async-start | bytes 8388608
  22.6 7.9 %slice-start.1 = ((s8[16777216]{0:T(1024)(128)(4,1)}), s8[4194304]{0:T(1024)(128)(4,1)S(1)}, s32[]{:S(2)}) async-start(s8[16777216]{0:T(1024)(128)(4,1)} %bitcast), calls=%async_computation.1 | async-start | bytes 8388608
  22.6 7.9 %slice-start.2 = ((s8[16777216]{0:T(1024)(128)(4,1)}), s8[4194304]{0:T(1024)(128)(4,1)S(1)}, s32[]{:S(2)}) async-start(s8[16777216]{0:T(1024)(128)(4,1)} %bitcast), calls=%async_computation.2 | async-start | bytes 8388608
  22.6 5.8 %collective-permute-start.8 = (bf16[32,2048]{1,0:T(8,128)(2,1)S(1)}, bf16[32,2048]{1,0:T(8,128)(2,1)S(1)}, u32[]{:S(2)}, u32[]{:S(2)}) collective-permute-start(bf16[32,2048]{1,0:T(8,128)(2,1)S(1)} %get-tuple-element.34.refs_1_), channel_id=1, source_target_pairs={{0,8},{4,12},{8,0},{12,4},{1,9},{5,13},{9,1},{13,5},{2,10},{6,14},... | collective-permute-start | bytes 393224 | tf_op jit(solution)/shard_map/ppermute | solution.py:41
  26.8 1.3 %collective-permute-start.5 = (bf16[32,1536]{1,0:T(8,128)(2,1)S(1)}, bf16[32,1536]{1,0:T(8,128)(2,1)S(1)}, u32[]{:S(2)}, u32[]{:S(2)}) collective-permute-start(bf16[32,1536]{1,0:T(8,128)(2,1)S(1)} %get-tuple-element.36), channel_id=1, source_target_pairs={{0,4},{4,0},{8,12},{12,8},{1,5},{5,1},{9,13},{13,9},{2,6},{6,2},{1... | collective-permute-start | bytes 294920 | tf_op jit(solution)/shard_map/ppermute | solution.py:41
  26.9 3.6 %slice-start.3 = ((s8[16777216]{0:T(1024)(128)(4,1)}), s8[4194304]{0:T(1024)(128)(4,1)S(1)}, s32[]{:S(2)}) async-start(s8[16777216]{0:T(1024)(128)(4,1)} %bitcast), calls=%async_computation.3 | async-start | bytes 8388608
  28.2 6.7 %collective-permute-start.7 = (bf16[32,1536]{1,0:T(8,128)(2,1)S(1)}, bf16[32,1536]{1,0:T(8,128)(2,1)S(1)}, u32[]{:S(2)}, u32[]{:S(2)}) collective-permute-start(bf16[32,1536]{1,0:T(8,128)(2,1)S(1)} %get-tuple-element.40.refs_0_), channel_id=1, source_target_pairs={{0,8},{4,12},{8,0},{12,4},{1,9},{5,13},{9,1},{13,5},{2,10},{6,14},... | collective-permute-start | bytes 294920 | tf_op jit(solution)/shard_map/ppermute | solution.py:41
  28.5 5.3 %collective-permute-start.9 = (bf16[32,1024]{1,0:T(8,128)(2,1)S(1)}, bf16[32,1024]{1,0:T(8,128)(2,1)S(1)}, u32[]{:S(2)}, u32[]{:S(2)}) collective-permute-start(bf16[32,1024]{1,0:T(8,128)(2,1)S(1)} %shard_map.68.refs_0_), channel_id=1, source_target_pairs={{0,4},{4,0},{8,12},{12,8},{1,5},{5,1},{9,13},{13,9},{2,6},{6,2},{1... | collective-permute-start | bytes 196616 | tf_op jit(solution)/shard_map/ppermute | solution.py:41
  28.6 5.2 %collective-permute-start.10 = (bf16[32,512]{1,0:T(8,128)(2,1)S(1)}, bf16[32,512]{1,0:T(8,128)(2,1)S(1)}, u32[]{:S(2)}, u32[]{:S(2)}) collective-permute-start(bf16[32,512]{1,0:T(8,128)(2,1)S(1)} %get-tuple-element.38.refs_0_), channel_id=1, source_target_pairs={{0,8},{4,12},{8,0},{12,4},{1,9},{5,13},{9,1},{13,5},{2,10},{6,14},... | collective-permute-start | bytes 98312 | tf_op jit(solution)/shard_map/ppermute | solution.py:41
  33.8 3.4 %copy-start.1 = (bf16[2048,1024]{1,0:T(8,128)(2,1)S(1)}, bf16[2048,1024]{1,0:T(8,128)(2,1)}, u32[]{:S(2)}) copy-start(bf16[2048,1024]{1,0:T(8,128)(2,1)} %copy-done) | copy-start | bytes 12582916
  34.9 2.2 %collective-permute-start.11 = (bf16[32,768]{1,0:T(8,128)(2,1)S(1)}, bf16[32,768]{1,0:T(8,128)(2,1)S(1)}, u32[]{:S(2)}, u32[]{:S(2)}) collective-permute-start(bf16[32,768]{1,0:T(8,128)(2,1)S(1)} %shard_map.72.refs_1_), channel_id=1, source_target_pairs={{0,4},{4,0},{8,12},{12,8},{1,5},{5,1},{9,13},{13,9},{2,6},{6,2},{1... | collective-permute-start | bytes 147464 | tf_op jit(solution)/shard_map/ppermute | solution.py:41
  35.0 1.3 %collective-permute-start.12 = (bf16[32,256]{1,0:T(8,128)(2,1)S(1)}, bf16[32,256]{1,0:T(8,128)(2,1)S(1)}, u32[]{:S(2)}, u32[]{:S(2)}) collective-permute-start(bf16[32,256]{1,0:T(8,128)(2,1)S(1)} %shard_map.70.refs_1_), channel_id=1, source_target_pairs={{0,4},{4,0},{8,12},{12,8},{1,5},{5,1},{9,13},{13,9},{2,6},{6,2},{1... | collective-permute-start | bytes 49160 | tf_op jit(solution)/shard_map/ppermute | solution.py:41
  38.6 4.8 %collective-permute-start.13 = (bf16[16,1024]{1,0:T(8,128)(2,1)S(1)}, bf16[16,1024]{1,0:T(8,128)(2,1)S(1)}, u32[]{:S(2)}, u32[]{:S(2)}) collective-permute-start(bf16[16,1024]{1,0:T(8,128)(2,1)S(1)} %get-tuple-element.44), channel_id=1, source_target_pairs={{0,2},{1,3},{2,0},{3,1},{4,6},{5,7},{6,4},{7,5},{8,10},{9,11},{10,... | collective-permute-start | bytes 98312 | tf_op jit(solution)/shard_map/ppermute | solution.py:41
  43.4 3.8 %collective-permute-start.14 = (bf16[8,1024]{1,0:T(8,128)(2,1)S(1)}, bf16[8,1024]{1,0:T(8,128)(2,1)S(1)}, u32[]{:S(2)}, u32[]{:S(2)}) collective-permute-start(bf16[8,1024]{1,0:T(8,128)(2,1)S(1)} %get-tuple-element.46), channel_id=1, source_target_pairs={{0,1},{1,0},{2,3},{3,2},{4,5},{5,4},{6,7},{7,6},{8,9},{9,8},{10,11... | collective-permute-start | bytes 49160 | tf_op jit(solution)/shard_map/ppermute | solution.py:41
  47.2 3.8 %collective-permute-start.15 = (bf16[8,1024]{1,0:T(8,128)(2,1)S(1)}, bf16[8,1024]{1,0:T(8,128)(2,1)S(1)}, u32[]{:S(2)}, u32[]{:S(2)}) collective-permute-start(bf16[8,1024]{1,0:T(8,128)(2,1)S(1)} %get-tuple-element.48), channel_id=1, source_target_pairs={{0,8},{4,12},{8,0},{12,4},{1,9},{5,13},{9,1},{13,5},{2,10},{6,14},... | collective-permute-start | bytes 49160 | tf_op jit(solution)/shard_map/ppermute | solution.py:41
  51.0 1.2 %collective-permute-start.16 = (f32[8,1024]{1,0:T(8,128)S(1)}, f32[8,1024]{1,0:T(8,128)S(1)}, u32[]{:S(2)}, u32[]{:S(2)}) collective-permute-start(f32[8,1024]{1,0:T(8,128)S(1)} %shard_map.77.a_ref), channel_id=1, source_target_pairs={{0,4},{4,0},{8,12},{12,8},{1,5},{5,1},{9,13},{13,9},{2,6},{6,2},{1... | collective-permute-start | bytes 98312 | tf_op jit(solution)/shard_map/ppermute | solution.py:41

commit v8 on v7

--- a/solution.py
+++ b/solution.py
@@ -261,7 +261,7 @@
     return call(final_body, sds((local, width), BF16), 1, codes, swap(codes, "dp", 1, dp), turned)
 
 
-SHARES = (4, 1, 3)
+SHARES = (4, 2, 2)
 
 
 def solution(mesh):

time: 53.7 us -> 51.5 us (0.959)
  waiting for transfers between devices: 18.2 us -> 14.7 us
  starting transfers between devices: 18.6 us -> 20.1 us
    ppermute x17, waiting for transfers between devices: 18.2 us -> 14.7 us  [swap(): return lax.ppermute(value, axis, [(i, i ^ mask) for i in range(size)])]
    ppermute x17, starting transfers between devices: 18.6 us -> 20.1 us  [swap(): return lax.ppermute(value, axis, [(i, i ^ mask) for i in range(size)])]
  transfers between devices with their start and end apart: 17 -> 17, of which waited for: 11 -> 12; matrix products, arithmetic and copies ran while one was open for 0% -> 0% of each run, Pallas kernels for 14% -> 14%
where the time goes in v8:
time: 51.5 us; the launch traced here: 51.4 us
  starting transfers between devices  20.1 us (39%)
  Pallas kernels  16.2 us (31%)
  waiting for transfers between devices  14.7 us (29%)
    ppermute x17, starting transfers between devices, swap(): return lax.ppermute(value, axis, [(i, i ^ mask) for i in range(size)])  20.1 us
    pallas_call x24, Pallas kernels, call(): pl.pallas_call(body, out_shape=out, in_specs=[HBM if i in fixed else VMEM...  16.2 us
    ppermute x17, waiting for transfers between devices, swap(): return lax.ppermute(value, axis, [(i, i ^ mask) for i in range(size)])  14.7 us
  transfers between devices with their start and end apart: 17, of which 12 were waited for; matrix products, arithmetic and copies ran while one was open for 0% of the time, Pallas kernels for 14%

profile of v8, /device:TPU:0, one launch (start us, length us, event | category | flops | bytes accessed | tf_op | source)
XLA Modules:
  0.0 51.4 jit_solution(16281001961943444460)
XLA Ops:
  0.0 2.4 %shard_map.55 = (f32[8,1024]{1,0:T(8,128)S(1)}, bf16[2048,1024]{1,0:T(8,128)(2,1)S(1)}) custom-call(bf16[8,2048]{1,0:T(8,128)(2,1)} %x_ref.1, bf16[2048,1024]{1,0:T(8,128)(2,1)} %basis_ref.1), custom_call_target="tpu_custom_call" | custom-call | flops 1150000000 | bytes 65536 | tf_op jit(solution)/shard_map/pallas_call | solution.py:29
  2.4 0.0 slice-start.4
  2.5 0.0 slice-start.8
  2.5 0.0 slice-start.6
  2.5 0.0 slice-start.7
  2.5 0.5 %collective-permute-start = (f32[8,1024]{1,0:T(8,128)S(1)}, f32[8,1024]{1,0:T(8,128)S(1)}, u32[]{:S(2)}, u32[]{:S(2)}) collective-permute-start(f32[8,1024]{1,0:T(8,128)S(1)} %get-tuple-element.27.a_ref), channel_id=1, source_target_pairs={{0,4},{4,0},{8,12},{12,8},{1,5},{5,1},{9,13},{13,9},{2,6},{6,2},{1... | collective-permute-start | bytes 98312 | tf_op jit(solution)/shard_map/ppermute | solution.py:41
  3.1 0.9 %collective-permute-done.b_ref = f32[8,1024]{1,0:T(8,128)S(1)} collective-permute-done((f32[8,1024]{1,0:T(8,128)S(1)}, f32[8,1024]{1,0:T(8,128)S(1)}, u32[]{:S(2)}, u32[]{:S(2)}) %collective-permute-start) | collective-permute-done | bytes 32800 | tf_op jit(solution)/shard_map/ppermute | solution.py:41
  3.9 2.8 %collective-permute-start.1 = (bf16[8,1024]{1,0:T(8,128)(2,1)S(1)}, bf16[8,1024]{1,0:T(8,128)(2,1)S(1)}, u32[]{:S(2)}, u32[]{:S(2)}) collective-permute-start(bf16[8,1024]{1,0:T(8,128)(2,1)S(1)} %get-tuple-element.29), channel_id=1, source_target_pairs={{0,8},{4,12},{8,0},{12,4},{1,9},{5,13},{9,1},{13,5},{2,10},{6,14},... | collective-permute-start | bytes 49160 | tf_op jit(solution)/shard_map/ppermute | solution.py:41
  6.8 1.7 %collective-permute-done.1.b_ref = bf16[8,1024]{1,0:T(8,128)(2,1)S(1)} collective-permute-done((bf16[8,1024]{1,0:T(8,128)(2,1)S(1)}, bf16[8,1024]{1,0:T(8,128)(2,1)S(1)}, u32[]{:S(2)}, u32[]{:S(2)}) %collective-permute-start.1) | collective-permute-done | bytes 16416 | tf_op jit(solution)/shard_map/ppermute | solution.py:41
  8.5 2.1 %collective-permute-start.2 = (bf16[8,1024]{1,0:T(8,128)(2,1)S(1)}, bf16[8,1024]{1,0:T(8,128)(2,1)S(1)}, u32[]{:S(2)}, u32[]{:S(2)}) collective-permute-start(bf16[8,1024]{1,0:T(8,128)(2,1)S(1)} %shard_map.57.a_ref), channel_id=1, source_target_pairs={{0,1},{1,0},{2,3},{3,2},{4,5},{5,4},{6,7},{7,6},{8,9},{9,8},{10,11... | collective-permute-start | bytes 49160 | tf_op jit(solution)/shard_map/ppermute | solution.py:41
  10.6 1.7 %collective-permute-done.2.b_ref = bf16[8,1024]{1,0:T(8,128)(2,1)S(1)} collective-permute-done((bf16[8,1024]{1,0:T(8,128)(2,1)S(1)}, bf16[8,1024]{1,0:T(8,128)(2,1)S(1)}, u32[]{:S(2)}, u32[]{:S(2)}) %collective-permute-start.2) | collective-permute-done | bytes 16416 | tf_op jit(solution)/shard_map/ppermute | solution.py:41
  12.3 3.0 %collective-permute-start.3 = (bf16[16,1024]{1,0:T(8,128)(2,1)S(1)}, bf16[16,1024]{1,0:T(8,128)(2,1)S(1)}, u32[]{:S(2)}, u32[]{:S(2)}) collective-permute-start(bf16[16,1024]{1,0:T(8,128)(2,1)S(1)} %shard_map.58.a_ref.refs_0_), channel_id=1, source_target_pairs={{0,2},{1,3},{2,0},{3,1},{4,6},{5,7},{6,4},{7,5},{8,10},{9,11},{10,... | collective-permute-start | bytes 98312 | tf_op jit(solution)/shard_map/ppermute | solution.py:41
  15.3 1.2 %shard_map.60.turned_ref = bf16[1024,2048]{1,0:T(8,128)(2,1)S(1)} custom-call(bf16[2048,1024]{1,0:T(8,128)(2,1)S(1)} %get-tuple-element.30.basis_ref, bf16[16,1024]{1,0:T(8,128)(2,1)S(1)} %shard_map.58.a_ref.refs_0_), custom_call_target="tpu_custom_call" | custom-call | flops 1150000000 | bytes 65536 | tf_op jit(solution)/shard_map/pallas_call | solution.py:29
  16.6 0.7 %collective-permute-done.3.b_ref = bf16[16,1024]{1,0:T(8,128)(2,1)S(1)} collective-permute-done((bf16[16,1024]{1,0:T(8,128)(2,1)S(1)}, bf16[16,1024]{1,0:T(8,128)(2,1)S(1)}, u32[]{:S(2)}, u32[]{:S(2)}) %collective-permute-start.3) | collective-permute-done | bytes 32800 | tf_op jit(solution)/shard_map/ppermute | solution.py:41
  17.2 0.8 %shard_map.61.x_ref = bf16[32,2048]{1,0:T(8,128)(2,1)S(1)} custom-call(bf16[32,1024]{1,0:T(8,128)(2,1)S(1)} %shard_map.59.codes_ref, bf16[1024,2048]{1,0:T(8,128)(2,1)S(1)} %shard_map.60.turned_ref), custom_call_target="tpu_custom_call" | custom-call | flops 575000000 | bytes 65536 | tf_op jit(solution)/shard_map/pallas_call | solution.py:29
  18.1 0.0 slice-done.8
  18.2 3.0 %shard_map.62 = (f32[32,2048]{1,0:T(8,128)S(1)}, bf16[32,2048]{1,0:T(8,128)(2,1)S(1)}) custom-call(bf16[32,2048]{1,0:T(8,128)(2,1)S(1)} %shard_map.61.x_ref, bf16[2048,4096]{1,0:T(8,128)(2,1)S(1)} %bitcast.3, bf16[2048,4096]{1,0:T(8,128)(2,1)S(1)} %bitcast.5), custom_call_target="tpu_custom_call" | custom-call | flops 3449999872 | bytes 65536 | tf_op jit(solution)/shard_map/pallas_call | solution.py:29
  21.2 1.6 %shard_map.63 = (f32[32,1024]{1,0:T(8,128)S(1)}, bf16[32,1024]{1,0:T(8,128)(2,1)S(1)}) custom-call(bf16[32,2048]{1,0:T(8,128)(2,1)S(1)} %shard_map.61.x_ref, bf16[2048,4096]{1,0:T(8,128)(2,1)S(1)} %bitcast.3, bf16[2048,4096]{1,0:T(8,128)(2,1)S(1)} %bitcast.5, f32[32,2048]{1,0:T(8,128)S(1)} %get-tuple-element.31.refs_0_.a_ref), custom_call_target="tpu_custom_call" | custom-call | flops 1724999936 | bytes 65536 | tf_op jit(solution)/shard_map/pallas_call | solution.py:29
  22.8 0.5 %collective-permute-start.6 = (bf16[32,1024]{1,0:T(8,128)(2,1)S(1)}, bf16[32,1024]{1,0:T(8,128)(2,1)S(1)}, u32[]{:S(2)}, u32[]{:S(2)}) collective-permute-start(bf16[32,1024]{1,0:T(8,128)(2,1)S(1)} %get-tuple-element.37), channel_id=1, source_target_pairs={{0,4},{4,0},{8,12},{12,8},{1,5},{5,1},{9,13},{13,9},{2,6},{6,2},{1... | collective-permute-start | bytes 196616 | tf_op jit(solution)/shard_map/ppermute | solution.py:41
  23.3 0.0 slice-start
  23.3 0.0 slice-start.1
  23.4 0.0 slice-start.2
  23.4 1.9 %collective-permute-start.8 = (bf16[32,2048]{1,0:T(8,128)(2,1)S(1)}, bf16[32,2048]{1,0:T(8,128)(2,1)S(1)}, u32[]{:S(2)}, u32[]{:S(2)}) collective-permute-start(bf16[32,2048]{1,0:T(8,128)(2,1)S(1)} %get-tuple-element.34.refs_1_), channel_id=1, source_target_pairs={{0,8},{4,12},{8,0},{12,4},{1,9},{5,13},{9,1},{13,5},{2,10},{6,14},... | collective-permute-start | bytes 393224 | tf_op jit(solution)/shard_map/ppermute | solution.py:41
  25.3 1.6 %shard_map.65 = (f32[32,1024]{1,0:T(8,128)S(1)}, bf16[32,1024]{1,0:T(8,128)(2,1)S(1)}) custom-call(bf16[32,2048]{1,0:T(8,128)(2,1)S(1)} %shard_map.61.x_ref, bf16[2048,4096]{1,0:T(8,128)(2,1)S(1)} %bitcast.3, bf16[2048,4096]{1,0:T(8,128)(2,1)S(1)} %bitcast.5, f32[32,1024]{1,0:T(8,128)S(1)} %get-tuple-element.32.refs_0_.a_ref, ...), custom_call_target="tpu_custom_call" | custom-call | flops 1724999936 | bytes 65536 | tf_op jit(solution)/shard_map/pallas_call | solution.py:29
  26.8 0.0 collective-permute-done.6.b_ref
  26.8 0.0 slice-start.3
  26.9 0.3 collective-permute-start.10
  27.1 0.9 %collective-permute-done.5.b_ref = bf16[32,1024]{1,0:T(8,128)(2,1)S(1)} collective-permute-done((bf16[32,1024]{1,0:T(8,128)(2,1)S(1)}, bf16[32,1024]{1,0:T(8,128)(2,1)S(1)}, u32[]{:S(2)}, u32[]{:S(2)}) %collective-permute-start.5) | collective-permute-done | bytes 65568 | tf_op jit(solution)/shard_map/ppermute | solution.py:41
  28.1 0.8 %collective-permute-done.8.b_ref = bf16[32,2048]{1,0:T(8,128)(2,1)S(1)} collective-permute-done((bf16[32,2048]{1,0:T(8,128)(2,1)S(1)}, bf16[32,2048]{1,0:T(8,128)(2,1)S(1)}, u32[]{:S(2)}, u32[]{:S(2)}) %collective-permute-start.8) | collective-permute-done | bytes 131104 | tf_op jit(solution)/shard_map/ppermute | solution.py:41
  28.9 0.1 shard_map.68.refs_0_
  29.0 0.1 collective-permute-start.9
  29.1 2.1 %collective-permute-start.7 = (bf16[32,1024]{1,0:T(8,128)(2,1)S(1)}, bf16[32,1024]{1,0:T(8,128)(2,1)S(1)}, u32[]{:S(2)}, u32[]{:S(2)}) collective-permute-start(bf16[32,1024]{1,0:T(8,128)(2,1)S(1)} %get-tuple-element.40.refs_0_), channel_id=1, source_target_pairs={{0,8},{4,12},{8,0},{12,4},{1,9},{5,13},{9,1},{13,5},{2,10},{6,14},... | collective-permute-start | bytes 196616 | tf_op jit(solution)/shard_map/ppermute | solution.py:41
  31.2 0.8 %shard_map.69.refs_0_.refs_3_ = f32[32,2048]{1,0:T(8,128)S(1)} custom-call(bf16[32,1024]{1,0:T(8,128)(2,1)S(1)} %shard_map.68.refs_0_, bf16[4096,2048]{1,0:T(8,128)(2,1)S(1)} %bitcast.1), custom_call_target="tpu_custom_call" | custom-call | flops 115000000 | bytes 65536 | tf_op jit(solution)/shard_map/pallas_call | solution.py:29
  32.1 0.2 collective-permute-start.12
  32.3 1.2 %shard_map.71.refs_0_.refs_3_ = f32[32,2048]{1,0:T(8,128)S(1)} custom-call(bf16[32,1024]{1,0:T(8,128)(2,1)S(1)} %collective-permute-done.9.refs_0_, bf16[32,512]{1,0:T(8,128)(2,1)S(1)} %shard_map.70.refs_1_, bf16[4096,2048]{1,0:T(8,128)(2,1)S(1)} %bitcast.1, f32[32,2048]{1,0:T(8,128)S(1)} %shard_map.69.refs_0_.refs_3_), custom_call_target="tpu_custom_call" | custom-call | flops 115000000 | bytes 65536 | tf_op jit(solution)/shard_map/pallas_call | solution.py:29
  33.5 0.3 collective-permute-done.7.b_ref
  33.9 0.1 collective-permute-start.11
  34.0 0.8 %shard_map.73.acc_ref = f32[32,2048]{1,0:T(8,128)S(1)} custom-call(bf16[32,512]{1,0:T(8,128)(2,1)S(1)} %collective-permute-done.12.refs_0_, bf16[32,512]{1,0:T(8,128)(2,1)S(1)} %shard_map.72.refs_1_, bf16[4096,2048]{1,0:T(8,128)(2,1)S(1)} %bitcast.1, f32[32,2048]{1,0:T(8,128)S(1)} %shard_map.71.refs_0_.refs_3_), custom_call_target="tpu_custom_call" | custom-call | flops 115000000 | bytes 65536 | tf_op jit(solution)/shard_map/pallas_call | solution.py:29
  34.8 0.4 collective-permute-done.11.h_ref
  35.2 1.2 %shard_map.74 = (f32[16,1024]{1,0:T(8,128)S(1)}, bf16[16,1024]{1,0:T(8,128)(2,1)S(1)}) custom-call(bf16[32,512]{1,0:T(8,128)(2,1)S(1)} %collective-permute-done.11.h_ref, bf16[4096,2048]{1,0:T(8,128)(2,1)S(1)} %bitcast.1, f32[32,2048]{1,0:T(8,128)S(1)} %shard_map.73.acc_ref, bf16[2048,1024]{1,0:T(8,128)(2,1)S(1)} %copy-done.1), custom_call_target="tpu_custom_call" | custom-call | flops 1150000000 | bytes 65536 | tf_op jit(solution)/shard_map/pallas_call | solution.py:29
  36.4 2.6 %collective-permute-start.13 = (bf16[16,1024]{1,0:T(8,128)(2,1)S(1)}, bf16[16,1024]{1,0:T(8,128)(2,1)S(1)}, u32[]{:S(2)}, u32[]{:S(2)}) collective-permute-start(bf16[16,1024]{1,0:T(8,128)(2,1)S(1)} %get-tuple-element.44), channel_id=1, source_target_pairs={{0,2},{1,3},{2,0},{3,1},{4,6},{5,7},{6,4},{7,5},{8,10},{9,11},{10,... | collective-permute-start | bytes 98312 | tf_op jit(solution)/shard_map/ppermute | solution.py:41
  39.0 2.2 %collective-permute-done.13.b_ref = bf16[16,1024]{1,0:T(8,128)(2,1)S(1)} collective-permute-done((bf16[16,1024]{1,0:T(8,128)(2,1)S(1)}, bf16[16,1024]{1,0:T(8,128)(2,1)S(1)}, u32[]{:S(2)}, u32[]{:S(2)}) %collective-permute-start.13) | collective-permute-done | bytes 32800 | tf_op jit(solution)/shard_map/ppermute | solution.py:41
  41.2 1.6 %collective-permute-start.14 = (bf16[8,1024]{1,0:T(8,128)(2,1)S(1)}, bf16[8,1024]{1,0:T(8,128)(2,1)S(1)}, u32[]{:S(2)}, u32[]{:S(2)}) collective-permute-start(bf16[8,1024]{1,0:T(8,128)(2,1)S(1)} %get-tuple-element.46), channel_id=1, source_target_pairs={{0,1},{1,0},{2,3},{3,2},{4,5},{5,4},{6,7},{7,6},{8,9},{9,8},{10,11... | collective-permute-start | bytes 49160 | tf_op jit(solution)/shard_map/ppermute | solution.py:41
  42.8 2.2 %collective-permute-done.14.b_ref = bf16[8,1024]{1,0:T(8,128)(2,1)S(1)} collective-permute-done((bf16[8,1024]{1,0:T(8,128)(2,1)S(1)}, bf16[8,1024]{1,0:T(8,128)(2,1)S(1)}, u32[]{:S(2)}, u32[]{:S(2)}) %collective-permute-start.14) | collective-permute-done | bytes 16416 | tf_op jit(solution)/shard_map/ppermute | solution.py:41
  45.0 2.2 %collective-permute-start.15 = (bf16[8,1024]{1,0:T(8,128)(2,1)S(1)}, bf16[8,1024]{1,0:T(8,128)(2,1)S(1)}, u32[]{:S(2)}, u32[]{:S(2)}) collective-permute-start(bf16[8,1024]{1,0:T(8,128)(2,1)S(1)} %get-tuple-element.48), channel_id=1, source_target_pairs={{0,8},{4,12},{8,0},{12,4},{1,9},{5,13},{9,1},{13,5},{2,10},{6,14},... | collective-permute-start | bytes 49160 | tf_op jit(solution)/shard_map/ppermute | solution.py:41
  47.2 1.7 %collective-permute-done.15.b_ref = bf16[8,1024]{1,0:T(8,128)(2,1)S(1)} collective-permute-done((bf16[8,1024]{1,0:T(8,128)(2,1)S(1)}, bf16[8,1024]{1,0:T(8,128)(2,1)S(1)}, u32[]{:S(2)}, u32[]{:S(2)}) %collective-permute-start.15) | collective-permute-done | bytes 16416 | tf_op jit(solution)/shard_map/ppermute | solution.py:41
  48.9 1.2 %collective-permute-done.16.b_ref = f32[8,1024]{1,0:T(8,128)S(1)} collective-permute-done((f32[8,1024]{1,0:T(8,128)S(1)}, f32[8,1024]{1,0:T(8,128)S(1)}, u32[]{:S(2)}, u32[]{:S(2)}) %collective-permute-start.16) | collective-permute-done | bytes 32800 | tf_op jit(solution)/shard_map/ppermute | solution.py:41
  50.1 1.3 %shard_map.78 = bf16[8,2048]{1,0:T(8,128)(2,1)} custom-call(f32[8,1024]{1,0:T(8,128)S(1)} %shard_map.77.a_ref, f32[8,1024]{1,0:T(8,128)S(1)} %collective-permute-done.16.b_ref, bf16[1024,2048]{1,0:T(8,128)(2,1)S(1)} %shard_map.60.turned_ref), custom_call_target="tpu_custom_call" | custom-call | flops 1150000000 | bytes 65536 | tf_op jit(solution)/shard_map/pallas_call | solution.py:29
  (41 shorter events, 0.3 us)
Async XLA Ops:
  2.4 12.9 %copy-start = (bf16[2048,1024]{1,0:T(8,128)(2,1)}, bf16[2048,1024]{1,0:T(8,128)(2,1)S(1)}, u32[]{:S(2)}) copy-start(bf16[2048,1024]{1,0:T(8,128)(2,1)S(1)} %get-tuple-element.30.basis_ref) | copy-start | bytes 12582916
  2.4 15.6 %slice-start.4 = ((s8[16777216]{0:T(1024)(128)(4,1)}), s8[4194304]{0:T(1024)(128)(4,1)S(1)}, s32[]{:S(2)}) async-start(s8[16777216]{0:T(1024)(128)(4,1)} %bitcast.2), calls=%async_computation.4 | async-start | bytes 8388608
  2.5 15.6 %slice-start.8 = ((s8[16777216]{0:T(1024)(128)(4,1)}), s8[4194304]{0:T(1024)(128)(4,1)S(1)}, s32[]{:S(2)}) async-start(s8[16777216]{0:T(1024)(128)(4,1)} %bitcast.4), calls=%async_computation.8 | async-start | bytes 8388608
  2.5 15.6 %slice-start.5 = ((s8[16777216]{0:T(1024)(128)(4,1)}), s8[4194304]{0:T(1024)(128)(4,1)S(1)}, s32[]{:S(2)}) async-start(s8[16777216]{0:T(1024)(128)(4,1)} %bitcast.2), calls=%async_computation.5 | async-start | bytes 8388608
  2.5 15.6 %slice-start.6 = ((s8[16777216]{0:T(1024)(128)(4,1)}), s8[4194304]{0:T(1024)(128)(4,1)S(1)}, s32[]{:S(2)}) async-start(s8[16777216]{0:T(1024)(128)(4,1)} %bitcast.2), calls=%async_computation.6 | async-start | bytes 8388608
  2.5 15.6 %slice-start.7 = ((s8[16777216]{0:T(1024)(128)(4,1)}), s8[4194304]{0:T(1024)(128)(4,1)S(1)}, s32[]{:S(2)}) async-start(s8[16777216]{0:T(1024)(128)(4,1)} %bitcast.2), calls=%async_computation.7 | async-start | bytes 8388608
  2.5 15.6 %slice-start.9 = ((s8[16777216]{0:T(1024)(128)(4,1)}), s8[4194304]{0:T(1024)(128)(4,1)S(1)}, s32[]{:S(2)}) async-start(s8[16777216]{0:T(1024)(128)(4,1)} %bitcast.4), calls=%async_computation.9 | async-start | bytes 8388608
  2.5 15.6 %slice-start.10 = ((s8[16777216]{0:T(1024)(128)(4,1)}), s8[4194304]{0:T(1024)(128)(4,1)S(1)}, s32[]{:S(2)}) async-start(s8[16777216]{0:T(1024)(128)(4,1)} %bitcast.4), calls=%async_computation.10 | async-start | bytes 8388608
  2.5 15.6 %slice-start.11 = ((s8[16777216]{0:T(1024)(128)(4,1)}), s8[4194304]{0:T(1024)(128)(4,1)S(1)}, s32[]{:S(2)}) async-start(s8[16777216]{0:T(1024)(128)(4,1)} %bitcast.4), calls=%async_computation.11 | async-start | bytes 8388608
  2.5 1.4 %collective-permute-start = (f32[8,1024]{1,0:T(8,128)S(1)}, f32[8,1024]{1,0:T(8,128)S(1)}, u32[]{:S(2)}, u32[]{:S(2)}) collective-permute-start(f32[8,1024]{1,0:T(8,128)S(1)} %get-tuple-element.27.a_ref), channel_id=1, source_target_pairs={{0,4},{4,0},{8,12},{12,8},{1,5},{5,1},{9,13},{13,9},{2,6},{6,2},{1... | collective-permute-start | bytes 98312 | tf_op jit(solution)/shard_map/ppermute | solution.py:41
  3.9 4.5 %collective-permute-start.1 = (bf16[8,1024]{1,0:T(8,128)(2,1)S(1)}, bf16[8,1024]{1,0:T(8,128)(2,1)S(1)}, u32[]{:S(2)}, u32[]{:S(2)}) collective-permute-start(bf16[8,1024]{1,0:T(8,128)(2,1)S(1)} %get-tuple-element.29), channel_id=1, source_target_pairs={{0,8},{4,12},{8,0},{12,4},{1,9},{5,13},{9,1},{13,5},{2,10},{6,14},... | collective-permute-start | bytes 49160 | tf_op jit(solution)/shard_map/ppermute | solution.py:41
  8.5 3.8 %collective-permute-start.2 = (bf16[8,1024]{1,0:T(8,128)(2,1)S(1)}, bf16[8,1024]{1,0:T(8,128)(2,1)S(1)}, u32[]{:S(2)}, u32[]{:S(2)}) collective-permute-start(bf16[8,1024]{1,0:T(8,128)(2,1)S(1)} %shard_map.57.a_ref), channel_id=1, source_target_pairs={{0,1},{1,0},{2,3},{3,2},{4,5},{5,4},{6,7},{7,6},{8,9},{9,8},{10,11... | collective-permute-start | bytes 49160 | tf_op jit(solution)/shard_map/ppermute | solution.py:41
  12.3 4.9 %collective-permute-start.3 = (bf16[16,1024]{1,0:T(8,128)(2,1)S(1)}, bf16[16,1024]{1,0:T(8,128)(2,1)S(1)}, u32[]{:S(2)}, u32[]{:S(2)}) collective-permute-start(bf16[16,1024]{1,0:T(8,128)(2,1)S(1)} %shard_map.58.a_ref.refs_0_), channel_id=1, source_target_pairs={{0,2},{1,3},{2,0},{3,1},{4,6},{5,7},{6,4},{7,5},{8,10},{9,11},{10,... | collective-permute-start | bytes 98312 | tf_op jit(solution)/shard_map/ppermute | solution.py:41
  21.2 2.1 %collective-permute-start.4 = (bf16[32,2048]{1,0:T(8,128)(2,1)S(1)}, bf16[32,2048]{1,0:T(8,128)(2,1)S(1)}, u32[]{:S(2)}, u32[]{:S(2)}) collective-permute-start(bf16[32,2048]{1,0:T(8,128)(2,1)S(1)} %get-tuple-element.33), channel_id=1, source_target_pairs={{0,4},{4,0},{8,12},{12,8},{1,5},{5,1},{9,13},{13,9},{2,6},{6,2},{1... | collective-permute-start | bytes 393224 | tf_op jit(solution)/shard_map/ppermute | solution.py:41
  22.8 4.1 %collective-permute-start.6 = (bf16[32,1024]{1,0:T(8,128)(2,1)S(1)}, bf16[32,1024]{1,0:T(8,128)(2,1)S(1)}, u32[]{:S(2)}, u32[]{:S(2)}) collective-permute-start(bf16[32,1024]{1,0:T(8,128)(2,1)S(1)} %get-tuple-element.37), channel_id=1, source_target_pairs={{0,4},{4,0},{8,12},{12,8},{1,5},{5,1},{9,13},{13,9},{2,6},{6,2},{1... | collective-permute-start | bytes 196616 | tf_op jit(solution)/shard_map/ppermute | solution.py:41
  23.3 7.8 %slice-start = ((s8[16777216]{0:T(1024)(128)(4,1)}), s8[4194304]{0:T(1024)(128)(4,1)S(1)}, s32[]{:S(2)}) async-start(s8[16777216]{0:T(1024)(128)(4,1)} %bitcast), calls=%async_computation | async-start | bytes 8388608
  23.3 7.8 %slice-start.1 = ((s8[16777216]{0:T(1024)(128)(4,1)}), s8[4194304]{0:T(1024)(128)(4,1)S(1)}, s32[]{:S(2)}) async-start(s8[16777216]{0:T(1024)(128)(4,1)} %bitcast), calls=%async_computation.1 | async-start | bytes 8388608
  23.4 7.8 %slice-start.2 = ((s8[16777216]{0:T(1024)(128)(4,1)}), s8[4194304]{0:T(1024)(128)(4,1)S(1)}, s32[]{:S(2)}) async-start(s8[16777216]{0:T(1024)(128)(4,1)} %bitcast), calls=%async_computation.2 | async-start | bytes 8388608
  23.4 5.6 %collective-permute-start.8 = (bf16[32,2048]{1,0:T(8,128)(2,1)S(1)}, bf16[32,2048]{1,0:T(8,128)(2,1)S(1)}, u32[]{:S(2)}, u32[]{:S(2)}) collective-permute-start(bf16[32,2048]{1,0:T(8,128)(2,1)S(1)} %get-tuple-element.34.refs_1_), channel_id=1, source_target_pairs={{0,8},{4,12},{8,0},{12,4},{1,9},{5,13},{9,1},{13,5},{2,10},{6,14},... | collective-permute-start | bytes 393224 | tf_op jit(solution)/shard_map/ppermute | solution.py:41
  26.8 1.3 %collective-permute-start.5 = (bf16[32,1024]{1,0:T(8,128)(2,1)S(1)}, bf16[32,1024]{1,0:T(8,128)(2,1)S(1)}, u32[]{:S(2)}, u32[]{:S(2)}) collective-permute-start(bf16[32,1024]{1,0:T(8,128)(2,1)S(1)} %get-tuple-element.36), channel_id=1, source_target_pairs={{0,4},{4,0},{8,12},{12,8},{1,5},{5,1},{9,13},{13,9},{2,6},{6,2},{1... | collective-permute-start | bytes 196616 | tf_op jit(solution)/shard_map/ppermute | solution.py:41
  26.8 4.3 %slice-start.3 = ((s8[16777216]{0:T(1024)(128)(4,1)}), s8[4194304]{0:T(1024)(128)(4,1)S(1)}, s32[]{:S(2)}) async-start(s8[16777216]{0:T(1024)(128)(4,1)} %bitcast), calls=%async_computation.3 | async-start | bytes 8388608
  26.9 5.1 %collective-permute-start.10 = (bf16[32,1024]{1,0:T(8,128)(2,1)S(1)}, bf16[32,1024]{1,0:T(8,128)(2,1)S(1)}, u32[]{:S(2)}, u32[]{:S(2)}) collective-permute-start(bf16[32,1024]{1,0:T(8,128)(2,1)S(1)} %get-tuple-element.38.refs_0_), channel_id=1, source_target_pairs={{0,8},{4,12},{8,0},{12,4},{1,9},{5,13},{9,1},{13,5},{2,10},{6,14},... | collective-permute-start | bytes 196616 | tf_op jit(solution)/shard_map/ppermute | solution.py:41
  29.0 3.3 %collective-permute-start.9 = (bf16[32,1024]{1,0:T(8,128)(2,1)S(1)}, bf16[32,1024]{1,0:T(8,128)(2,1)S(1)}, u32[]{:S(2)}, u32[]{:S(2)}) collective-permute-start(bf16[32,1024]{1,0:T(8,128)(2,1)S(1)} %shard_map.68.refs_0_), channel_id=1, source_target_pairs={{0,4},{4,0},{8,12},{12,8},{1,5},{5,1},{9,13},{13,9},{2,6},{6,2},{1... | collective-permute-start | bytes 196616 | tf_op jit(solution)/shard_map/ppermute | solution.py:41
  29.1 4.8 %collective-permute-start.7 = (bf16[32,1024]{1,0:T(8,128)(2,1)S(1)}, bf16[32,1024]{1,0:T(8,128)(2,1)S(1)}, u32[]{:S(2)}, u32[]{:S(2)}) collective-permute-start(bf16[32,1024]{1,0:T(8,128)(2,1)S(1)} %get-tuple-element.40.refs_0_), channel_id=1, source_target_pairs={{0,8},{4,12},{8,0},{12,4},{1,9},{5,13},{9,1},{13,5},{2,10},{6,14},... | collective-permute-start | bytes 196616 | tf_op jit(solution)/shard_map/ppermute | solution.py:41
  32.1 3.1 %copy-start.1 = (bf16[2048,1024]{1,0:T(8,128)(2,1)S(1)}, bf16[2048,1024]{1,0:T(8,128)(2,1)}, u32[]{:S(2)}) copy-start(bf16[2048,1024]{1,0:T(8,128)(2,1)} %copy-done) | copy-start | bytes 12582916
  32.1 1.9 %collective-permute-start.12 = (bf16[32,512]{1,0:T(8,128)(2,1)S(1)}, bf16[32,512]{1,0:T(8,128)(2,1)S(1)}, u32[]{:S(2)}, u32[]{:S(2)}) collective-permute-start(bf16[32,512]{1,0:T(8,128)(2,1)S(1)} %shard_map.70.refs_1_), channel_id=1, source_target_pairs={{0,4},{4,0},{8,12},{12,8},{1,5},{5,1},{9,13},{13,9},{2,6},{6,2},{1... | collective-permute-start | bytes 98312 | tf_op jit(solution)/shard_map/ppermute | solution.py:41
  33.9 1.3 %collective-permute-start.11 = (bf16[32,512]{1,0:T(8,128)(2,1)S(1)}, bf16[32,512]{1,0:T(8,128)(2,1)S(1)}, u32[]{:S(2)}, u32[]{:S(2)}) collective-permute-start(bf16[32,512]{1,0:T(8,128)(2,1)S(1)} %shard_map.72.refs_1_), channel_id=1, source_target_pairs={{0,4},{4,0},{8,12},{12,8},{1,5},{5,1},{9,13},{13,9},{2,6},{6,2},{1... | collective-permute-start | bytes 98312 | tf_op jit(solution)/shard_map/ppermute | solution.py:41
  36.4 4.8 %collective-permute-start.13 = (bf16[16,1024]{1,0:T(8,128)(2,1)S(1)}, bf16[16,1024]{1,0:T(8,128)(2,1)S(1)}, u32[]{:S(2)}, u32[]{:S(2)}) collective-permute-start(bf16[16,1024]{1,0:T(8,128)(2,1)S(1)} %get-tuple-element.44), channel_id=1, source_target_pairs={{0,2},{1,3},{2,0},{3,1},{4,6},{5,7},{6,4},{7,5},{8,10},{9,11},{10,... | collective-permute-start | bytes 98312 | tf_op jit(solution)/shard_map/ppermute | solution.py:41
  41.2 3.8 %collective-permute-start.14 = (bf16[8,1024]{1,0:T(8,128)(2,1)S(1)}, bf16[8,1024]{1,0:T(8,128)(2,1)S(1)}, u32[]{:S(2)}, u32[]{:S(2)}) collective-permute-start(bf16[8,1024]{1,0:T(8,128)(2,1)S(1)} %get-tuple-element.46), channel_id=1, source_target_pairs={{0,1},{1,0},{2,3},{3,2},{4,5},{5,4},{6,7},{7,6},{8,9},{9,8},{10,11... | collective-permute-start | bytes 49160 | tf_op jit(solution)/shard_map/ppermute | solution.py:41
  45.0 3.9 %collective-permute-start.15 = (bf16[8,1024]{1,0:T(8,128)(2,1)S(1)}, bf16[8,1024]{1,0:T(8,128)(2,1)S(1)}, u32[]{:S(2)}, u32[]{:S(2)}) collective-permute-start(bf16[8,1024]{1,0:T(8,128)(2,1)S(1)} %get-tuple-element.48), channel_id=1, source_target_pairs={{0,8},{4,12},{8,0},{12,4},{1,9},{5,13},{9,1},{13,5},{2,10},{6,14},... | collective-permute-start | bytes 49160 | tf_op jit(solution)/shard_map/ppermute | solution.py:41
  48.9 1.2 %collective-permute-start.16 = (f32[8,1024]{1,0:T(8,128)S(1)}, f32[8,1024]{1,0:T(8,128)S(1)}, u32[]{:S(2)}, u32[]{:S(2)}) collective-permute-start(f32[8,1024]{1,0:T(8,128)S(1)} %shard_map.77.a_ref), channel_id=1, source_target_pairs={{0,4},{4,0},{8,12},{12,8},{1,5},{5,1},{9,13},{13,9},{2,6},{6,2},{1... | collective-permute-start | bytes 98312 | tf_op jit(solution)/shard_map/ppermute | solution.py:41

commit v9 on v5

--- a/solution.py
+++ b/solution.py
@@ -12,7 +12,7 @@
 F32 = jnp.float32
 BF16 = jnp.bfloat16
 LIMIT = 2 * 1024 * 1024
-PIECES = 4
+PIECES = 8
 WAIT = 30
 TURN = 1
 SUMS = (0.1, 1, 0.1)

time: 51.4 us -> 51.4 us (level)
  no operation moved by 1% of the time
where the time goes in v9:
time: 51.4 us; the launch traced here: 51.2 us
  starting transfers between devices  17.3 us (34%)
  waiting for transfers between devices  17 us (33%)
  Pallas kernels  16.2 us (32%)
    ppermute x17, starting transfers between devices, swap(): return lax.ppermute(value, axis, [(i, i ^ mask) for i in range(size)])  17.3 us
    ppermute x17, waiting for transfers between devices, swap(): return lax.ppermute(value, axis, [(i, i ^ mask) for i in range(size)])  17 us
    pallas_call x24, Pallas kernels, call(): pl.pallas_call(body, out_shape=out, in_specs=[HBM if i in fixed else VMEM...  16.2 us
  transfers between devices with their start and end apart: 17, of which 11 were waited for; matrix products, arithmetic and copies ran while one was open for 0% of the time, Pallas kernels for 14%

profile of v9, /device:TPU:0, one launch (start us, length us, event | category | flops | bytes accessed | tf_op | source)
XLA Modules:
  0.0 51.2 jit_solution(10946362927522191660)
XLA Ops:
  0.0 2.4 %shard_map.55 = (f32[8,1024]{1,0:T(8,128)S(1)}, bf16[2048,1024]{1,0:T(8,128)(2,1)S(1)}) custom-call(bf16[8,2048]{1,0:T(8,128)(2,1)} %x_ref.1, bf16[2048,1024]{1,0:T(8,128)(2,1)} %basis_ref.1), custom_call_target="tpu_custom_call" | custom-call | flops 1150000000 | bytes 65536 | tf_op jit(solution)/shard_map/pallas_call | solution.py:29
  2.4 0.0 slice-start.4
  2.5 0.0 slice-start.8
  2.5 0.5 %collective-permute-start = (f32[8,1024]{1,0:T(8,128)S(1)}, f32[8,1024]{1,0:T(8,128)S(1)}, u32[]{:S(2)}, u32[]{:S(2)}) collective-permute-start(f32[8,1024]{1,0:T(8,128)S(1)} %get-tuple-element.27.a_ref), channel_id=1, source_target_pairs={{0,4},{4,0},{8,12},{12,8},{1,5},{5,1},{9,13},{13,9},{2,6},{6,2},{1... | collective-permute-start | bytes 98312 | tf_op jit(solution)/shard_map/ppermute | solution.py:41
  3.1 0.9 %collective-permute-done.b_ref = f32[8,1024]{1,0:T(8,128)S(1)} collective-permute-done((f32[8,1024]{1,0:T(8,128)S(1)}, f32[8,1024]{1,0:T(8,128)S(1)}, u32[]{:S(2)}, u32[]{:S(2)}) %collective-permute-start) | collective-permute-done | bytes 32800 | tf_op jit(solution)/shard_map/ppermute | solution.py:41
  3.9 2.8 %collective-permute-start.1 = (bf16[8,1024]{1,0:T(8,128)(2,1)S(1)}, bf16[8,1024]{1,0:T(8,128)(2,1)S(1)}, u32[]{:S(2)}, u32[]{:S(2)}) collective-permute-start(bf16[8,1024]{1,0:T(8,128)(2,1)S(1)} %get-tuple-element.29), channel_id=1, source_target_pairs={{0,8},{4,12},{8,0},{12,4},{1,9},{5,13},{9,1},{13,5},{2,10},{6,14},... | collective-permute-start | bytes 49160 | tf_op jit(solution)/shard_map/ppermute | solution.py:41
  6.8 1.7 %collective-permute-done.1.b_ref = bf16[8,1024]{1,0:T(8,128)(2,1)S(1)} collective-permute-done((bf16[8,1024]{1,0:T(8,128)(2,1)S(1)}, bf16[8,1024]{1,0:T(8,128)(2,1)S(1)}, u32[]{:S(2)}, u32[]{:S(2)}) %collective-permute-start.1) | collective-permute-done | bytes 16416 | tf_op jit(solution)/shard_map/ppermute | solution.py:41
  8.5 2.1 %collective-permute-start.2 = (bf16[8,1024]{1,0:T(8,128)(2,1)S(1)}, bf16[8,1024]{1,0:T(8,128)(2,1)S(1)}, u32[]{:S(2)}, u32[]{:S(2)}) collective-permute-start(bf16[8,1024]{1,0:T(8,128)(2,1)S(1)} %shard_map.57.a_ref), channel_id=1, source_target_pairs={{0,1},{1,0},{2,3},{3,2},{4,5},{5,4},{6,7},{7,6},{8,9},{9,8},{10,11... | collective-permute-start | bytes 49160 | tf_op jit(solution)/shard_map/ppermute | solution.py:41
  10.6 1.7 %collective-permute-done.2.b_ref = bf16[8,1024]{1,0:T(8,128)(2,1)S(1)} collective-permute-done((bf16[8,1024]{1,0:T(8,128)(2,1)S(1)}, bf16[8,1024]{1,0:T(8,128)(2,1)S(1)}, u32[]{:S(2)}, u32[]{:S(2)}) %collective-permute-start.2) | collective-permute-done | bytes 16416 | tf_op jit(solution)/shard_map/ppermute | solution.py:41
  12.3 3.0 %collective-permute-start.3 = (bf16[16,1024]{1,0:T(8,128)(2,1)S(1)}, bf16[16,1024]{1,0:T(8,128)(2,1)S(1)}, u32[]{:S(2)}, u32[]{:S(2)}) collective-permute-start(bf16[16,1024]{1,0:T(8,128)(2,1)S(1)} %shard_map.58.a_ref.refs_0_), channel_id=1, source_target_pairs={{0,2},{1,3},{2,0},{3,1},{4,6},{5,7},{6,4},{7,5},{8,10},{9,11},{10,... | collective-permute-start | bytes 98312 | tf_op jit(solution)/shard_map/ppermute | solution.py:41
  15.3 1.2 %shard_map.60.turned_ref = bf16[1024,2048]{1,0:T(8,128)(2,1)S(1)} custom-call(bf16[2048,1024]{1,0:T(8,128)(2,1)S(1)} %get-tuple-element.30.basis_ref, bf16[16,1024]{1,0:T(8,128)(2,1)S(1)} %shard_map.58.a_ref.refs_0_), custom_call_target="tpu_custom_call" | custom-call | flops 1150000000 | bytes 65536 | tf_op jit(solution)/shard_map/pallas_call | solution.py:29
  16.6 0.7 %collective-permute-done.3.b_ref = bf16[16,1024]{1,0:T(8,128)(2,1)S(1)} collective-permute-done((bf16[16,1024]{1,0:T(8,128)(2,1)S(1)}, bf16[16,1024]{1,0:T(8,128)(2,1)S(1)}, u32[]{:S(2)}, u32[]{:S(2)}) %collective-permute-start.3) | collective-permute-done | bytes 32800 | tf_op jit(solution)/shard_map/ppermute | solution.py:41
  17.2 0.8 %shard_map.61.x_ref = bf16[32,2048]{1,0:T(8,128)(2,1)S(1)} custom-call(bf16[32,1024]{1,0:T(8,128)(2,1)S(1)} %shard_map.59.codes_ref, bf16[1024,2048]{1,0:T(8,128)(2,1)S(1)} %shard_map.60.turned_ref), custom_call_target="tpu_custom_call" | custom-call | flops 575000000 | bytes 65536 | tf_op jit(solution)/shard_map/pallas_call | solution.py:29
  18.1 0.0 slice-done.8
  18.2 3.0 %shard_map.62 = (f32[32,2048]{1,0:T(8,128)S(1)}, bf16[32,2048]{1,0:T(8,128)(2,1)S(1)}) custom-call(bf16[32,2048]{1,0:T(8,128)(2,1)S(1)} %shard_map.61.x_ref, bf16[2048,4096]{1,0:T(8,128)(2,1)S(1)} %bitcast.3, bf16[2048,4096]{1,0:T(8,128)(2,1)S(1)} %bitcast.5), custom_call_target="tpu_custom_call" | custom-call | flops 3449999872 | bytes 65536 | tf_op jit(solution)/shard_map/pallas_call | solution.py:29
  21.2 1.6 %shard_map.63 = (f32[32,1024]{1,0:T(8,128)S(1)}, bf16[32,1024]{1,0:T(8,128)(2,1)S(1)}) custom-call(bf16[32,2048]{1,0:T(8,128)(2,1)S(1)} %shard_map.61.x_ref, bf16[2048,4096]{1,0:T(8,128)(2,1)S(1)} %bitcast.3, bf16[2048,4096]{1,0:T(8,128)(2,1)S(1)} %bitcast.5, f32[32,2048]{1,0:T(8,128)S(1)} %get-tuple-element.31.refs_0_.a_ref), custom_call_target="tpu_custom_call" | custom-call | flops 1724999936 | bytes 65536 | tf_op jit(solution)/shard_map/pallas_call | solution.py:29
  22.8 0.5 %collective-permute-start.6 = (bf16[32,1024]{1,0:T(8,128)(2,1)S(1)}, bf16[32,1024]{1,0:T(8,128)(2,1)S(1)}, u32[]{:S(2)}, u32[]{:S(2)}) collective-permute-start(bf16[32,1024]{1,0:T(8,128)(2,1)S(1)} %get-tuple-element.37), channel_id=1, source_target_pairs={{0,4},{4,0},{8,12},{12,8},{1,5},{5,1},{9,13},{13,9},{2,6},{6,2},{1... | collective-permute-start | bytes 196616 | tf_op jit(solution)/shard_map/ppermute | solution.py:41
  23.3 0.0 slice-start
  23.3 0.0 slice-start.1
  23.4 1.9 %collective-permute-start.9 = (bf16[32,2048]{1,0:T(8,128)(2,1)S(1)}, bf16[32,2048]{1,0:T(8,128)(2,1)S(1)}, u32[]{:S(2)}, u32[]{:S(2)}) collective-permute-start(bf16[32,2048]{1,0:T(8,128)(2,1)S(1)} %get-tuple-element.34.refs_1_), channel_id=1, source_target_pairs={{0,8},{4,12},{8,0},{12,4},{1,9},{5,13},{9,1},{13,5},{2,10},{6,14},... | collective-permute-start | bytes 393224 | tf_op jit(solution)/shard_map/ppermute | solution.py:41
  25.3 1.6 %shard_map.65 = (f32[32,1024]{1,0:T(8,128)S(1)}, bf16[32,1024]{1,0:T(8,128)(2,1)S(1)}) custom-call(bf16[32,2048]{1,0:T(8,128)(2,1)S(1)} %shard_map.61.x_ref, bf16[2048,4096]{1,0:T(8,128)(2,1)S(1)} %bitcast.3, bf16[2048,4096]{1,0:T(8,128)(2,1)S(1)} %bitcast.5, f32[32,1024]{1,0:T(8,128)S(1)} %get-tuple-element.32.refs_0_.a_ref, ...), custom_call_target="tpu_custom_call" | custom-call | flops 1724999936 | bytes 65536 | tf_op jit(solution)/shard_map/pallas_call | solution.py:29
  26.8 0.0 collective-permute-done.6.b_ref
  26.8 0.0 slice-start.3
  26.9 0.3 collective-permute-start.8
  27.1 0.9 %collective-permute-done.5.b_ref = bf16[32,1024]{1,0:T(8,128)(2,1)S(1)} collective-permute-done((bf16[32,1024]{1,0:T(8,128)(2,1)S(1)}, bf16[32,1024]{1,0:T(8,128)(2,1)S(1)}, u32[]{:S(2)}, u32[]{:S(2)}) %collective-permute-start.5) | collective-permute-done | bytes 65568 | tf_op jit(solution)/shard_map/ppermute | solution.py:41
  28.1 1.0 %collective-permute-start.7 = (bf16[32,1024]{1,0:T(8,128)(2,1)S(1)}, bf16[32,1024]{1,0:T(8,128)(2,1)S(1)}, u32[]{:S(2)}, u32[]{:S(2)}) collective-permute-start(bf16[32,1024]{1,0:T(8,128)(2,1)S(1)} %get-tuple-element.40.refs_0_), channel_id=1, source_target_pairs={{0,8},{4,12},{8,0},{12,4},{1,9},{5,13},{9,1},{13,5},{2,10},{6,14},... | collective-permute-start | bytes 196616 | tf_op jit(solution)/shard_map/ppermute | solution.py:41
  29.1 0.1 shard_map.68.refs_0_
  29.1 0.1 collective-permute-start.12
  29.2 0.2 slice-done.3
  29.4 0.8 %shard_map.69.refs_0_.refs_3_ = f32[32,2048]{1,0:T(8,128)S(1)} custom-call(bf16[32,1024]{1,0:T(8,128)(2,1)S(1)} %shard_map.68.refs_0_, bf16[4096,2048]{1,0:T(8,128)(2,1)S(1)} %bitcast.1), custom_call_target="tpu_custom_call" | custom-call | flops 115000000 | bytes 65536 | tf_op jit(solution)/shard_map/pallas_call | solution.py:29
  30.2 1.6 %collective-permute-done.8.b_ref = bf16[32,1024]{1,0:T(8,128)(2,1)S(1)} collective-permute-done((bf16[32,1024]{1,0:T(8,128)(2,1)S(1)}, bf16[32,1024]{1,0:T(8,128)(2,1)S(1)}, u32[]{:S(2)}, u32[]{:S(2)}) %collective-permute-start.8) | collective-permute-done | bytes 65568 | tf_op jit(solution)/shard_map/ppermute | solution.py:41
  31.9 0.1 collective-permute-start.11
  32.0 0.9 %collective-permute-done.7.b_ref = bf16[32,1024]{1,0:T(8,128)(2,1)S(1)} collective-permute-done((bf16[32,1024]{1,0:T(8,128)(2,1)S(1)}, bf16[32,1024]{1,0:T(8,128)(2,1)S(1)}, u32[]{:S(2)}, u32[]{:S(2)}) %collective-permute-start.7) | collective-permute-done | bytes 65568 | tf_op jit(solution)/shard_map/ppermute | solution.py:41
  32.9 0.1 collective-permute-start.10
  33.0 1.2 %shard_map.72.refs_3_ = f32[32,2048]{1,0:T(8,128)S(1)} custom-call(bf16[32,1024]{1,0:T(8,128)(2,1)S(1)} %collective-permute-done.12.refs_0_, bf16[32,512]{1,0:T(8,128)(2,1)S(1)} %shard_map.70.refs_0_.refs_1_, bf16[4096,2048]{1,0:T(8,128)(2,1)S(1)} %bitcast.1, f32[32,2048]{1,0:T(8,128)S(1)} %shard_map.69.refs_0_.refs_3_), custom_call_target="tpu_custom_call" | custom-call | flops 115000000 | bytes 65536 | tf_op jit(solution)/shard_map/pallas_call | solution.py:29
  34.2 0.0 collective-permute-done.11.refs_0_
  34.2 0.8 %shard_map.73.acc_ref = f32[32,2048]{1,0:T(8,128)S(1)} custom-call(bf16[32,512]{1,0:T(8,128)(2,1)S(1)} %collective-permute-done.11.refs_0_, bf16[32,512]{1,0:T(8,128)(2,1)S(1)} %shard_map.71.refs_1_, bf16[4096,2048]{1,0:T(8,128)(2,1)S(1)} %bitcast.1, f32[32,2048]{1,0:T(8,128)S(1)} %shard_map.72.refs_3_), custom_call_target="tpu_custom_call" | custom-call | flops 115000000 | bytes 65536 | tf_op jit(solution)/shard_map/pallas_call | solution.py:29
  35.0 0.0 collective-permute-done.10.h_ref
  35.0 0.0 copy-done.1
  35.1 1.2 %shard_map.74 = (f32[16,1024]{1,0:T(8,128)S(1)}, bf16[16,1024]{1,0:T(8,128)(2,1)S(1)}) custom-call(bf16[32,512]{1,0:T(8,128)(2,1)S(1)} %collective-permute-done.10.h_ref, bf16[4096,2048]{1,0:T(8,128)(2,1)S(1)} %bitcast.1, f32[32,2048]{1,0:T(8,128)S(1)} %shard_map.73.acc_ref, bf16[2048,1024]{1,0:T(8,128)(2,1)S(1)} %copy-done.1), custom_call_target="tpu_custom_call" | custom-call | flops 1150000000 | bytes 65536 | tf_op jit(solution)/shard_map/pallas_call | solution.py:29
  36.3 2.6 %collective-permute-start.13 = (bf16[16,1024]{1,0:T(8,128)(2,1)S(1)}, bf16[16,1024]{1,0:T(8,128)(2,1)S(1)}, u32[]{:S(2)}, u32[]{:S(2)}) collective-permute-start(bf16[16,1024]{1,0:T(8,128)(2,1)S(1)} %get-tuple-element.44), channel_id=1, source_target_pairs={{0,2},{1,3},{2,0},{3,1},{4,6},{5,7},{6,4},{7,5},{8,10},{9,11},{10,... | collective-permute-start | bytes 98312 | tf_op jit(solution)/shard_map/ppermute | solution.py:41
  38.9 2.2 %collective-permute-done.13.b_ref = bf16[16,1024]{1,0:T(8,128)(2,1)S(1)} collective-permute-done((bf16[16,1024]{1,0:T(8,128)(2,1)S(1)}, bf16[16,1024]{1,0:T(8,128)(2,1)S(1)}, u32[]{:S(2)}, u32[]{:S(2)}) %collective-permute-start.13) | collective-permute-done | bytes 32800 | tf_op jit(solution)/shard_map/ppermute | solution.py:41
  41.1 1.7 %collective-permute-start.14 = (bf16[8,1024]{1,0:T(8,128)(2,1)S(1)}, bf16[8,1024]{1,0:T(8,128)(2,1)S(1)}, u32[]{:S(2)}, u32[]{:S(2)}) collective-permute-start(bf16[8,1024]{1,0:T(8,128)(2,1)S(1)} %get-tuple-element.46), channel_id=1, source_target_pairs={{0,1},{1,0},{2,3},{3,2},{4,5},{5,4},{6,7},{7,6},{8,9},{9,8},{10,11... | collective-permute-start | bytes 49160 | tf_op jit(solution)/shard_map/ppermute | solution.py:41
  42.8 2.1 %collective-permute-done.14.b_ref = bf16[8,1024]{1,0:T(8,128)(2,1)S(1)} collective-permute-done((bf16[8,1024]{1,0:T(8,128)(2,1)S(1)}, bf16[8,1024]{1,0:T(8,128)(2,1)S(1)}, u32[]{:S(2)}, u32[]{:S(2)}) %collective-permute-start.14) | collective-permute-done | bytes 16416 | tf_op jit(solution)/shard_map/ppermute | solution.py:41
  44.9 0.7 %collective-permute-start.15 = (bf16[8,1024]{1,0:T(8,128)(2,1)S(1)}, bf16[8,1024]{1,0:T(8,128)(2,1)S(1)}, u32[]{:S(2)}, u32[]{:S(2)}) collective-permute-start(bf16[8,1024]{1,0:T(8,128)(2,1)S(1)} %get-tuple-element.48), channel_id=1, source_target_pairs={{0,8},{4,12},{8,0},{12,4},{1,9},{5,13},{9,1},{13,5},{2,10},{6,14},... | collective-permute-start | bytes 49160 | tf_op jit(solution)/shard_map/ppermute | solution.py:41
  45.6 3.1 %collective-permute-done.15.b_ref = bf16[8,1024]{1,0:T(8,128)(2,1)S(1)} collective-permute-done((bf16[8,1024]{1,0:T(8,128)(2,1)S(1)}, bf16[8,1024]{1,0:T(8,128)(2,1)S(1)}, u32[]{:S(2)}, u32[]{:S(2)}) %collective-permute-start.15) | collective-permute-done | bytes 16416 | tf_op jit(solution)/shard_map/ppermute | solution.py:41
  48.7 1.2 %collective-permute-done.16.b_ref = f32[8,1024]{1,0:T(8,128)S(1)} collective-permute-done((f32[8,1024]{1,0:T(8,128)S(1)}, f32[8,1024]{1,0:T(8,128)S(1)}, u32[]{:S(2)}, u32[]{:S(2)}) %collective-permute-start.16) | collective-permute-done | bytes 32800 | tf_op jit(solution)/shard_map/ppermute | solution.py:41
  49.9 1.3 %shard_map.78 = bf16[8,2048]{1,0:T(8,128)(2,1)} custom-call(f32[8,1024]{1,0:T(8,128)S(1)} %shard_map.77.a_ref, f32[8,1024]{1,0:T(8,128)S(1)} %collective-permute-done.16.b_ref, bf16[1024,2048]{1,0:T(8,128)(2,1)S(1)} %shard_map.60.turned_ref), custom_call_target="tpu_custom_call" | custom-call | flops 1150000000 | bytes 65536 | tf_op jit(solution)/shard_map/pallas_call | solution.py:29
  (41 shorter events, 0.3 us)
Async XLA Ops:
  2.4 12.9 %copy-start = (bf16[2048,1024]{1,0:T(8,128)(2,1)}, bf16[2048,1024]{1,0:T(8,128)(2,1)S(1)}, u32[]{:S(2)}) copy-start(bf16[2048,1024]{1,0:T(8,128)(2,1)S(1)} %get-tuple-element.30.basis_ref) | copy-start | bytes 12582916
  2.4 15.6 %slice-start.4 = ((s8[16777216]{0:T(1024)(128)(4,1)}), s8[4194304]{0:T(1024)(128)(4,1)S(1)}, s32[]{:S(2)}) async-start(s8[16777216]{0:T(1024)(128)(4,1)} %bitcast.2), calls=%async_computation.4 | async-start | bytes 8388608
  2.5 15.6 %slice-start.8 = ((s8[16777216]{0:T(1024)(128)(4,1)}), s8[4194304]{0:T(1024)(128)(4,1)S(1)}, s32[]{:S(2)}) async-start(s8[16777216]{0:T(1024)(128)(4,1)} %bitcast.4), calls=%async_computation.8 | async-start | bytes 8388608
  2.5 15.6 %slice-start.5 = ((s8[16777216]{0:T(1024)(128)(4,1)}), s8[4194304]{0:T(1024)(128)(4,1)S(1)}, s32[]{:S(2)}) async-start(s8[16777216]{0:T(1024)(128)(4,1)} %bitcast.2), calls=%async_computation.5 | async-start | bytes 8388608
  2.5 15.6 %slice-start.6 = ((s8[16777216]{0:T(1024)(128)(4,1)}), s8[4194304]{0:T(1024)(128)(4,1)S(1)}, s32[]{:S(2)}) async-start(s8[16777216]{0:T(1024)(128)(4,1)} %bitcast.2), calls=%async_computation.6 | async-start | bytes 8388608
  2.5 15.6 %slice-start.7 = ((s8[16777216]{0:T(1024)(128)(4,1)}), s8[4194304]{0:T(1024)(128)(4,1)S(1)}, s32[]{:S(2)}) async-start(s8[16777216]{0:T(1024)(128)(4,1)} %bitcast.2), calls=%async_computation.7 | async-start | bytes 8388608
  2.5 15.6 %slice-start.9 = ((s8[16777216]{0:T(1024)(128)(4,1)}), s8[4194304]{0:T(1024)(128)(4,1)S(1)}, s32[]{:S(2)}) async-start(s8[16777216]{0:T(1024)(128)(4,1)} %bitcast.4), calls=%async_computation.9 | async-start | bytes 8388608
  2.5 15.6 %slice-start.10 = ((s8[16777216]{0:T(1024)(128)(4,1)}), s8[4194304]{0:T(1024)(128)(4,1)S(1)}, s32[]{:S(2)}) async-start(s8[16777216]{0:T(1024)(128)(4,1)} %bitcast.4), calls=%async_computation.10 | async-start | bytes 8388608
  2.5 15.6 %slice-start.11 = ((s8[16777216]{0:T(1024)(128)(4,1)}), s8[4194304]{0:T(1024)(128)(4,1)S(1)}, s32[]{:S(2)}) async-start(s8[16777216]{0:T(1024)(128)(4,1)} %bitcast.4), calls=%async_computation.11 | async-start | bytes 8388608
  2.5 1.4 %collective-permute-start = (f32[8,1024]{1,0:T(8,128)S(1)}, f32[8,1024]{1,0:T(8,128)S(1)}, u32[]{:S(2)}, u32[]{:S(2)}) collective-permute-start(f32[8,1024]{1,0:T(8,128)S(1)} %get-tuple-element.27.a_ref), channel_id=1, source_target_pairs={{0,4},{4,0},{8,12},{12,8},{1,5},{5,1},{9,13},{13,9},{2,6},{6,2},{1... | collective-permute-start | bytes 98312 | tf_op jit(solution)/shard_map/ppermute | solution.py:41
  3.9 4.5 %collective-permute-start.1 = (bf16[8,1024]{1,0:T(8,128)(2,1)S(1)}, bf16[8,1024]{1,0:T(8,128)(2,1)S(1)}, u32[]{:S(2)}, u32[]{:S(2)}) collective-permute-start(bf16[8,1024]{1,0:T(8,128)(2,1)S(1)} %get-tuple-element.29), channel_id=1, source_target_pairs={{0,8},{4,12},{8,0},{12,4},{1,9},{5,13},{9,1},{13,5},{2,10},{6,14},... | collective-permute-start | bytes 49160 | tf_op jit(solution)/shard_map/ppermute | solution.py:41
  8.5 3.8 %collective-permute-start.2 = (bf16[8,1024]{1,0:T(8,128)(2,1)S(1)}, bf16[8,1024]{1,0:T(8,128)(2,1)S(1)}, u32[]{:S(2)}, u32[]{:S(2)}) collective-permute-start(bf16[8,1024]{1,0:T(8,128)(2,1)S(1)} %shard_map.57.a_ref), channel_id=1, source_target_pairs={{0,1},{1,0},{2,3},{3,2},{4,5},{5,4},{6,7},{7,6},{8,9},{9,8},{10,11... | collective-permute-start | bytes 49160 | tf_op jit(solution)/shard_map/ppermute | solution.py:41
  12.3 4.9 %collective-permute-start.3 = (bf16[16,1024]{1,0:T(8,128)(2,1)S(1)}, bf16[16,1024]{1,0:T(8,128)(2,1)S(1)}, u32[]{:S(2)}, u32[]{:S(2)}) collective-permute-start(bf16[16,1024]{1,0:T(8,128)(2,1)S(1)} %shard_map.58.a_ref.refs_0_), channel_id=1, source_target_pairs={{0,2},{1,3},{2,0},{3,1},{4,6},{5,7},{6,4},{7,5},{8,10},{9,11},{10,... | collective-permute-start | bytes 98312 | tf_op jit(solution)/shard_map/ppermute | solution.py:41
  21.2 2.1 %collective-permute-start.4 = (bf16[32,2048]{1,0:T(8,128)(2,1)S(1)}, bf16[32,2048]{1,0:T(8,128)(2,1)S(1)}, u32[]{:S(2)}, u32[]{:S(2)}) collective-permute-start(bf16[32,2048]{1,0:T(8,128)(2,1)S(1)} %get-tuple-element.33), channel_id=1, source_target_pairs={{0,4},{4,0},{8,12},{12,8},{1,5},{5,1},{9,13},{13,9},{2,6},{6,2},{1... | collective-permute-start | bytes 393224 | tf_op jit(solution)/shard_map/ppermute | solution.py:41
  22.8 4.1 %collective-permute-start.6 = (bf16[32,1024]{1,0:T(8,128)(2,1)S(1)}, bf16[32,1024]{1,0:T(8,128)(2,1)S(1)}, u32[]{:S(2)}, u32[]{:S(2)}) collective-permute-start(bf16[32,1024]{1,0:T(8,128)(2,1)S(1)} %get-tuple-element.37), channel_id=1, source_target_pairs={{0,4},{4,0},{8,12},{12,8},{1,5},{5,1},{9,13},{13,9},{2,6},{6,2},{1... | collective-permute-start | bytes 196616 | tf_op jit(solution)/shard_map/ppermute | solution.py:41
  23.3 5.9 %slice-start = ((s8[16777216]{0:T(1024)(128)(4,1)}), s8[4194304]{0:T(1024)(128)(4,1)S(1)}, s32[]{:S(2)}) async-start(s8[16777216]{0:T(1024)(128)(4,1)} %bitcast), calls=%async_computation | async-start | bytes 8388608
  23.3 5.9 %slice-start.1 = ((s8[16777216]{0:T(1024)(128)(4,1)}), s8[4194304]{0:T(1024)(128)(4,1)S(1)}, s32[]{:S(2)}) async-start(s8[16777216]{0:T(1024)(128)(4,1)} %bitcast), calls=%async_computation.1 | async-start | bytes 8388608
  23.4 5.9 %slice-start.2 = ((s8[16777216]{0:T(1024)(128)(4,1)}), s8[4194304]{0:T(1024)(128)(4,1)S(1)}, s32[]{:S(2)}) async-start(s8[16777216]{0:T(1024)(128)(4,1)} %bitcast), calls=%async_computation.2 | async-start | bytes 8388608
  23.4 5.7 %collective-permute-start.9 = (bf16[32,2048]{1,0:T(8,128)(2,1)S(1)}, bf16[32,2048]{1,0:T(8,128)(2,1)S(1)}, u32[]{:S(2)}, u32[]{:S(2)}) collective-permute-start(bf16[32,2048]{1,0:T(8,128)(2,1)S(1)} %get-tuple-element.34.refs_1_), channel_id=1, source_target_pairs={{0,8},{4,12},{8,0},{12,4},{1,9},{5,13},{9,1},{13,5},{2,10},{6,14},... | collective-permute-start | bytes 393224 | tf_op jit(solution)/shard_map/ppermute | solution.py:41
  26.8 1.3 %collective-permute-start.5 = (bf16[32,1024]{1,0:T(8,128)(2,1)S(1)}, bf16[32,1024]{1,0:T(8,128)(2,1)S(1)}, u32[]{:S(2)}, u32[]{:S(2)}) collective-permute-start(bf16[32,1024]{1,0:T(8,128)(2,1)S(1)} %get-tuple-element.36), channel_id=1, source_target_pairs={{0,4},{4,0},{8,12},{12,8},{1,5},{5,1},{9,13},{13,9},{2,6},{6,2},{1... | collective-permute-start | bytes 196616 | tf_op jit(solution)/shard_map/ppermute | solution.py:41
  26.8 2.6 %slice-start.3 = ((s8[16777216]{0:T(1024)(128)(4,1)}), s8[4194304]{0:T(1024)(128)(4,1)S(1)}, s32[]{:S(2)}) async-start(s8[16777216]{0:T(1024)(128)(4,1)} %bitcast), calls=%async_computation.3 | async-start | bytes 8388608
  26.9 5.0 %collective-permute-start.8 = (bf16[32,1024]{1,0:T(8,128)(2,1)S(1)}, bf16[32,1024]{1,0:T(8,128)(2,1)S(1)}, u32[]{:S(2)}, u32[]{:S(2)}) collective-permute-start(bf16[32,1024]{1,0:T(8,128)(2,1)S(1)} %get-tuple-element.38.refs_0_), channel_id=1, source_target_pairs={{0,8},{4,12},{8,0},{12,4},{1,9},{5,13},{9,1},{13,5},{2,10},{6,14},... | collective-permute-start | bytes 196616 | tf_op jit(solution)/shard_map/ppermute | solution.py:41
  28.1 4.7 %collective-permute-start.7 = (bf16[32,1024]{1,0:T(8,128)(2,1)S(1)}, bf16[32,1024]{1,0:T(8,128)(2,1)S(1)}, u32[]{:S(2)}, u32[]{:S(2)}) collective-permute-start(bf16[32,1024]{1,0:T(8,128)(2,1)S(1)} %get-tuple-element.40.refs_0_), channel_id=1, source_target_pairs={{0,8},{4,12},{8,0},{12,4},{1,9},{5,13},{9,1},{13,5},{2,10},{6,14},... | collective-permute-start | bytes 196616 | tf_op jit(solution)/shard_map/ppermute | solution.py:41
  29.1 3.8 %collective-permute-start.12 = (bf16[32,1024]{1,0:T(8,128)(2,1)S(1)}, bf16[32,1024]{1,0:T(8,128)(2,1)S(1)}, u32[]{:S(2)}, u32[]{:S(2)}) collective-permute-start(bf16[32,1024]{1,0:T(8,128)(2,1)S(1)} %shard_map.68.refs_0_), channel_id=1, source_target_pairs={{0,4},{4,0},{8,12},{12,8},{1,5},{5,1},{9,13},{13,9},{2,6},{6,2},{1... | collective-permute-start | bytes 196616 | tf_op jit(solution)/shard_map/ppermute | solution.py:41
  31.9 2.3 %collective-permute-start.11 = (bf16[32,512]{1,0:T(8,128)(2,1)S(1)}, bf16[32,512]{1,0:T(8,128)(2,1)S(1)}, u32[]{:S(2)}, u32[]{:S(2)}) collective-permute-start(bf16[32,512]{1,0:T(8,128)(2,1)S(1)} %shard_map.70.refs_0_.refs_1_), channel_id=1, source_target_pairs={{0,4},{4,0},{8,12},{12,8},{1,5},{5,1},{9,13},{13,9},{2,6},{6,2},{1... | collective-permute-start | bytes 98312 | tf_op jit(solution)/shard_map/ppermute | solution.py:41
  32.9 2.2 %copy-start.1 = (bf16[2048,1024]{1,0:T(8,128)(2,1)S(1)}, bf16[2048,1024]{1,0:T(8,128)(2,1)}, u32[]{:S(2)}) copy-start(bf16[2048,1024]{1,0:T(8,128)(2,1)} %copy-done) | copy-start | bytes 12582916
  32.9 2.1 %collective-permute-start.10 = (bf16[32,512]{1,0:T(8,128)(2,1)S(1)}, bf16[32,512]{1,0:T(8,128)(2,1)S(1)}, u32[]{:S(2)}, u32[]{:S(2)}) collective-permute-start(bf16[32,512]{1,0:T(8,128)(2,1)S(1)} %shard_map.71.refs_1_), channel_id=1, source_target_pairs={{0,4},{4,0},{8,12},{12,8},{1,5},{5,1},{9,13},{13,9},{2,6},{6,2},{1... | collective-permute-start | bytes 98312 | tf_op jit(solution)/shard_map/ppermute | solution.py:41
  36.3 4.8 %collective-permute-start.13 = (bf16[16,1024]{1,0:T(8,128)(2,1)S(1)}, bf16[16,1024]{1,0:T(8,128)(2,1)S(1)}, u32[]{:S(2)}, u32[]{:S(2)}) collective-permute-start(bf16[16,1024]{1,0:T(8,128)(2,1)S(1)} %get-tuple-element.44), channel_id=1, source_target_pairs={{0,2},{1,3},{2,0},{3,1},{4,6},{5,7},{6,4},{7,5},{8,10},{9,11},{10,... | collective-permute-start | bytes 98312 | tf_op jit(solution)/shard_map/ppermute | solution.py:41
  41.1 3.8 %collective-permute-start.14 = (bf16[8,1024]{1,0:T(8,128)(2,1)S(1)}, bf16[8,1024]{1,0:T(8,128)(2,1)S(1)}, u32[]{:S(2)}, u32[]{:S(2)}) collective-permute-start(bf16[8,1024]{1,0:T(8,128)(2,1)S(1)} %get-tuple-element.46), channel_id=1, source_target_pairs={{0,1},{1,0},{2,3},{3,2},{4,5},{5,4},{6,7},{7,6},{8,9},{9,8},{10,11... | collective-permute-start | bytes 49160 | tf_op jit(solution)/shard_map/ppermute | solution.py:41
  44.9 3.8 %collective-permute-start.15 = (bf16[8,1024]{1,0:T(8,128)(2,1)S(1)}, bf16[8,1024]{1,0:T(8,128)(2,1)S(1)}, u32[]{:S(2)}, u32[]{:S(2)}) collective-permute-start(bf16[8,1024]{1,0:T(8,128)(2,1)S(1)} %get-tuple-element.48), channel_id=1, source_target_pairs={{0,8},{4,12},{8,0},{12,4},{1,9},{5,13},{9,1},{13,5},{2,10},{6,14},... | collective-permute-start | bytes 49160 | tf_op jit(solution)/shard_map/ppermute | solution.py:41
  48.7 1.2 %collective-permute-start.16 = (f32[8,1024]{1,0:T(8,128)S(1)}, f32[8,1024]{1,0:T(8,128)S(1)}, u32[]{:S(2)}, u32[]{:S(2)}) collective-permute-start(f32[8,1024]{1,0:T(8,128)S(1)} %shard_map.77.a_ref), channel_id=1, source_target_pairs={{0,4},{4,0},{8,12},{12,8},{1,5},{5,1},{9,13},{13,9},{2,6},{6,2},{1... | collective-permute-start | bytes 98312 | tf_op jit(solution)/shard_map/ppermute | solution.py:41
